TPU v7x, 32 devices: a whole 2x2x4 slice. The times are simulated.
32 devices in a mesh: dp: 8 (over y, x, core), tensor: 4 (over z).
Axes of the slice: x: 2, y: 2, z: 4, core: 2. Of those that a mesh axis runs over, the one named last changes fastest.
Arguments:
- hidden_in: bfloat16 [6144, 2048], P('dp'), may hold values from -6 to 6
- segment_ids: int32 [6144], P('dp'), may hold values from 0 to 63, never falling along the last dimension, each value on 1 to 384 neighbouring positions
- modality: int32 [6144], P('dp'), may hold values from 0 to 1
- norm_gain: float32 [2048], replicated, may hold values from 0.5 to 1.5
- in_proj: bfloat16 [2, 2048, 2, 4096], P(None, None, None, 'tensor'), may hold values from -0.125 to 0.125
- conv_weight: float32 [4, 4096], P(None, 'tensor'), may hold values from -0.8 to 0.8
- conv_bias: float32 [4096], P('tensor'), may hold values from -1 to 1
- x_proj: bfloat16 [2, 4096, 160], P(None, 'tensor'), may hold values from -0.1875 to 0.1875
- dt_proj: bfloat16 [2, 128, 4096], P(None, None, 'tensor'), may hold values from -0.5 to 0.5
- dt_bias: float32 [2, 4096], P(None, 'tensor'), may hold values from -5 to -1
- a_log: float32 [16, 4096], P(None, 'tensor'), may hold values from -2 to 2.5
- skip_gain: float32 [4096], P('tensor'), may hold values from 0.5 to 1.5
- out_proj: bfloat16 [2, 4096, 2048], P(None, 'tensor'), may hold values from -0.1875 to 0.1875
- out_grad: bfloat16 [6144, 2048], P('dp'), may hold values from -6 to 6
Outputs:
- output: bfloat16 [6144, 2048], P('dp')
- input_grad: bfloat16 [6144, 2048], P('dp')
- norm_gain_grad: float32 [2048], replicated
- in_proj_grad: float32 [2, 2048, 2, 4096], P(None, None, None, 'tensor')
- conv_weight_grad: float32 [4, 4096], P(None, 'tensor')
- conv_bias_grad: float32 [4096], P('tensor')
- x_proj_grad: float32 [2, 4096, 160], P(None, 'tensor')
- dt_proj_grad: float32 [2, 128, 4096], P(None, None, 'tensor')
- dt_bias_grad: float32 [2, 4096], P(None, 'tensor')
- a_log_grad: float32 [16, 4096], P(None, 'tensor')
- skip_grad: float32 [4096], P('tensor')
- out_proj_grad: float32 [2, 4096, 2048], P(None, 'tensor')
Inputs may be any that keep to these rules, and one draw needn't show every extreme that they name: `segment_ids`: segment ids never fall along the tokens; a segment holds 1 to 384 tokens and one holds exactly that many.
All inputs are finite; a program needn't handle non-finite values.
Results may differ from a plain program's by a relative error of at most 0.011.
Values may be sent and summed in bfloat16 or wider, within the bound.
A program may use at most 320 MiB of HBM per device.

v0:
```python
import jax
import jax.numpy as jnp
from jax import lax
from jax.sharding import PartitionSpec as P

EPS = 1e-05


def lagged(values, offset):
    padding = [(offset, 0)] + [(0, 0)] * (values.ndim - 1)
    return jnp.pad(values, padding)[: values.shape[0]]


def leading(values, offset):
    padding = [(0, offset)] + [(0, 0)] * (values.ndim - 1)
    return jnp.pad(values, padding)[offset:]


def pick_dot(left_side, weights, first_mode):
    first_part = jnp.dot(left_side, weights[0], preferred_element_type=jnp.float32)
    second_part = jnp.dot(left_side, weights[1], preferred_element_type=jnp.float32)
    return jnp.where(first_mode, first_part, second_part)


def pick_back(gradient, weights, first_mode):
    dims = (((1,), (1,)), ((), ()))
    first_part = lax.dot_general(gradient, weights[0], dims, preferred_element_type=jnp.float32)
    second_part = lax.dot_general(gradient, weights[1], dims, preferred_element_type=jnp.float32)
    return jnp.where(first_mode, first_part, second_part)


def weight_grads(left_side, gradient, first_mode):
    nothing = jnp.zeros_like(gradient)
    dims = (((0,), (0,)), ((), ()))
    first_part = lax.dot_general(
        left_side,
        jnp.where(first_mode, gradient, nothing),
        dims,
        preferred_element_type=jnp.float32,
    )
    second_part = lax.dot_general(
        left_side,
        jnp.where(first_mode, nothing, gradient),
        dims,
        preferred_element_type=jnp.float32,
    )
    return jnp.stack([first_part, second_part])


def finish_rows(normed_grad, hidden, inverse, cotan, norm_gain):
    scaled = normed_grad * norm_gain
    gain_terms = jnp.sum(normed_grad * hidden * inverse, axis=0)
    cubed = inverse * inverse * inverse
    rows = (
        cotan + inverse * scaled - hidden * cubed * jnp.mean(scaled * hidden, axis=1, keepdims=True)
    )
    return (rows.astype(jnp.bfloat16), gain_terms)


def shards(
    hidden_in,
    segment_ids,
    modality,
    norm_gain,
    in_proj,
    conv_weight,
    conv_bias,
    x_proj,
    dt_proj,
    dt_bias,
    a_log,
    skip_gain,
    out_proj,
    out_grad,
):
    tokens = hidden_in.shape[0]
    model_width = hidden_in.shape[1]
    channels = conv_weight.shape[1]
    conv_taps = conv_weight.shape[0]
    rank_dim = dt_proj.shape[1]
    state_dim = a_log.shape[0]
    block_len = 32
    block_count = tokens // block_len
    first_mode = (modality == 0)[:, None]
    hidden = hidden_in.astype(jnp.float32)
    inverse = lax.rsqrt(jnp.mean(hidden * hidden, axis=1, keepdims=True) + EPS)
    normed_b = (hidden * inverse * norm_gain).astype(jnp.bfloat16)
    in_wide = in_proj.reshape(2, model_width, 2 * channels)
    both_parts = pick_dot(normed_b, in_wide, first_mode)
    inner_x = both_parts[:, :channels]
    gate_z = both_parts[:, channels:]
    same_doc = [jnp.ones((tokens, 1), jnp.float32)]
    for offset in range(1, conv_taps):
        earlier_seg = jnp.pad(segment_ids, (offset, 0), constant_values=-1)[:tokens]
        same_doc.append((earlier_seg == segment_ids).astype(jnp.float32)[:, None])
    conv_sum = conv_bias + conv_weight[conv_taps - 1] * inner_x
    for offset in range(1, conv_taps):
        conv_sum = (
            conv_sum
            + conv_weight[conv_taps - 1 - offset] * lagged(inner_x, offset) * same_doc[offset]
        )
    activated_b = jax.nn.silu(conv_sum).astype(jnp.bfloat16)
    activated = activated_b.astype(jnp.float32)
    projected = lax.psum(pick_dot(activated_b, x_proj, first_mode), "tensor")
    rank_b = projected[:, :rank_dim].astype(jnp.bfloat16)
    b_coeff = projected[:, rank_dim : rank_dim + state_dim]
    c_coeff = projected[:, rank_dim + state_dim :]
    step_pre = pick_dot(rank_b, dt_proj, first_mode) + jnp.where(first_mode, dt_bias[0], dt_bias[1])
    step_size = jax.nn.softplus(step_pre)
    decay = -jnp.exp(a_log)
    keep_mask = same_doc[1][:, 0]
    position = jnp.arange(block_len)
    ordered = position[:, None] >= position[None, :]

    def split_blocks(values):
        return values.reshape((block_count, block_len) + values.shape[1:])

    def block_terms(step_blk, act_blk, b_blk, keep_blk):
        log_factor = step_blk[:, None, :] * decay[None]
        factor = jnp.exp(log_factor) * keep_blk[:, None, None]
        source = (step_blk * act_blk)[:, None, :] * b_blk[:, :, None]
        running = jnp.cumsum(log_factor, axis=0)
        resets = jnp.cumsum(1.0 - keep_blk)
        linked = (resets[:, None] == resets[None, :]) & ordered
        spread = jnp.minimum(running[:, None] - running[None, :], 0.0)
        weights = jnp.where(linked[:, :, None, None], jnp.exp(spread), 0.0)
        from_start = jnp.where((resets == 0.0)[:, None, None], jnp.exp(running), 0.0)
        return (factor, source, weights, from_start)

    def block_states(source, weights, from_start, start_state):
        return jnp.sum(weights * source[None], axis=1) + from_start * start_state[None]

    def forward_block(start_state, inputs):
        step_blk, act_blk, b_blk, c_blk, keep_blk = inputs
        factor, source, weights, from_start = block_terms(step_blk, act_blk, b_blk, keep_blk)
        states = block_states(source, weights, from_start, start_state)
        emitted = jnp.sum(c_blk[:, :, None] * states, axis=1)
        return (states[-1], (emitted, start_state))

    scan_inputs = (
        split_blocks(step_size),
        split_blocks(activated),
        split_blocks(b_coeff),
        split_blocks(c_coeff),
        split_blocks(keep_mask),
    )
    _, (scanned, starts) = lax.scan(
        forward_block, jnp.zeros((state_dim, channels), jnp.float32), scan_inputs
    )
    scanned = scanned.reshape(tokens, channels)
    sig_z = jax.nn.sigmoid(gate_z)
    silu_z = gate_z * sig_z
    mixed_out = scanned + skip_gain * activated
    gated_b = (mixed_out * silu_z).astype(jnp.bfloat16)
    partial_out = pick_dot(gated_b, out_proj, first_mode)
    output = (hidden + lax.psum(partial_out, "tensor")).astype(jnp.bfloat16)
    cotan = out_grad.astype(jnp.float32)
    out_proj_grad = weight_grads(gated_b, out_grad, first_mode)
    gated_grad = pick_back(out_grad, out_proj, first_mode)
    mixed_grad = gated_grad * silu_z
    gate_grad = gated_grad * mixed_out * sig_z * (1.0 + gate_z * (1.0 - sig_z))
    skip_grad = jnp.sum(mixed_grad * activated, axis=0)

    def backward_block(carried, inputs):
        later_term, rate_grad = carried
        step_blk, act_blk, b_blk, c_blk, keep_blk, dy_blk, start_state = inputs
        factor, source, weights, from_start = block_terms(step_blk, act_blk, b_blk, keep_blk)
        states = block_states(source, weights, from_start, start_state)
        emitted = c_blk[:, :, None] * dy_blk[:, None, :]
        emitted = emitted.at[-1].add(later_term)
        dstate = jnp.sum(weights * emitted[:, None], axis=0)
        log_grad = dstate * (states - source)
        weighted = jnp.sum(dstate * b_blk[:, :, None], axis=1)
        step_grad = weighted * act_blk + jnp.sum(log_grad * decay[None], axis=1)
        act_grad = weighted * step_blk
        b_grad = jnp.sum(dstate * (step_blk * act_blk)[:, None, :], axis=2)
        c_grad = jnp.sum(dy_blk[:, None, :] * states, axis=2)
        rate_grad = rate_grad + jnp.sum(log_grad * step_blk[:, None, :], axis=0)
        return ((factor[0] * dstate[0], rate_grad), (step_grad, act_grad, b_grad, c_grad))

    zero_state = jnp.zeros((state_dim, channels), jnp.float32)
    (_, rate_grad), (step_grad, scan_act_grad, b_grad, c_grad) = lax.scan(
        backward_block,
        (zero_state, zero_state),
        scan_inputs + (split_blocks(mixed_grad), starts),
        reverse=True,
    )
    step_grad = step_grad.reshape(tokens, channels)
    scan_act_grad = scan_act_grad.reshape(tokens, channels)
    b_grad = b_grad.reshape(tokens, state_dim)
    c_grad = c_grad.reshape(tokens, state_dim)
    a_log_grad = rate_grad * decay
    pre_grad_b = (step_grad * jax.nn.sigmoid(step_pre)).astype(jnp.bfloat16)
    pre_grad = pre_grad_b.astype(jnp.float32)
    dt_bias_grad = jnp.stack(
        [
            jnp.sum(jnp.where(first_mode, pre_grad, 0.0), axis=0),
            jnp.sum(jnp.where(first_mode, 0.0, pre_grad), axis=0),
        ]
    )
    dt_proj_grad = weight_grads(rank_b, pre_grad_b, first_mode)
    rank_part = pick_back(pre_grad_b, dt_proj, first_mode)
    proj_grad = lax.psum(jnp.concatenate([rank_part, b_grad, c_grad], axis=1), "tensor")
    proj_grad_b = proj_grad.astype(jnp.bfloat16)
    x_proj_grad = weight_grads(activated_b, proj_grad_b, first_mode)
    act_grad = mixed_grad * skip_gain + scan_act_grad + pick_back(proj_grad_b, x_proj, first_mode)
    sig_conv = jax.nn.sigmoid(conv_sum)
    conv_grad = act_grad * sig_conv * (1.0 + conv_sum * (1.0 - sig_conv))
    conv_bias_grad = jnp.sum(conv_grad, axis=0)
    weight_rows = []
    x_grad = jnp.zeros_like(inner_x)
    for tap_index in range(conv_taps):
        offset = conv_taps - 1 - tap_index
        masked = conv_grad * same_doc[offset]
        weight_rows.append(jnp.sum(masked * lagged(inner_x, offset), axis=0))
        x_grad = x_grad + conv_weight[tap_index] * leading(masked, offset)
    conv_weight_grad = jnp.stack(weight_rows)
    both_grad_b = jnp.concatenate([x_grad, gate_grad], axis=1).astype(jnp.bfloat16)
    in_proj_grad = weight_grads(normed_b, both_grad_b, first_mode).reshape(
        2, model_width, 2, channels
    )
    normed_part = pick_back(both_grad_b, in_wide, first_mode)
    normed_grad = lax.psum(normed_part, "tensor")
    input_grad, norm_gain_grad = finish_rows(normed_grad, hidden, inverse, cotan, norm_gain)
    shares = (
        lax.psum_scatter(norm_gain_grad, "dp", scatter_dimension=0, tiled=True),
        lax.psum_scatter(in_proj_grad, "dp", scatter_dimension=1, tiled=True),
        lax.psum_scatter(conv_weight_grad, "dp", scatter_dimension=1, tiled=True),
        lax.psum_scatter(conv_bias_grad, "dp", scatter_dimension=0, tiled=True),
        lax.psum_scatter(x_proj_grad, "dp", scatter_dimension=1, tiled=True),
        lax.psum_scatter(dt_proj_grad, "dp", scatter_dimension=2, tiled=True),
        lax.psum_scatter(dt_bias_grad, "dp", scatter_dimension=1, tiled=True),
        lax.psum_scatter(a_log_grad, "dp", scatter_dimension=1, tiled=True),
        lax.psum_scatter(skip_grad, "dp", scatter_dimension=0, tiled=True),
        lax.psum_scatter(out_proj_grad, "dp", scatter_dimension=2, tiled=True),
    )
    summed = (
        lax.all_gather(shares[0], "dp", axis=0, tiled=True),
        lax.all_gather(shares[1], "dp", axis=1, tiled=True),
        lax.all_gather(shares[2], "dp", axis=1, tiled=True),
        lax.all_gather(shares[3], "dp", axis=0, tiled=True),
        lax.all_gather(shares[4], "dp", axis=1, tiled=True),
        lax.all_gather(shares[5], "dp", axis=2, tiled=True),
        lax.all_gather(shares[6], "dp", axis=1, tiled=True),
        lax.all_gather(shares[7], "dp", axis=1, tiled=True),
        lax.all_gather(shares[8], "dp", axis=0, tiled=True),
        lax.all_gather(shares[9], "dp", axis=2, tiled=True),
    )
    return (
        output,
        input_grad,
        summed[0],
        summed[1],
        summed[2],
        summed[3],
        summed[4],
        summed[5],
        summed[6],
        summed[7],
        summed[8],
        summed[9],
    )


def solution(mesh):
    in_specs = (
        P("dp", None),
        P("dp"),
        P("dp"),
        P(),
        P(None, None, None, "tensor"),
        P(None, "tensor"),
        P("tensor"),
        P(None, "tensor", None),
        P(None, None, "tensor"),
        P(None, "tensor"),
        P(None, "tensor"),
        P("tensor"),
        P(None, "tensor", None),
        P("dp", None),
    )
    out_specs = (
        P("dp", None),
        P("dp", None),
        P(),
        P(None, None, None, "tensor"),
        P(None, "tensor"),
        P("tensor"),
        P(None, "tensor", None),
        P(None, None, "tensor"),
        P(None, "tensor"),
        P(None, "tensor"),
        P("tensor"),
        P(None, "tensor", None),
    )
    return jax.shard_map(shards, mesh=mesh, in_specs=in_specs, out_specs=out_specs, check_vma=False)
```

profile of v0, /device:TPU:0, one launch (start us, length us, event | category | flops | bytes accessed | tf_op | source)
XLA Modules:
  0.0 3215.7 jit_solution(3848984042884975198)
XLA Ops:
  88.4 38.5 %all-reduce.18.cloned.1.call-done = f32[768,160]{0,1:T(8,128)} async-done(((f32[768,160]{0,1:T(8,128)}), f32[768,160]{0,1:T(8,128)}) %all-reduce.18.cloned.1.call-update) | async-done | bytes 491536 | tf_op jit(solution)/shard_map/psum | solution.py:104
  137.4 665.2 %while.41 = (s32[]{:T(128)}, f32[16,1024]{1,0:T(8,128)S(1)}, f32[24,32,1024]{2,1,0:T(8,128)}, f32[24,16,1024]{2,1,0:T(8,128)}, f32[24,32]{1,0:T(8,128)S(1)}, /*i...) while((s32[]{:T(128)}, f32[16,1024]{1,0:T(8,128)S(1)}, ...), condition=%wide.region_7.8_spmd.clone, body=%wide.region_2.7_spmd.clone.sunk | while | flops 103288864 | bytes 18501096 | solution.py:147
  808.3 1080.5 %while.42 = (s32[]{:T(128)}, f32[16,1024]{1,0:T(8,128)S(1)}, f32[16,1024]{1,0:T(8,128)S(1)}, f32[24,32,1024]{2,1,0:T(8,128)}, f32[24,32,1024]{2,1,0:T(8,128)}, /...) while((s32[]{:T(128)}, f32[16,1024]{1,0:T(8,128)S(1)}, ...), condition=%wide.region_19.20_spmd.clone, body=%wide.region_9.19_spmd.clone.sunk | while | flops 143264800 | bytes 28964544 | solution.py:182
  816.6 28.1 multiply_reduce_fusion.20
  861.6 28.1 multiply_reduce_fusion.20
  906.6 28.1 multiply_reduce_fusion.20
  951.7 28.1 multiply_reduce_fusion.20
  996.7 28.1 multiply_reduce_fusion.20
  1041.7 28.1 multiply_reduce_fusion.20
  1086.7 28.1 multiply_reduce_fusion.20
  1131.7 28.1 multiply_reduce_fusion.20
  1176.7 28.1 multiply_reduce_fusion.20
  1221.8 28.1 multiply_reduce_fusion.20
  1266.8 28.1 multiply_reduce_fusion.20
  1311.8 28.1 multiply_reduce_fusion.20
  1356.8 28.1 multiply_reduce_fusion.20
  1401.8 28.1 multiply_reduce_fusion.20
  1446.9 28.1 multiply_reduce_fusion.20
  1491.9 28.1 multiply_reduce_fusion.20
  1536.9 28.1 multiply_reduce_fusion.20
  1581.9 28.1 multiply_reduce_fusion.20
  1626.9 28.1 multiply_reduce_fusion.20
  1671.9 28.1 multiply_reduce_fusion.20
  1717.0 28.1 multiply_reduce_fusion.20
  1807.0 28.1 multiply_reduce_fusion.20
  1852.0 28.1 multiply_reduce_fusion.20
  2075.1 43.0 %reshape.370 = f32[2048,4096]{1,0:T(8,128)} reshape(f32[2048,2,2,1024]{3,2,1,0:T(2,128)} %copy_bitcast_fusion) | data formatting | bytes 67108864
  2170.2 153.0 %reduce-scatter.23.cloned.1.call-done = f32[256,4096]{1,0:T(8,128)} async-done(((f32[2048,4096]{1,0:T(8,128)}), f32[256,4096]{1,0:T(8,128)}) %reduce-scatter.23.cloned.1.call-update) | async-done | bytes 4194320
  2370.0 28.4 reduce-scatter.25.cloned.1.call-done
  2485.7 430.8 %all-reduce.20.cloned.1.call-done = (f32[768,2048]{1,0:T(8,128)}, f32[768,2048]{1,0:T(8,128)}) async-done(((f32[768,2048]{1,0:T(8,128)}, f32[768,2048]{1,0:T(8,128)}), (f32[768,2048]{1,0:T(8,128)}, f32[768,2048]{1,0:T(8,128)})) %all-reduce.20.cloned.1.call-update) | async-done | bytes 12582928 | tf_op jit(solution)/shard_map/psum | solution.py:156
  2978.2 32.4 %all-gather.14.cloned.1.call-done = f32[2,1024,2048]{2,1,0:T(8,128)} async-done(((f32[2,1024,256]{2,1,0:T(8,128)}), f32[2,1024,2048]{2,1,0:T(8,128)}) %all-gather.14.cloned.1.call-update) | async-done | bytes 16777232 | tf_op jit(solution)/shard_map/all_gather | solution.py:247
  3010.6 162.9 %all-gather.8.cloned.1.call-done = f32[2,2048,2,1024]{3,2,1,0:T(2,128)} async-done(((f32[2,256,2,1024]{3,2,1,0:T(2,128)}), f32[2,2048,2,1024]{3,2,1,0:T(2,128)}) %all-gather.8.cloned.1.call-update) | async-done | bytes 33554448 | tf_op jit(solution)/shard_map/all_gather | solution.py:239
  (1206 shorter events, 1660.8 us)
Async XLA Ops:
  7.2 119.7 %all-reduce.18.cloned.1.call-start = ((), (), s32[]{:S(2)}) async-start(), calls=%async_computation.7 | async-start | bytes 983040 | tf_op jit(solution)/shard_map/psum | solution.py:104
  21.3 10.3 copy-start.2
  32.9 20.0 copy-start.22
  43.2 28.2 copy-start.42
  43.2 28.2 copy-start.44
  43.2 43.1 %copy-start.28 = (f32[768]{0:T(1024)}, f32[768]{0:T(1024)S(1)}, u32[]{:S(2)}) copy-start(f32[768]{0:T(1024)S(1)} %get-tuple-element.691) | copy-start | bytes 9220
  71.5 12.6 copy-start.12
  86.2 42.7 %copy-start.15 = (bf16[2,128,1024]{2,1,0:T(8,128)(2,1)S(1)}, bf16[2,128,1024]{2,1,0:T(8,128)(2,1)}, u32[]{:S(2)}) copy-start(bf16[2,128,1024]{2,1,0:T(8,128)(2,1)} %param.28) | copy-start | bytes 1572868
  86.2 2035.0 %reduce-scatter.17.cloned.1.call-start = ((), (), s32[]{:S(2)}) async-start(), calls=%async_computation.11 | async-start | bytes 1179648 | tf_op jit(solution)/shard_map/reduce_scatter | solution.py:231
  1895.9 32.6 %copy-start.1 = (bf16[768,1024]{1,0:T(8,128)(2,1)S(1)}, bf16[768,1024]{1,0:T(8,128)(2,1)}, u32[]{:S(2)}) copy-start(bf16[768,1024]{1,0:T(8,128)(2,1)} %copy-done) | copy-start | bytes 4718596
  1895.9 248.0 %reduce-scatter.15.cloned.1.call-start = ((), (), s32[]{:S(2)}) async-start(), calls=%async_computation.9 | async-start | bytes 1474560 | tf_op jit(solution)/shard_map/reduce_scatter | solution.py:230
  1932.8 236.6 %reduce-scatter.21.cloned.1.call-start = ((), (), s32[]{:S(2)}) async-start(), calls=%async_computation.14 | async-start | bytes 18874368 | tf_op jit(solution)/shard_map/reduce_scatter | solution.py:235
  1967.6 355.6 %reduce-scatter.23.cloned.1.call-start = ((), (), s32[]{:S(2)}) async-start(), calls=%async_computation.16 | async-start | bytes 37748736
  1974.4 12.3 copy-start.9
  2118.1 242.1 %reduce-scatter.27.cloned.1.call-start = ((), (), s32[]{:S(2)}) async-start(), calls=%async_computation.18 | async-start | bytes 589824
  2119.3 279.1 %reduce-scatter.25.cloned.1.call-start = ((), (), s32[]{:S(2)}) async-start(), calls=%async_computation.17 | async-start | bytes 589824
  2120.4 313.0 %reduce-scatter.19.cloned.1.call-start = ((), (), s32[]{:S(2)}) async-start(), calls=%async_computation.13 | async-start | bytes 73728 | tf_op jit(solution)/shard_map/reduce_scatter | solution.py:233
  2121.2 337.9 %all-gather.12.cloned.1.call-start = ((), (), s32[]{:S(2)}) async-start(), calls=%async_computation.12 | async-start | bytes 1179648 | tf_op jit(solution)/shard_map/all_gather | solution.py:243
  2121.9 363.8 %all-gather.10.cloned.1.call-start = ((), (), s32[]{:S(2)}) async-start(), calls=%async_computation.10 | async-start | bytes 1474560 | tf_op jit(solution)/shard_map/all_gather | solution.py:242
  2122.1 10.3 copy-start.10
  2144.0 772.5 %all-reduce.20.cloned.1.call-start = ((), (), s32[]{:S(2)}) async-start(), calls=%async_computation.19 | async-start | bytes 25165824 | tf_op jit(solution)/shard_map/psum | solution.py:156
  2144.0 13.7 copy-start.11
  2144.0 13.7 copy-start.51
  2144.0 13.6 copy-start.54
  2169.3 841.3 %all-gather.14.cloned.1.call-start = ((), (), s32[]{:S(2)}) async-start(), calls=%async_computation.15 | async-start | bytes 18874368 | tf_op jit(solution)/shard_map/all_gather | solution.py:247
  2169.9 1003.6 %all-gather.8.cloned.1.call-start = ((), (), s32[]{:S(2)}) async-start(), calls=%async_computation.8 | async-start | bytes 37748736 | tf_op jit(solution)/shard_map/all_gather | solution.py:239
  2916.4 53.2 %copy-start.26 = (f32[768]{0:T(1024)S(1)}, f32[768]{0:T(1024)}, u32[]{:S(2)}) copy-start(f32[768]{0:T(1024)} %get-tuple-element.689) | copy-start | bytes 9220
  3173.5 29.3 slice-start
  3174.1 24.5 copy-start.14
  3174.1 28.7 slice-start.1
  3174.1 28.7 slice-start.2
  3174.1 28.7 slice-start.3
  (40 other events, 191.9 us)
Sparse Core Ops, SparseCore 0:
  86.3 40.5 all-reduce.17
  1896.0 35.8 reduce-scatter.16
  1936.1 37.2 reduce-scatter.14
  1977.3 115.9 reduce-scatter.20
  2118.3 204.8 reduce-scatter.22
  2326.1 34.1 reduce-scatter.26
  2364.2 34.0 reduce-scatter.24
  2401.9 31.3 reduce-scatter.18
  2435.4 23.5 all-gather.11
  2460.9 24.7 all-gather.9
  2489.6 426.7 all-reduce.19
  2918.3 92.2 all-gather.13
  3012.7 160.7 all-gather.7
where the time goes:
time: 3240 us; the launch traced here: 3220 us
  other arithmetic  1630 us (50%)
  waiting for transfers between devices  938 us (29%)
  local copies, waits for them, and re-layouts  369 us (11%)
  matrix products  154 us (5%)
  blocking collectives  102 us (3%)
    reduce_sum x48, other arithmetic, block_states(): jnp.sum(weights * source[None], axis=1) + from_start * start_state[None]  1170 us
    psum x1, waiting for transfers between devices, shards(): output = (hidden + lax.psum(partial_out, 'tensor')).astype(jnp.bfloat16)  431 us
    unnamed x16, waiting for transfers between devices  205 us
    all_gather x1, waiting for transfers between devices, shards(): lax.all_gather(shares[1], 'dp', axis=1, tiled=True)  163 us
    unnamed x142, local copies, waits for them, and re-layouts  122 us
    mul x96, other arithmetic, block_terms(): source = (step_blk * act_blk)[:, None, :] * b_blk[:, :, None]  122 us
    reduce_sum x24, other arithmetic, backward_block(): step_grad = weighted * act_blk + jnp.sum(log_grad * decay[None], axis=1)  93.5 us
  transfers between devices with their start and end apart: 13, of which 10 were waited for; matrix products, arithmetic and copies ran while one was open for 9% of the time, Pallas kernels for 0%

commit v1 on v0

v1 whole, which is shorter than its diff:
```python
import functools

import jax
import jax.numpy as jnp
from jax import lax
from jax.experimental import pallas as pl
from jax.experimental.pallas import tpu as pltpu
from jax.sharding import PartitionSpec as P

EPS = 1e-05

LANES = 128
BIG = 1000.0
LOG2E = 1.4426950408889634


def softplus(v):
    return jnp.maximum(v, 0.0) + jnp.log1p(jnp.exp(-jnp.abs(v)))


def spread_rows(scratch, values, groups):
    rows = values.shape[0]
    for g in range(groups):
        scratch[pl.ds(g, rows, stride=groups), :] = values[:, g * LANES:(g + 1) * LANES]


def gather_rows(scratch, rows, groups):
    return jnp.concatenate(
        [scratch[pl.ds(g, rows, stride=groups), :] for g in range(groups)], axis=1)


def scan_forward_kernel(states, groups, rows, unroll,
                        bc_ref, pre_ref, act_ref, z_ref, gg_ref, keep_ref, alog_ref, skip_ref,
                        gated_ref, ggrad_ref, mixed_ref, h_ref, start_ref,
                        rate_scr, state_scr, sk_scr, u_scr, y_scr):
    chunk = pl.program_id(0)

    @pl.when(chunk == 0)
    def _():
        rate_scr[...] = jnp.exp(alog_ref[...]) * (-LOG2E)
        state_scr[...] = jnp.zeros_like(state_scr)

    step = softplus(pre_ref[...])
    act = act_ref[...].astype(jnp.float32)
    spread_rows(u_scr, step * act, groups)
    spread_rows(sk_scr, jnp.where(keep_ref[...] > 0.0, step, BIG), groups)
    start_ref[0] = state_scr[...]

    def one(t, held):
        at = pl.multiple_of(t * groups, groups)
        sk = sk_scr[pl.ds(at, groups), :]
        u = u_scr[pl.ds(at, groups), :]
        y = jnp.zeros_like(u)
        new = []
        for n in range(states):
            h = jnp.exp2(sk * rate_scr[n]) * held[n] + u * bc_ref[t, n]
            h_ref[t, n] = h
            y = y + h * bc_ref[t, states + n]
            new.append(h)
        y_scr[pl.ds(at, groups), :] = y
        return tuple(new)

    last = lax.fori_loop(0, rows, one, tuple(state_scr[n] for n in range(states)), unroll=unroll)
    for n in range(states):
        state_scr[n] = last[n]
    mixed_out = gather_rows(y_scr, rows, groups) + skip_ref[...] * act
    z = z_ref[...].astype(jnp.float32)
    gg = gg_ref[...].astype(jnp.float32)
    sig = jax.nn.sigmoid(z)
    silu = z * sig
    gated_ref[...] = (mixed_out * silu).astype(gated_ref.dtype)
    mixed_ref[...] = gg * silu
    ggrad_ref[...] = (gg * mixed_out * sig * (1.0 + z * (1.0 - sig))).astype(ggrad_ref.dtype)


def scan_forward(bc, pre, act, z, gg, keep, a_log3, skip, rows=64, unroll=4):
    tokens, channels = pre.shape
    groups = channels // LANES
    states = a_log3.shape[0]
    count = tokens // rows
    wide = pl.BlockSpec((rows, channels), lambda i: (i, 0))
    whole3 = pl.BlockSpec((states, groups, LANES), lambda i: (0, 0, 0))
    return pl.pallas_call(
        functools.partial(scan_forward_kernel, states, groups, rows, unroll),
        grid=(count,),
        in_specs=[
            pl.BlockSpec((rows, 2 * states), lambda i: (i, 0), memory_space=pltpu.SMEM),
            wide, wide, wide, wide,
            pl.BlockSpec((rows, 1), lambda i: (i, 0)),
            whole3,
            pl.BlockSpec((1, channels), lambda i: (0, 0)),
        ],
        out_specs=[
            wide, wide, wide,
            pl.BlockSpec((rows, states, groups, LANES), lambda i: (i, 0, 0, 0)),
            pl.BlockSpec((1, states, groups, LANES), lambda i: (i, 0, 0, 0)),
        ],
        out_shape=[
            jax.ShapeDtypeStruct((tokens, channels), jnp.bfloat16),
            jax.ShapeDtypeStruct((tokens, channels), jnp.bfloat16),
            jax.ShapeDtypeStruct((tokens, channels), jnp.float32),
            jax.ShapeDtypeStruct((tokens, states, groups, LANES), jnp.float32),
            jax.ShapeDtypeStruct((count, states, groups, LANES), jnp.float32),
        ],
        scratch_shapes=[
            pltpu.VMEM((states, groups, LANES), jnp.float32),
            pltpu.VMEM((states, groups, LANES), jnp.float32),
            pltpu.VMEM((rows * groups, LANES), jnp.float32),
            pltpu.VMEM((rows * groups, LANES), jnp.float32),
            pltpu.VMEM((rows * groups, LANES), jnp.float32),
        ],
        compiler_params=pltpu.CompilerParams(vmem_limit_bytes=48 * 1024 * 1024),
        name="scan_forward",
    )(bc, pre, act, z, gg, keep, a_log3, skip)


def scan_backward_kernel(states, groups, rows, unroll,
                         bc_ref, pre_ref, act_ref, mixed_ref, keep_ref, alog_ref, skip_ref, h_ref, start_ref,
                         pgrad_ref, apart_ref, bcg_ref, ratesum_ref, skipsum_ref,
                         rate_scr, decay_scr, carry_scr, sum_scr, sk_scr, u_scr, dy_scr, w_scr, s_scr, p_scr, q_scr):
    chunk = pl.program_id(0)
    count = pl.num_programs(0)

    @pl.when(chunk == 0)
    def _():
        decay = -jnp.exp(alog_ref[...])
        decay_scr[...] = decay
        rate_scr[...] = decay * LOG2E
        carry_scr[...] = jnp.zeros_like(carry_scr)
        sum_scr[...] = jnp.zeros_like(sum_scr)
        skipsum_ref[...] = jnp.zeros_like(skipsum_ref)

    step = softplus(pre_ref[...])
    act = act_ref[...].astype(jnp.float32)
    mixed = mixed_ref[...].astype(jnp.float32)
    spread_rows(u_scr, step * act, groups)
    spread_rows(dy_scr, mixed, groups)
    spread_rows(sk_scr, jnp.where(keep_ref[...] > 0.0, step, BIG), groups)
    skipsum_ref[...] += jnp.sum(mixed * act, axis=0, keepdims=True)

    def one(t, carried, before):
        at = pl.multiple_of(t * groups, groups)
        sk = sk_scr[pl.ds(at, groups), :]
        u = u_scr[pl.ds(at, groups), :]
        dy = dy_scr[pl.ds(at, groups), :]
        w = jnp.zeros_like(u)
        s = jnp.zeros_like(u)
        new, pb, pc = [], [], []
        for n in range(states):
            g = dy * bc_ref[t, states + n] + carried[n]
            pb.append(g * u)
            pc.append(dy * h_ref[t, n])
            w = w + g * bc_ref[t, n]
            fg = jnp.exp2(sk * rate_scr[n]) * g
            lg = fg * before(n)
            s = s + lg * decay_scr[n]
            sum_scr[n] += lg * sk
            new.append(fg)
        w_scr[pl.ds(at, groups), :] = w
        s_scr[pl.ds(at, groups), :] = s
        both = pb + pc
        batch = max(1, 16 // groups)
        for j in range(0, 2 * states, batch):
            p_scr[t, pl.ds(j * groups, batch * groups), :] = jnp.concatenate(
                both[j:j + batch], axis=0).astype(jnp.bfloat16)
        return tuple(new)

    def looped(i, carried):
        t = rows - 1 - i
        return one(t, carried, lambda n: h_ref[t - 1, n])

    last = lax.fori_loop(0, rows - 1, looped, tuple(carry_scr[n] for n in range(states)), unroll=unroll)
    last = one(0, last, lambda n: start_ref[0, n])
    for n in range(states):
        carry_scr[n] = last[n]

    ones = jnp.ones((16, LANES), jnp.bfloat16)

    def reduce_one(t, nothing):
        q = lax.dot_general(ones, p_scr[t], (((1,), (1,)), ((), ())), preferred_element_type=jnp.float32)
        q_scr[pl.ds(t, 1), :] = q[0:1]
        return nothing

    lax.fori_loop(0, rows, reduce_one, 0, unroll=4)
    pick = (lax.broadcasted_iota(jnp.int32, (2 * states * groups, 2 * states), 0) // groups
            == lax.broadcasted_iota(jnp.int32, (2 * states * groups, 2 * states), 1)).astype(jnp.float32).astype(jnp.bfloat16)
    q = q_scr[...]
    high = q.astype(jnp.bfloat16)
    low = (q - high.astype(jnp.float32)).astype(jnp.bfloat16)
    bcg_ref[...] = (jnp.dot(high, pick, preferred_element_type=jnp.float32)
                    + jnp.dot(low, pick, preferred_element_type=jnp.float32))
    w = gather_rows(w_scr, rows, groups)
    s = gather_rows(s_scr, rows, groups)
    pgrad_ref[...] = ((act * w + s) * jax.nn.sigmoid(pre_ref[...])).astype(pgrad_ref.dtype)
    apart_ref[...] = mixed * skip_ref[...] + step * w

    @pl.when(chunk == count - 1)
    def _():
        ratesum_ref[...] = sum_scr[...] * decay_scr[...]


def scan_backward(bc, pre, act, mixed, keep, a_log3, skip, h, starts, rows=64, unroll=3):
    tokens, channels = pre.shape
    groups = channels // LANES
    states = a_log3.shape[0]
    count = tokens // rows
    wide = pl.BlockSpec((rows, channels), lambda i: (count - 1 - i, 0))
    whole3 = pl.BlockSpec((states, groups, LANES), lambda i: (0, 0, 0))
    row = pl.BlockSpec((1, channels), lambda i: (0, 0))
    small = lambda: pltpu.VMEM((states, groups, LANES), jnp.float32)
    long = lambda: pltpu.VMEM((rows * groups, LANES), jnp.float32)
    return pl.pallas_call(
        functools.partial(scan_backward_kernel, states, groups, rows, unroll),
        grid=(count,),
        in_specs=[
            pl.BlockSpec((rows, 2 * states), lambda i: (count - 1 - i, 0), memory_space=pltpu.SMEM),
            wide, wide, wide,
            pl.BlockSpec((rows, 1), lambda i: (count - 1 - i, 0)),
            whole3, row,
            pl.BlockSpec((rows, states, groups, LANES), lambda i: (count - 1 - i, 0, 0, 0)),
            pl.BlockSpec((1, states, groups, LANES), lambda i: (count - 1 - i, 0, 0, 0)),
        ],
        out_specs=[
            wide, wide,
            pl.BlockSpec((rows, 2 * states), lambda i: (count - 1 - i, 0)),
            whole3, row,
        ],
        out_shape=[
            jax.ShapeDtypeStruct((tokens, channels), jnp.bfloat16),
            jax.ShapeDtypeStruct((tokens, channels), jnp.float32),
            jax.ShapeDtypeStruct((tokens, 2 * states), jnp.float32),
            jax.ShapeDtypeStruct((states, groups, LANES), jnp.float32),
            jax.ShapeDtypeStruct((1, channels), jnp.float32),
        ],
        scratch_shapes=[small(), small(), small(), small(), long(), long(), long(), long(), long(),
                        pltpu.VMEM((rows, 2 * states * groups, LANES), jnp.bfloat16),
                        pltpu.VMEM((rows, 2 * states * groups), jnp.float32)],
        compiler_params=pltpu.CompilerParams(vmem_limit_bytes=48 * 1024 * 1024),
        name="scan_backward",
    )(bc, pre, act, mixed, keep, a_log3, skip, h, starts)


def lagged(values, offset):
    padding = [(offset, 0)] + [(0, 0)] * (values.ndim - 1)
    return jnp.pad(values, padding)[: values.shape[0]]


def leading(values, offset):
    padding = [(0, offset)] + [(0, 0)] * (values.ndim - 1)
    return jnp.pad(values, padding)[offset:]


def pick_dot(left_side, weights, first_mode):
    first_part = jnp.dot(left_side, weights[0], preferred_element_type=jnp.float32)
    second_part = jnp.dot(left_side, weights[1], preferred_element_type=jnp.float32)
    return jnp.where(first_mode, first_part, second_part)


def pick_back(gradient, weights, first_mode):
    dims = (((1,), (1,)), ((), ()))
    first_part = lax.dot_general(gradient, weights[0], dims, preferred_element_type=jnp.float32)
    second_part = lax.dot_general(gradient, weights[1], dims, preferred_element_type=jnp.float32)
    return jnp.where(first_mode, first_part, second_part)


def weight_grads(left_side, gradient, first_mode):
    nothing = jnp.zeros_like(gradient)
    dims = (((0,), (0,)), ((), ()))
    first_part = lax.dot_general(
        left_side,
        jnp.where(first_mode, gradient, nothing),
        dims,
        preferred_element_type=jnp.float32,
    )
    second_part = lax.dot_general(
        left_side,
        jnp.where(first_mode, nothing, gradient),
        dims,
        preferred_element_type=jnp.float32,
    )
    return jnp.stack([first_part, second_part])


def finish_rows(normed_grad, hidden, inverse, cotan, norm_gain):
    scaled = normed_grad * norm_gain
    gain_terms = jnp.sum(normed_grad * hidden * inverse, axis=0)
    cubed = inverse * inverse * inverse
    rows = (
        cotan + inverse * scaled - hidden * cubed * jnp.mean(scaled * hidden, axis=1, keepdims=True)
    )
    return (rows.astype(jnp.bfloat16), gain_terms)


def shards(hidden_in, segment_ids, modality, norm_gain, in_proj, conv_weight, conv_bias, x_proj, dt_proj, dt_bias,
           a_log, skip_gain, out_proj, out_grad):
    tokens, model_width = hidden_in.shape
    conv_taps, channels = conv_weight.shape
    rank_dim = dt_proj.shape[1]
    state_dim = a_log.shape[0]
    groups = channels // LANES
    low = jnp.bfloat16
    first_mode = (modality == 0)[:, None]
    hidden = hidden_in.astype(jnp.float32)
    inverse = lax.rsqrt(jnp.mean(hidden * hidden, axis=1, keepdims=True) + EPS)
    normed_b = (hidden * inverse * norm_gain).astype(low)
    in_inner = in_proj[:, :, 0, :]
    in_gate = in_proj[:, :, 1, :]
    inner_x = pick_dot(normed_b, in_inner, first_mode)
    gate_z = pick_dot(normed_b, in_gate, first_mode)
    same_doc = [jnp.ones((tokens, 1), jnp.float32)]
    for offset in range(1, conv_taps):
        earlier_seg = jnp.pad(segment_ids, (offset, 0), constant_values=-1)[:tokens]
        same_doc.append((earlier_seg == segment_ids).astype(jnp.float32)[:, None])
    conv_sum = conv_bias + conv_weight[conv_taps - 1] * inner_x
    for offset in range(1, conv_taps):
        conv_sum = conv_sum + conv_weight[conv_taps - 1 - offset] * lagged(inner_x, offset) * same_doc[offset]
    activated_b = jax.nn.silu(conv_sum).astype(low)
    projected = lax.psum(pick_dot(activated_b, x_proj, first_mode), "tensor")
    rank_b = projected[:, :rank_dim].astype(low)
    coeffs = projected[:, rank_dim:]
    gated_grad = pick_back(out_grad, out_proj, first_mode)
    step_pre = pick_dot(rank_b, dt_proj, first_mode) + jnp.where(first_mode, dt_bias[0], dt_bias[1])
    keep = same_doc[1]
    a_log3 = a_log.reshape(state_dim, groups, LANES)
    skip_row = skip_gain[None]
    gated_b, gate_grad_b, mixed_grad, states, starts = scan_forward(
        coeffs, step_pre, activated_b, gate_z, gated_grad, keep, a_log3, skip_row)
    partial_out = pick_dot(gated_b, out_proj, first_mode).astype(low)
    summed_out = lax.psum(partial_out, "tensor")
    output = (hidden + summed_out.astype(jnp.float32)).astype(low)
    cotan = out_grad.astype(jnp.float32)
    out_proj_grad = weight_grads(gated_b, out_grad, first_mode).astype(low)
    out_proj_grad = lax.psum(out_proj_grad, "dp").astype(jnp.float32)
    gate_proj_grad = lax.psum(weight_grads(normed_b, gate_grad_b, first_mode).astype(low), "dp")
    pre_grad_b, act_part, coeff_grad, a_log_grad, skip_grad = scan_backward(
        coeffs, step_pre, activated_b, mixed_grad, keep, a_log3, skip_row, states, starts)
    a_log_grad = a_log_grad.reshape(state_dim, channels)
    pre_grad = pre_grad_b.astype(jnp.float32)
    dt_bias_grad = jnp.stack([
        jnp.sum(jnp.where(first_mode, pre_grad, 0.0), axis=0),
        jnp.sum(jnp.where(first_mode, 0.0, pre_grad), axis=0)])
    rank_part = pick_back(pre_grad_b, dt_proj, first_mode)
    proj_grad = lax.psum(jnp.concatenate([rank_part, coeff_grad], axis=1), "tensor")
    proj_grad_b = proj_grad.astype(low)
    act_grad = act_part + pick_back(proj_grad_b, x_proj, first_mode)
    sig_conv = jax.nn.sigmoid(conv_sum)
    conv_grad = act_grad * sig_conv * (1.0 + conv_sum * (1.0 - sig_conv))
    conv_bias_grad = jnp.sum(conv_grad, axis=0)
    weight_rows = []
    x_grad = jnp.zeros_like(inner_x)
    for tap_index in range(conv_taps):
        offset = conv_taps - 1 - tap_index
        masked = conv_grad * same_doc[offset]
        weight_rows.append(jnp.sum(masked * lagged(inner_x, offset), axis=0))
        x_grad = x_grad + conv_weight[tap_index] * leading(masked, offset)
    x_grad_b = x_grad.astype(low)
    normed_part = pick_back(x_grad_b, in_inner, first_mode) + pick_back(gate_grad_b, in_gate, first_mode)
    normed_grad = lax.psum(normed_part.astype(low), "tensor").astype(jnp.float32)
    inner_proj_grad = lax.psum(weight_grads(normed_b, x_grad_b, first_mode).astype(low), "dp")
    in_proj_grad = jnp.stack([inner_proj_grad, gate_proj_grad], axis=2).astype(jnp.float32)
    input_grad, norm_gain_grad = finish_rows(normed_grad, hidden, inverse, cotan, norm_gain)
    x_proj_grad = lax.psum(weight_grads(activated_b, proj_grad_b, first_mode).astype(low), "dp").astype(jnp.float32)
    dt_proj_grad = lax.psum(weight_grads(rank_b, pre_grad_b, first_mode).astype(low), "dp").astype(jnp.float32)
    rows = jnp.concatenate([jnp.stack(weight_rows), conv_bias_grad[None], dt_bias_grad, a_log_grad, skip_grad], axis=0)
    rows = lax.psum(rows, "dp")
    norm_gain_grad = lax.psum(norm_gain_grad, "dp")
    at = conv_taps + 1
    return (output, input_grad, norm_gain_grad, in_proj_grad, rows[:conv_taps], rows[conv_taps], x_proj_grad,
            dt_proj_grad, rows[at:at + 2], rows[at + 2:at + 2 + state_dim], rows[at + 2 + state_dim], out_proj_grad)


def solution(mesh):
    in_specs = (
        P("dp", None),
        P("dp"),
        P("dp"),
        P(),
        P(None, None, None, "tensor"),
        P(None, "tensor"),
        P("tensor"),
        P(None, "tensor", None),
        P(None, None, "tensor"),
        P(None, "tensor"),
        P(None, "tensor"),
        P("tensor"),
        P(None, "tensor", None),
        P("dp", None),
    )
    out_specs = (
        P("dp", None),
        P("dp", None),
        P(),
        P(None, None, None, "tensor"),
        P(None, "tensor"),
        P("tensor"),
        P(None, "tensor", None),
        P(None, None, "tensor"),
        P(None, "tensor"),
        P(None, "tensor"),
        P("tensor"),
        P(None, "tensor", None),
    )
    return jax.shard_map(shards, mesh=mesh, in_specs=in_specs, out_specs=out_specs, check_vma=False)
```

time: 3240 us -> 1010 us (0.31)
  other arithmetic: 1630 us -> 83.8 us
  waiting for transfers between devices: 938 us -> 507 us
  local copies, waits for them, and re-layouts: 369 us -> 102 us
  Pallas kernels: 0 us -> 103 us
  blocking collectives: 102 us -> 50.7 us
    reduce_sum x97 -> x1, other arithmetic: 1290 us -> 1.21 us  [shards(): jnp.sum(jnp.where(first_mode, 0.0, pre_grad), axis=0)]
    all_gather x4 -> x0, waiting for transfers between devices: 239 us -> none  [the longest x1 163 us: shards(): lax.all_gather(shares[1], 'dp', axis=1, tiled=True)]
    unnamed x16 -> x4, waiting for transfers between devices: 205 us -> 0.07 us
    mul x169 -> x0, other arithmetic: 184 us -> none  [the longest x96 122 us: block_terms(): source = (step_blk * act_blk)[:, None, :] * b_blk[:, :, None]]
    pallas_call x0 -> x2, Pallas kernels: none -> 103 us  [the longest x1 76.7 us: scan_backward(): pl.pallas_call(functools.partial(scan_backward_kernel, states, groups, ro...]
    mul x144 -> x0, local copies, waits for them, and re-layouts: 102 us -> none  [the longest x48 41 us: backward_block(): emitted = c_blk[:, :, None] * dy_blk[:, None, :]]
    unnamed x142 -> x121, local copies, waits for them, and re-layouts: 122 us -> 58.1 us
    another operation x10 -> x0, local copies, waits for them, and re-layouts: 60.3 us -> none  [the longest x2 52.4 us: weight_grads(): return jnp.stack([first_part, second_part])]
  transfers between devices with their start and end apart: 13 -> 4, of which waited for: 10 -> 3; matrix products, arithmetic and copies ran while one was open for 9% -> 13% of each run, Pallas kernels for 0% -> 0%
where the time goes in v1:
time: 1010 us; the launch traced here: 1000 us
  waiting for transfers between devices  507 us (50%)
  matrix products  140 us (14%)
  Pallas kernels  103 us (10%)
  local copies, waits for them, and re-layouts  102 us (10%)
  other arithmetic  83.8 us (8%)
  blocking collectives  50.7 us (5%)
  between operations  15 us (1%)
    psum x1, waiting for transfers between devices, shards(): lax.psum(weight_grads(normed_b, gate_grad_b, first_mode).astype(low), 'dp')  304 us
    psum x1, waiting for transfers between devices, shards(): summed_out = lax.psum(partial_out, 'tensor')  181 us
    pallas_call x1, Pallas kernels, scan_backward(): pl.pallas_call(functools.partial(scan_backward_kernel, states, groups, ro...  76.7 us
    unnamed x121, local copies, waits for them, and re-layouts  58.1 us
    dot_general x5, matrix products, pick_back(): lax.dot_general(gradient, weights[1], dims, preferred_element_type=jnp.fl...  39.2 us
    psum x1, blocking collectives, shards(): lax.psum(jnp.concatenate([rank_part, coeff_grad], axis=1), 'tensor')  35.9 us
    slice x1, local copies, waits for them, and re-layouts, pick_dot(): weights[1]  32.8 us
    pallas_call x1, Pallas kernels, scan_forward(): pl.pallas_call(functools.partial(scan_forward_kernel, states, groups, row...  26.3 us
  transfers between devices with their start and end apart: 4, of which 3 were waited for; matrix products, arithmetic and copies ran while one was open for 13% of the time, Pallas kernels for 0%

profile of v1, /device:TPU:0, one launch (start us, length us, event | category | flops | bytes accessed | tf_op | source)
XLA Modules:
  0.0 1002.8 jit_solution(2571926119257635938)
XLA Ops:
  10.5 32.8 %fusion.131 = (bf16[1,2048,1,1024]{3,2,1,0:T(2,128)(2,1)}, bf16[1,2048,1,1024]{3,2,1,0:T(2,128)(2,1)}, bf16[1,2048,1,1024]{3,2,1,0:T(2,128)(2,1)}, bf16[1,2048,1,1024]{3,2,1,0:T(2,128)(2,1)}) fusion(bf16[2,2048,2,1024]{3,2,1,0:T(2,128)(2,1)} %param.18), kind=kLoop, calls=%fused_computation.172 | loop fusion | bytes 33554432 | tf_op jit(solution)/shard_map/slice | solution.py:255
  43.5 6.2 fusion.43
  59.8 7.2 fusion.46
  67.1 5.6 fusion.14
  78.0 5.2 fusion.39.gg_ref
  83.4 22.6 %all-reduce.17.cloned.1.call-done = f32[768,160]{1,0:T(8,128)} async-done(((f32[768,160]{1,0:T(8,128)}), f32[768,160]{1,0:T(8,128)}) %all-reduce.17.cloned.1.call-update) | async-done | bytes 491536 | tf_op jit(solution)/shard_map/psum | solution.py:318
  111.1 26.3 %scan_forward.1 = (bf16[768,1024]{1,0:T(8,128)(2,1)S(1)}, bf16[768,1024]{1,0:T(8,128)(2,1)S(1)}, f32[768,1024]{1,0:T(8,128)}, f32[768,16,8,128]{3,2,1,0:T(8,128)}, f32[12,16,8,128]{3,2,1,0:T(8,128)S(1)}) custom-call(f32[768,32]{1,0:T(8,128)S(1)} %slice.156.bc_ref, f32[768,1024]{1,0:T(8,128)} %select_add_fusion.pre_ref, bf16[768,1024]{1,0:T(8,128)(2,1)} %copy-done, ...), custom_call_target="tpu_custom_call" | custom-call | tf_op jit(solution)/shard_map/scan_forward/pallas_call | solution.py:83
  139.4 76.7 %scan_backward.1 = (bf16[768,1024]{1,0:T(8,128)(2,1)S(1)}, f32[768,1024]{1,0:T(8,128)}, f32[768,32]{1,0:T(8,128)S(1)}, f32[16,8,128]{2,1,0:T(8,128)S(1)}, f32[1,1024]{1,0:T(1,128)S(1)}) custom-call(f32[768,32]{1,0:T(8,128)S(1)} %slice.156.bc_ref, f32[768,1024]{1,0:T(8,128)} %select_add_fusion.pre_ref, bf16[768,1024]{1,0:T(8,128)(2,1)S(1)} %copy-done.1, ...), custom_call_target="tpu_custom_call" | custom-call | tf_op jit(solution)/shard_map/scan_backward/pallas_call | solution.py:212
  219.4 35.9 %all-reduce.24 = bf16[768,160]{1,0:T(8,128)(2,1)S(1)} all-reduce(f32[768,160]{1,0:T(8,128)} %pad_maximum_fusion.1), channel_id=1, replica_groups=mesh['dp'=8,'tensor'=4] {'tensor'}, use_global_device_ids=true, to_apply=%region_3.4 | all-reduce | flops 122880 | bytes 737280 | tf_op jit(solution)/shard_map/psum | solution.py:343
  258.7 14.2 %fusion.130 = (f32[1024]{0:T(1024)}, f32[1024]{0:T(1024)}, f32[1024]{0:T(1024)}, f32[1024]{0:T(1024)}, f32[1024]{0:T(1024)}, /*index=5*/f32[768,1024]{1,0:T(8,12...) fusion(f32[768,1024]{1,0:T(8,128)} %copy-done.19, f32[768]{0:T(1024)S(1)} %get-tuple-element.93, ...), kind=kOutput, calls=%fused_computation.171 | convolution fusion | flops 268954624 | bytes 25771776 | tf_op jit(solution)/shard_map/dot_general | solution.py:262
  277.7 5.8 fusion.44
  283.5 5.8 fusion.42
  289.3 5.7 fusion.45
  300.3 6.2 fusion.12
  306.5 7.2 select_convert_fusion
  313.7 13.1 %add_convert_fusion = bf16[768,2048]{1,0:T(8,128)(2,1)} fusion(f32[768,2048]{1,0:T(8,128)} %fusion.45, f32[768,2048]{1,0:T(8,128)} %fusion.42, f32[768,2048]{1,0:T(8,128)} %fusion.44, bf16[768,1024]{1,0:T(8,128)(2,1)S(1)} %copy-done.4, pred[768]{0:T(1024)(128)(4,1)S(1)} %get-tuple-element.97, bf16[1,2048,1,1024]{3,2,1,0:T(2,128)(2,1)} %get-tuple-element.77), kind=kOutput, calls=%fused_computation.23 | convolution fusion | flops 3227516928 | bytes 27788032 | tf_op jit(solution)/shard_map/dot_general | solution.py:262
  333.1 5.4 convert_bitcast_fusion.4
  338.5 5.4 convert_bitcast_fusion.5
  343.9 7.7 maximum_bitcast_fusion
  351.7 7.2 convert_bitcast_fusion
  358.8 5.2 convert_bitcast_fusion.1
  364.1 7.6 pad_maximum_fusion
  371.7 5.5 convert_bitcast_fusion.2
  377.2 5.6 convert_bitcast_fusion.3
  382.8 7.6 maximum_bitcast_fusion.1
  396.3 181.1 %all-reduce.23.cloned.1.call-done = (bf16[768,2048]{1,0:T(8,128)(2,1)}, bf16[768,2048]{1,0:T(8,128)(2,1)}) async-done(((bf16[768,2048]{1,0:T(8,128)(2,1)}, bf16[768,2048]{1,0:T(8,128)(2,1)}), (bf16[768,2048]{1,0:T(8,128)(2,1)}, bf16[768,2048]{1,0:T(8,128)(2,1)})) %all-reduce.23.cloned.1.call-update) | async-done | bytes 6291472 | tf_op jit(solution)/shard_map/psum | solution.py:329
  581.1 14.8 %psum.81 = f32[2048]{0:T(1024)} all-reduce(f32[2048]{0:T(1024)S(1)} %get-tuple-element.56), channel_id=1, replica_groups=mesh['dp'=8,'tensor'=4] {'dp'}, use_global_device_ids=true, to_apply=%region_7.8 | all-reduce | flops 2048 | bytes 16384 | tf_op jit(solution)/shard_map/psum | solution.py:366
  595.9 6.9 fusion.3
  602.9 303.6 %all-reduce.21.cloned.1.call-done = (bf16[2,2048,1,1024]{3,1,0,2:T(8,128)(2,1)}, bf16[2,2048,1,1024]{3,1,0,2:T(8,128)(2,1)}, bf16[2,1024,160]{1,2,0:T(8,128)(2,1...) async-done(((bf16[2,2048,1,1024]{3,1,0,2:T(8,128)(2,1)}, bf16[2,2048,1,1024]{3,1,0,2:T(8,128)(2,1)}, bf16[2,1024,160]{1,2,0:T(8,128)(2,1)}, ...) | async-done | bytes 26345488 | tf_op jit(solution)/shard_map/psum | solution.py:334
  910.9 18.2 %maximum_convert_fusion = f32[2,2048,2,1024]{3,1,0,2:T(8,128)} fusion(bf16[2,2048,1,1024]{3,1,0,2:T(8,128)(2,1)} %get-tuple-element.65, bf16[2,2048,1,1024]{3,1,0,2:T(8,128)(2,1)} %get-tuple-element.66), kind=kLoop, calls=%fused_computation | loop fusion | flops 16777216 | bytes 50331648 | tf_op jit(solution)/shard_map/convert_element_type | solution.py:360
  929.0 55.1 %copy.41 = f32[2,2048,2,1024]{3,2,1,0:T(2,128)} copy(f32[2,2048,2,1024]{3,1,0,2:T(8,128)} %maximum_convert_fusion) | data formatting | bytes 67108864
  984.2 11.7 %convert_element_type.100 = f32[2,1024,2048]{2,1,0:T(8,128)} convert(bf16[2,1024,2048]{2,1,0:T(8,128)(2,1)} %get-tuple-element.69) | non-fusion elementwise | flops 4194304 | bytes 25165824 | tf_op jit(solution)/shard_map/convert_element_type | solution.py:333
  (169 shorter events, 62.7 us)
Async XLA Ops:
  7.2 98.8 %all-reduce.17.cloned.1.call-start = ((), (), s32[]{:S(2)}) async-start(), calls=%async_computation | async-start | bytes 1572864 | tf_op jit(solution)/shard_map/psum | solution.py:318
  10.4 42.9 %copy-start.29 = (f32[1,1024]{1,0:T(1,128)}, f32[1,1024]{1,0:T(1,128)S(1)}, u32[]{:S(2)}) copy-start(f32[1,1024]{1,0:T(1,128)S(1)} %get-tuple-element.85) | copy-start | bytes 12292
  10.4 42.9 %copy-start.31 = (f32[1,1024]{1,0:T(1,128)}, f32[1,1024]{1,0:T(1,128)S(1)}, u32[]{:S(2)}) copy-start(f32[1,1024]{1,0:T(1,128)S(1)} %get-tuple-element.86) | copy-start | bytes 12292
  10.5 42.9 %copy-start.33 = (f32[1,1024]{1,0:T(1,128)}, f32[1,1024]{1,0:T(1,128)S(1)}, u32[]{:S(2)}) copy-start(f32[1,1024]{1,0:T(1,128)S(1)} %get-tuple-element.87) | copy-start | bytes 12292
  10.5 42.9 %copy-start.35 = (f32[1,1024]{1,0:T(1,128)}, f32[1,1024]{1,0:T(1,128)S(1)}, u32[]{:S(2)}) copy-start(f32[1,1024]{1,0:T(1,128)S(1)} %get-tuple-element.88) | copy-start | bytes 12292
  10.5 32.9 %copy-start.47 = (s32[768]{0:T(1024)S(1)}, s32[768]{0:T(1024)}, u32[]{:S(2)}) copy-start(s32[768]{0:T(1024)} %param.15) | copy-start | bytes 9220
  10.5 32.9 %copy-start.48 = (s32[768]{0:T(1024)S(1)}, s32[768]{0:T(1024)}, u32[]{:S(2)}) copy-start(s32[768]{0:T(1024)} %param.16) | copy-start | bytes 9220
  10.5 33.0 %copy-start.14 = (bf16[768,2048]{1,0:T(8,128)(2,1)S(1)}, bf16[768,2048]{1,0:T(8,128)(2,1)}, u32[]{:S(2)}) copy-start(bf16[768,2048]{1,0:T(8,128)(2,1)} %param.14) | copy-start | bytes 9437188
  10.5 33.0 %copy-start.37 = (f32[2048]{0:T(1024)S(1)}, f32[2048]{0:T(1024)}, u32[]{:S(2)}) copy-start(f32[2048]{0:T(1024)} %param.17) | copy-start | bytes 24580
  43.5 9.9 copy-start.42
  43.5 9.9 copy-start.43
  59.5 331.0 %all-reduce.19.cloned.1.call-start = ((), (), s32[]{:S(2)}) async-start(), calls=%async_computation.1 | async-start | bytes 196608 | tf_op jit(solution)/shard_map/psum | solution.py:365
  59.8 12.9 %slice-start = ((s8[8388608]{0:T(1024)(128)(4,1)}), s8[4194304]{0:T(1024)(128)(4,1)S(1)}, s32[]{:S(2)}) async-start(s8[8388608]{0:T(1024)(128)(4,1)} %bitcast.121), calls=%async_computation.4 | async-start | bytes 8388608
  67.0 10.9 %slice-start.8 = ((s8[8388608]{0:T(1024)(128)(4,1)}), s8[4194304]{0:T(1024)(128)(4,1)S(1)}, s32[]{:S(2)}) async-start(s8[8388608]{0:T(1024)(128)(4,1)} %bitcast.150), calls=%async_computation.12 | async-start | bytes 8388608
  77.9 29.2 %copy-start.22 = (bf16[2,128,1024]{2,1,0:T(8,128)(2,1)S(1)}, bf16[2,128,1024]{2,1,0:T(8,128)(2,1)}, u32[]{:S(2)}) copy-start(bf16[2,128,1024]{2,1,0:T(8,128)(2,1)} %param.22) | copy-start | bytes 1572868
  83.4 27.7 %copy-start.6 = (f32[2,8,8,128]{3,2,1,0:T(8,128)}, f32[2,8,8,128]{3,2,1,0:T(8,128)S(1)}, u32[]{:S(2)}) copy-start(f32[2,8,8,128]{3,2,1,0:T(8,128)S(1)} %copy.50) | copy-start | bytes 196612
  111.0 27.4 %copy-start.1 = (bf16[768,1024]{1,0:T(8,128)(2,1)S(1)}, bf16[768,1024]{1,0:T(8,128)(2,1)}, u32[]{:S(2)}) copy-start(bf16[768,1024]{1,0:T(8,128)(2,1)} %copy-done) | copy-start | bytes 4718596
  138.5 77.6 %copy-start.11 = (bf16[768,1024]{1,0:T(8,128)(2,1)}, bf16[768,1024]{1,0:T(8,128)(2,1)S(1)}, u32[]{:S(2)}) copy-start(bf16[768,1024]{1,0:T(8,128)(2,1)S(1)} %get-tuple-element.22) | copy-start | bytes 4718596
  139.4 77.9 %copy-start.23 = (bf16[2,128,1024]{2,1,0:T(8,128)(2,1)S(1)}, bf16[2,128,1024]{2,1,0:T(8,128)(2,1)}, u32[]{:S(2)}) copy-start(bf16[2,128,1024]{2,1,0:T(8,128)(2,1)} %param.22) | copy-start | bytes 1572868
  255.3 22.4 %slice-start.6 = ((s8[8388608]{0:T(1024)(128)(4,1)}), s8[4194304]{0:T(1024)(128)(4,1)S(1)}, s32[]{:S(2)}) async-start(s8[8388608]{0:T(1024)(128)(4,1)} %bitcast.127), calls=%async_computation.10 | async-start | bytes 8388608
  258.6 14.2 %copy-start.30 = (f32[1,1024]{1,0:T(1,128)S(1)}, f32[1,1024]{1,0:T(1,128)}, u32[]{:S(2)}) copy-start(f32[1,1024]{1,0:T(1,128)} %copy-done.29) | copy-start | bytes 12292
  258.6 14.2 %copy-start.32 = (f32[1,1024]{1,0:T(1,128)S(1)}, f32[1,1024]{1,0:T(1,128)}, u32[]{:S(2)}) copy-start(f32[1,1024]{1,0:T(1,128)} %copy-done.31) | copy-start | bytes 12292
  258.6 14.2 %copy-start.34 = (f32[1,1024]{1,0:T(1,128)S(1)}, f32[1,1024]{1,0:T(1,128)}, u32[]{:S(2)}) copy-start(f32[1,1024]{1,0:T(1,128)} %copy-done.33) | copy-start | bytes 12292
  258.7 14.2 %copy-start.36 = (f32[1,1024]{1,0:T(1,128)S(1)}, f32[1,1024]{1,0:T(1,128)}, u32[]{:S(2)}) copy-start(f32[1,1024]{1,0:T(1,128)} %copy-done.35) | copy-start | bytes 12292
  258.7 19.0 %slice-start.7 = ((s8[8388608]{0:T(1024)(128)(4,1)}), s8[4194304]{0:T(1024)(128)(4,1)S(1)}, s32[]{:S(2)}) async-start(s8[8388608]{0:T(1024)(128)(4,1)} %bitcast.127), calls=%async_computation.11 | async-start | bytes 8388608
  272.9 10.6 %slice-start.4 = ((s8[8388608]{0:T(1024)(128)(4,1)}), s8[4194304]{0:T(1024)(128)(4,1)S(1)}, s32[]{:S(2)}) async-start(s8[8388608]{0:T(1024)(128)(4,1)} %bitcast.125), calls=%async_computation.8 | async-start | bytes 8388608
  277.7 11.6 %slice-start.2 = ((s8[8388608]{0:T(1024)(128)(4,1)}), s8[4194304]{0:T(1024)(128)(4,1)S(1)}, s32[]{:S(2)}) async-start(s8[8388608]{0:T(1024)(128)(4,1)} %bitcast.123), calls=%async_computation.6 | async-start | bytes 8388608
  300.0 277.3 %all-reduce.23.cloned.1.call-start = ((), (), s32[]{:S(2)}) async-start(), calls=%async_computation.3 | async-start | bytes 12582912 | tf_op jit(solution)/shard_map/psum | solution.py:329
  330.6 575.9 %all-reduce.21.cloned.1.call-start = ((), (), s32[]{:S(2)}) async-start(), calls=%async_computation.2 | async-start | bytes 52690944 | tf_op jit(solution)/shard_map/psum | solution.py:334
  390.5 186.9 %copy-start.17 = (bf16[768,2048]{1,0:T(8,128)(2,1)S(1)}, bf16[768,2048]{1,0:T(8,128)(2,1)}, u32[]{:S(2)}) copy-start(bf16[768,2048]{1,0:T(8,128)(2,1)} %param.14) | copy-start | bytes 9437188
  390.5 186.9 %copy-start.39 = (f32[2048]{0:T(1024)S(1)}, f32[2048]{0:T(1024)}, u32[]{:S(2)}) copy-start(f32[2048]{0:T(1024)} %param.17) | copy-start | bytes 24580
  577.4 18.5 %copy-start.40 = (f32[768]{0:T(1024)S(1)}, f32[768]{0:T(1024)}, u32[]{:S(2)}) copy-start(f32[768]{0:T(1024)} %get-tuple-element.91) | copy-start | bytes 9220
  (31 other events, 145.9 us)
Sparse Core Ops, SparseCore 0:
  59.6 46.3 all-reduce.16
  300.2 50.0 all-reduce.18
  353.3 223.9 all-reduce.22
  583.8 322.6 all-reduce.20

commit v2 on v1

--- a/solution.py
+++ b/solution.py
@@ -114,20 +114,882 @@
     )(bc, pre, act, z, gg, keep, a_log3, skip)
 
 
-def scan_backward_kernel(states, groups, rows, unroll,
-                         bc_ref, pre_ref, act_ref, mixed_ref, keep_ref, alog_ref, skip_ref, h_ref, start_ref,
-                         pgrad_ref, apart_ref, bcg_ref, ratesum_ref, skipsum_ref,
-                         rate_scr, decay_scr, carry_scr, sum_scr, sk_scr, u_scr, dy_scr, w_scr, s_scr, p_scr, q_scr):
+MESH = pl.DeviceIdType.MESH
+DMA = pltpu.SemaphoreType.DMA
+
+
+def add_rows(target, left, right, rows, slab):
+    def body(i, nothing):
+        at = pl.ds(pl.multiple_of(i * slab, slab), slab)
+        target[at, :] = (left[at, :].astype(jnp.float32) + right[at, :].astype(jnp.float32)).astype(jnp.bfloat16)
+        return nothing
+    lax.fori_loop(0, rows // slab, body, 0)
+
+
+def place():
+    dp = lax.axis_index("dp")
+    x, y, core = (dp // 2) % 2, dp // 4, dp % 2
+    return x, y, {"dp": dp + 2 - 4 * x}, {"dp": dp + 4 - 8 * y}, {"dp": dp + 1 - 2 * core}
+
+
+def greet():
+    z = lax.axis_index("tensor")
+    barrier = pltpu.get_barrier_semaphore()
+    for target in place()[2:]:
+        pl.semaphore_signal(barrier, inc=1, device_id=target, device_id_type=MESH)
+
+    @pl.when(z > 0)
+    def _():
+        pl.semaphore_signal(barrier, inc=1, device_id={"tensor": z - 1}, device_id_type=MESH)
+
+    @pl.when(z < 3)
+    def _():
+        pl.semaphore_signal(barrier, inc=1, device_id={"tensor": z + 1}, device_id_type=MESH)
+
+    @pl.when((z > 0) & (z < 3))
+    def _():
+        pl.semaphore_wait(barrier, 5)
+
+    @pl.when((z == 0) | (z == 3))
+    def _():
+        pl.semaphore_wait(barrier, 4)
+
+
+class Exchange:
+    def __init__(self, prod, out, held, half_buf, quarter_buf, sems, summed=None):
+        self.summed = summed
+        self.prod, self.out, self.held, self.half_buf, self.quarter_buf = prod, out, held, half_buf, quarter_buf
+        (self.half_send, self.half_recv, self.quarter_send, self.quarter_recv,
+         self.share_send, self.share_recv, self.core_send, self.core_recv, self.local) = sems
+        x, y, self.to_x, self.to_y, self.to_core = place()
+        self.firsts, self.seconds = (x, y), (y, x)
+        self.ways = ((self.to_x, self.to_y), (self.to_y, self.to_x))
+        self.side = half_buf.shape[2]
+
+    @staticmethod
+    def scratch(side, depth):
+        low = jnp.bfloat16
+        return [pltpu.VMEM((2, 2, side, depth), low), pltpu.VMEM((2, 2, side, depth), low), pltpu.VMEM((2, side, depth), low),
+                DMA((2, 2)), DMA((2, 2)), DMA((2,)), DMA((2,)), DMA((2, 4)), DMA((2, 4)), DMA((2, 4)), DMA((2, 4)), DMA((2, 3))]
+
+    def rows(self, mode, k, mine):
+        first, second = self.firsts[mode], self.seconds[mode]
+        half = first if mine else 1 - first
+        quarter = 1 - second if k == 0 else second
+        return pl.ds(pl.multiple_of((half * 2 + quarter) * self.side, self.side), self.side)
+
+    def half_copy(self, mode, k):
+        return pltpu.make_async_remote_copy(
+            src_ref=self.prod.at[mode, self.rows(mode, k, False)], dst_ref=self.half_buf.at[mode, k],
+            send_sem=self.half_send.at[mode, k], recv_sem=self.half_recv.at[mode, k],
+            device_id=self.ways[mode][0], device_id_type=MESH)
+
+    def keep_copy(self, mode, k):
+        return pltpu.make_async_copy(self.prod.at[mode, self.rows(mode, k, True)], self.held.at[mode, k], self.local.at[mode, k])
+
+    def quarter_copy(self, mode):
+        return pltpu.make_async_remote_copy(
+            src_ref=self.half_buf.at[mode, 0], dst_ref=self.quarter_buf.at[mode],
+            send_sem=self.quarter_send.at[mode], recv_sem=self.quarter_recv.at[mode],
+            device_id=self.ways[mode][1], device_id_type=MESH)
+
+    def share_copy(self, mode, k):
+        own = self.held.at[mode, 1]
+        if k == 3:
+            source, way = (self.out.at[mode, 0, 1], self.to_x) if mode == 0 else (self.out.at[mode, 0, 2], self.to_y)
+        else:
+            source, way = own, self.to_y if k == 1 else self.to_x
+        return pltpu.make_async_remote_copy(
+            src_ref=source, dst_ref=self.out.at[mode, 0, k], send_sem=self.share_send.at[mode, k],
+            recv_sem=self.share_recv.at[mode, k], device_id=way, device_id_type=MESH)
+
+    def core_copy(self, mode, k):
+        return pltpu.make_async_remote_copy(
+            src_ref=self.held.at[mode, 1] if k == 0 else self.out.at[mode, 0, k], dst_ref=self.out.at[mode, 1, k],
+            send_sem=self.core_send.at[mode, k], recv_sem=self.core_recv.at[mode, k],
+            device_id=self.to_core, device_id_type=MESH)
+
+    def out_copy(self, mode):
+        return pltpu.make_async_copy(self.held.at[mode, 1], self.out.at[mode, 0, 0], self.local.at[mode, 2])
+
+    def start_shares(self, mode):
+        for k in ((1, 2) if mode == 0 else (2, 1)):
+            self.share_copy(mode, k).start()
+        self.core_copy(mode, 0).start()
+        self.out_copy(mode).start()
+
+    def event(self, number):
+        if number == 0:
+            for k in range(2):
+                for mode in range(2):
+                    self.half_copy(mode, k).start()
+                    self.keep_copy(mode, k).start()
+        elif number == 1:
+            for mode in range(2):
+                self.keep_copy(mode, 0).wait()
+                self.half_copy(mode, 0).wait_recv()
+                add_rows(self.half_buf.at[mode, 0], self.half_buf.at[mode, 0], self.held.at[mode, 0], self.side, 32)
+                self.quarter_copy(mode).start()
+        elif number == 2:
+            for mode in range(2):
+                self.keep_copy(mode, 1).wait()
+                self.half_copy(mode, 1).wait_recv()
+                add_rows(self.half_buf.at[mode, 1], self.half_buf.at[mode, 1], self.held.at[mode, 1], self.side, 32)
+        elif number == 3:
+            for mode in range(2):
+                self.quarter_copy(mode).wait_recv()
+                add_rows(self.held.at[mode, 1], self.half_buf.at[mode, 1], self.quarter_buf.at[mode], self.side, 32)
+                self.start_shares(mode)
+        elif number == 4:
+            for mode in range(2):
+                k = 1 if mode == 0 else 2
+                self.share_copy(mode, k).wait_recv()
+                self.share_copy(mode, 3).start()
+                self.core_copy(mode, k).start()
+        elif number == 5:
+            for mode in range(2):
+                k = 2 if mode == 0 else 1
+                self.share_copy(mode, k).wait_recv()
+                self.core_copy(mode, k).start()
+        elif number == 6:
+            for mode in range(2):
+                self.share_copy(mode, 3).wait_recv()
+                self.core_copy(mode, 3).start()
+        elif number == 8:
+            for mode in range(2):
+                pltpu.make_async_copy(self.prod.at[mode], self.held.at[mode, 1], self.local.at[mode, 1]).start()
+        elif number == 9:
+            for mode in range(2):
+                pltpu.make_async_copy(self.prod.at[mode], self.held.at[mode, 1], self.local.at[mode, 1]).wait()
+                self.start_shares(mode)
+        elif number == 7:
+            for mode in range(2):
+                if self.summed is None:
+                    for k in range(2):
+                        self.half_copy(mode, k).wait_send()
+                    self.quarter_copy(mode).wait_send()
+                for k in range(1, 4):
+                    self.share_copy(mode, k).wait_send()
+                for k in range(4):
+                    self.core_copy(mode, k).wait_send()
+                    self.core_copy(mode, k).wait_recv()
+                self.out_copy(mode).wait()
+
+
+class LineSum:
+    def __init__(self, part, res, acc, red, sems):
+        self.part, self.res, self.acc, self.red = part, res, acc, red
+        self.red_send, self.red_recv, self.back_send, self.back_recv, self.local = sems
+        self.z = lax.axis_index("tensor")
+        self.near = jnp.where(self.z < 2, 1, 0)
+        self.pieces, self.rows = acc.shape[1], acc.shape[2]
+        self.turns = 2 * self.pieces + 2
+
+    @staticmethod
+    def scratch(pieces, rows, width):
+        low = jnp.bfloat16
+        return [pltpu.VMEM((2, pieces, rows, width), low), pltpu.VMEM((2, pieces, rows, width), low),
+                DMA((2, pieces)), DMA((2, pieces)), DMA((2, pieces)), DMA((2, pieces)), DMA((2,))]
+
+    def place_of(self, half):
+        along = jnp.where(half == 0, 3 - self.z, self.z)
+        return along == 0, along == 3
+
+    def red_copy(self, half, c):
+        return pltpu.make_async_remote_copy(
+            src_ref=self.acc.at[half, c], dst_ref=self.red.at[half, c], send_sem=self.red_send.at[half, c],
+            recv_sem=self.red_recv.at[half, c], device_id={"tensor": self.z + 2 * half - 1}, device_id_type=MESH)
+
+    def back_copy(self, half, c, source):
+        return pltpu.make_async_remote_copy(
+            src_ref=source, dst_ref=self.res.at[half, c], send_sem=self.back_send.at[half, c],
+            recv_sem=self.back_recv.at[half, c], device_id={"tensor": self.z - 2 * half + 1}, device_id_type=MESH)
+
+    def load(self):
+        return pltpu.make_async_copy(self.part, self.acc, self.local.at[0])
+
+    def own(self, half):
+        return pltpu.make_async_copy(self.acc.at[half], self.res.at[half], self.local.at[1])
+
+    def begin(self):
+        self.load().wait()
+        for half in range(2):
+            begins, _ = self.place_of(half)
+
+            @pl.when(begins)
+            def _():
+                for c in range(self.pieces):
+                    self.red_copy(half, c).start()
+
+    def reduce_step(self, c, half):
+        begins, ends = self.place_of(half)
+
+        @pl.when(jnp.logical_not(begins))
+        def _():
+            self.red_copy(half, c).wait_recv()
+            add_rows(self.acc.at[half, c], self.acc.at[half, c], self.red.at[half, c], self.rows, 16)
+
+            @pl.when(ends)
+            def _():
+                self.back_copy(half, c, self.acc.at[half, c]).start()
+
+            @pl.when(jnp.logical_not(ends))
+            def _():
+                self.red_copy(half, c).start()
+
+    def back_step(self, c, half):
+        begins, ends = self.place_of(half)
+
+        @pl.when(jnp.logical_not(ends))
+        def _():
+            self.back_copy(half, c, self.res.at[half, c]).wait_recv()
+
+            @pl.when(jnp.logical_not(begins))
+            def _():
+                self.back_copy(half, c, self.res.at[half, c]).start()
+
+    def turn(self, turn):
+        near, far = self.near, 1 - self.near
+        if turn < self.pieces:
+            self.reduce_step(turn, near)
+        if 1 <= turn <= self.pieces:
+            self.reduce_step(turn - 1, far)
+        back = turn - self.pieces
+        if 0 <= back < self.pieces:
+            self.back_step(back, far)
+        if 1 <= back <= self.pieces:
+            self.back_step(back - 1, near)
+
+    def finish(self):
+        for half in range(2):
+            begins, ends = self.place_of(half)
+
+            @pl.when(ends)
+            def _():
+                self.own(half).start()
+                self.own(half).wait()
+
+            @pl.when(jnp.logical_not(ends))
+            def _():
+                for c in range(self.pieces):
+                    self.red_copy(half, c).wait_send()
+
+            @pl.when(jnp.logical_not(begins))
+            def _():
+                for c in range(self.pieces):
+                    self.back_copy(half, c, self.res.at[half, c]).wait_send()
+
+
+def tail_kernel(count, *refs):
+    prods, part = refs[:count], refs[count]
+    outs, res = refs[count + 1:2 * count + 1], refs[2 * count + 1]
+    scr = refs[2 * count + 2:]
+    line = LineSum(part, res, scr[0], scr[1], scr[2:7])
+    swaps = [Exchange(prods[i], outs[i], *scr[7 + 12 * i:10 + 12 * i], scr[10 + 12 * i:19 + 12 * i]) for i in range(count)]
+    swaps[0].summed = True
+    line.load().start()
+    swaps[0].event(8)
+    greet()
+    swaps[1].event(0)
+    swaps[0].event(9)
+    line.begin()
+    last = line.turns
+    plan = {4: [(1, 1)], 6: [(0, 4)], 8: [(1, 2)], 10: [(0, 5)], 12: [(1, 3)], 15: [(0, 6)], 17: [(1, 4)], 20: [(1, 5)],
+            24: [(1, 6)]}
+    for turn in range(last):
+        line.turn(turn)
+        for which, number in plan.get(turn, []):
+            swaps[which].event(number)
+    for swapped in swaps:
+        swapped.event(7)
+    line.finish()
+
+
+def tail_exchange(products, normed_part, pieces=12):
+    count = len(products)
+    side, depth = products[0].shape[1:]
+    tokens, width = normed_part.shape
+    part = normed_part.reshape(2, pieces, tokens // 2 // pieces, width)
+    low = jnp.bfloat16
+    anywhere = pl.BlockSpec(memory_space=pl.ANY)
+    scratch = LineSum.scratch(*part.shape[1:])
+    for _ in products:
+        scratch = scratch + Exchange.scratch(side, depth)
+    outs = pl.pallas_call(
+        functools.partial(tail_kernel, count),
+        in_specs=[anywhere] * (count + 1),
+        out_specs=[anywhere] * (count + 1),
+        out_shape=[jax.ShapeDtypeStruct((2, 2, 4, side, depth), low)] * count + [jax.ShapeDtypeStruct(part.shape, low)],
+        scratch_shapes=scratch,
+        cost_estimate=pl.CostEstimate(flops=100_000_000, bytes_accessed=300_000_000, transcendentals=0),
+        compiler_params=pltpu.CompilerParams(collective_id=1, has_side_effects=True, vmem_limit_bytes=40 * 1024 * 1024),
+        name="tail_exchange",
+    )(*products, part)
+    return outs[:count], outs[count].reshape(tokens, width)
+
+
+NT = (((1,), (1,)), ((), ()))
+TN = (((0,), (0,)), ((), ()))
+
+
+def dot_f32(left, right, dims=(((1,), (0,)), ((), ()))):
+    return lax.dot_general(left, right, dims, preferred_element_type=jnp.float32)
+
+
+def widened(column_block, width):
+    return jnp.concatenate([column_block] * (width // LANES), axis=1)
+
+
+def middle_kernel(pre_grad, act_part, coeff, conv_sum, inner_x, act_b, rank_b, dt_proj, x_wide, conv_w, docs, modes,
+                  gate_pair, normed_t, inv, extra, hidden, in_gate, in_inner,
+                  rows_out, normed_out, gate_own, inner_prod, gate_prod,
+                  w_buf, mask_buf, pair_buf, conv_buf, stage, stage_n, hid_buf, proj_buf, proj_recv, proj_fin, gain_buf, gain_recv,
+                  held, half_buf, quarter_buf,
+                  half_send, half_recv, quarter_send, quarter_recv, keep_sems,
+                  red_send, red_recv, all_send, all_recv, core_sems, gain_send, gain_recv_sem, w_sems, stage_sems, n_sems, hid_sems):
+    tokens, channels = pre_grad.shape
+    low = jnp.bfloat16
+    rank_dim = dt_proj.shape[1]
+    z = lax.axis_index("tensor")
+    x, y, to_x, to_y, to_core = place()
+    share = tokens // 4
+    gate = Exchange(gate_prod, None, held, half_buf, quarter_buf,
+                    (half_send, half_recv, quarter_send, quarter_recv, None, None, None, None, keep_sems))
+    width = hidden.shape[1]
+    slices = width // w_buf.shape[2]
+    cut = w_buf.shape[2]
+
+    def z_at(off):
+        return {"tensor": (z + off) % 4}
+
+    barrier = pltpu.get_barrier_semaphore()
+    for target in (to_x, to_y, to_core, z_at(1), z_at(2), z_at(3)):
+        pl.semaphore_signal(barrier, inc=1, device_id=target, device_id_type=MESH)
+    pl.semaphore_wait(barrier, 6)
+
+    def weight_copies(i):
+        slot = i % 2
+        found = []
+        for j, source in enumerate((in_gate, in_inner)):
+            for m in range(2):
+                found.append(pltpu.make_async_copy(source.at[m, pl.ds(i * cut, cut)], w_buf.at[slot, 2 * j + m],
+                                                   w_sems.at[slot, 2 * j + m]))
+        found.append(pltpu.make_async_copy(hidden.at[:, pl.ds(i * cut, cut)], hid_buf.at[slot], hid_sems.at[slot]))
+        return found
+
+    for i in range(2):
+        for copy in weight_copies(i):
+            copy.start()
+
+    block = 128
+
+    def proj_block(i, nothing):
+        at = pl.ds(pl.multiple_of(i * block, block), block)
+        grad = pre_grad[at, :]
+        part = dot_f32(grad * widened(modes[0, at, :], channels), dt_proj[0], NT)
+        part = part + dot_f32(grad * widened(modes[1, at, :], channels), dt_proj[1], NT)
+        proj_buf[at, 0:rank_dim] = part.astype(low)
+        proj_buf[at, rank_dim:rank_dim + LANES] = coeff[at, :].astype(low)
+        return nothing
+
+    lax.fori_loop(0, tokens // block, proj_block, 0)
+
+    def red_copy(off):
+        return pltpu.make_async_remote_copy(
+            src_ref=proj_buf.at[pl.ds(pl.multiple_of(((z + off) % 4) * share, share), share)], dst_ref=proj_recv.at[off - 1],
+            send_sem=red_send.at[off - 1], recv_sem=red_recv.at[off - 1], device_id=z_at(off), device_id_type=MESH)
+
+    for off in (1, 2, 3):
+        red_copy(off).start()
+
+    def product(pair, target, number):
+        pair_tokens = pair.shape[0]
+        tall = stage.shape[1]
+        turns = normed_t.shape[0] // tall
+        for m in range(2):
+            def mask_rows(i, nothing):
+                at = pl.ds(pl.multiple_of(i * block, block), block)
+                mask_buf[at, :] = pair[at, :] * widened(modes[m, at, :], channels)
+                return nothing
+            lax.fori_loop(0, pair_tokens // block, mask_rows, 0)
+            for j in range(turns):
+                slot = (m * turns + j) % 2
+                copy = pltpu.make_async_copy(stage.at[slot], target.at[m, pl.ds(j * tall, tall)], stage_sems.at[slot])
+                if m * turns + j >= 2:
+                    copy.wait()
+                stage[slot] = dot_f32(normed_t[pl.ds(j * tall, tall), :], mask_buf[...]).astype(low)
+                copy.start()
+        for slot in range(2):
+            pltpu.make_async_copy(stage.at[slot], target.at[0, pl.ds(0, tall)], stage_sems.at[slot]).wait()
+
+    product(gate_pair, gate_prod, 0)
+    gate.event(0)
+
+    for off in (1, 2, 3):
+        red_copy(off).wait_recv()
+    mine = pl.ds(pl.multiple_of(z * share, share), share)
+    total = proj_buf[mine, :].astype(jnp.float32)
+    for k in range(3):
+        total = total + proj_recv[k].astype(jnp.float32)
+    proj_fin[mine, :] = total.astype(low)
+
+    def all_copy(off):
+        return pltpu.make_async_remote_copy(
+            src_ref=proj_fin.at[mine], dst_ref=proj_fin.at[mine], send_sem=all_send.at[off - 1],
+            recv_sem=all_recv.at[off - 1], device_id=z_at(off), device_id_type=MESH)
+
+    for off in (1, 2, 3):
+        all_copy(off).start()
+    span = x_wide.shape[1] - 96
+    mode_rows = span + rank_dim
+    for m in range(2):
+        ranks = rank_b[...] * modes[m, pl.ds(0, tokens), :]
+        rows_out[pl.ds(m * mode_rows + span, rank_dim), :] = dot_f32(ranks, pre_grad[...], TN).astype(low)
+    def dt_sums(i, carried):
+        at = pl.ds(pl.multiple_of(i * block, block), block)
+        grad = pre_grad[at, :].astype(jnp.float32)
+        first = jnp.sum(grad * widened(modes[0, at, :].astype(jnp.float32), channels), axis=0, keepdims=True)
+        return carried[0] + first, carried[1] + jnp.sum(grad, axis=0, keepdims=True) - first
+
+    none_row = jnp.zeros((1, channels), jnp.float32)
+    bias0, bias1 = lax.fori_loop(0, tokens // block, dt_sums, (none_row, none_row))
+    for off in (1, 2, 3):
+        all_copy(off).wait_recv()
+
+    def act_block(i, bias):
+        at = pl.ds(pl.multiple_of(i * block, block), block)
+        proj = proj_fin[at, :]
+        two = proj.shape[1]
+        back = dot_f32(proj * widened(modes[0, at, :], two), x_wide[0])
+        back = back + dot_f32(proj * widened(modes[1, at, :], two), x_wide[1])
+        value = conv_sum[at, :]
+        sig = jax.nn.sigmoid(value)
+        grad = (act_part[at, :] + back) * sig * (1.0 + value * (1.0 - sig))
+        conv_buf[at, :] = grad
+        return bias + jnp.sum(grad, axis=0, keepdims=True)
+
+    conv_buf[pl.ds(tokens, 8), :] = jnp.zeros((8, channels), jnp.float32)
+    bias = lax.fori_loop(0, tokens // block, act_block, none_row)
+    gate.event(1)
+    taps = conv_w.shape[0]
+    thin = 64
+
+    def conv_block(i, sums):
+        base = pl.multiple_of(i * thin, thin)
+        grads = conv_buf[pl.ds(base, thin + 8), :]
+        doc = docs[pl.ds(base, thin), :]
+        inner = inner_x[pl.ds(base, thin), :]
+        result = jnp.zeros((thin, channels), jnp.float32)
+        new = []
+        for offset in range(taps):
+            moved = grads[offset:offset + thin, :] * doc[:, offset:offset + 1]
+            tap = taps - 1 - offset
+            result = result + moved * conv_w[tap:tap + 1, :]
+            new.append(sums[offset] + jnp.sum(moved * inner, axis=0, keepdims=True))
+        pair_buf[pl.ds(base, thin), :] = result.astype(low)
+        return tuple(new)
+
+    sums = lax.fori_loop(0, tokens // thin, conv_block, (none_row,) * taps)
+
+    def core_copy():
+        return pltpu.make_async_remote_copy(
+            src_ref=pair_buf.at[pl.ds(0, tokens)], dst_ref=pair_buf.at[pl.ds(tokens, tokens)],
+            send_sem=core_sems.at[0], recv_sem=core_sems.at[1], device_id=to_core, device_id_type=MESH)
+
+    core_copy().start()
+
+    for i in range(slices):
+        slot = i % 2
+        for copy in weight_copies(i):
+            copy.wait()
+        third = tokens // 3
+        out_copy = pltpu.make_async_copy(stage_n.at[slot], normed_out.at[:, pl.ds(i * cut, cut)], n_sems.at[slot])
+        if i >= 2:
+            out_copy.wait()
+
+        def normed_rows(j, gain, slot=slot):
+            at = pl.ds(pl.multiple_of(j * third, third), third)
+            gate_grad, grad = gate_pair[at, :], pair_buf[at, :]
+            zero = dot_f32(gate_grad, w_buf[slot, 0], NT) + dot_f32(grad, w_buf[slot, 2], NT)
+            one = dot_f32(gate_grad, w_buf[slot, 1], NT) + dot_f32(grad, w_buf[slot, 3], NT)
+            picked = jnp.where(inv[at, 1:2] > 0.5, zero, one)
+            stage_n[slot, at, :] = picked.astype(low)
+            return gain + jnp.sum(picked * hid_buf[slot, at, :].astype(jnp.float32) * inv[at, 0:1], axis=0, keepdims=True)
+
+        gain = lax.fori_loop(0, 3, normed_rows, jnp.zeros((1, cut), jnp.float32))
+        gain_buf[:, pl.ds(i * cut, cut)] = jnp.broadcast_to(gain, (8, cut))
+        out_copy.start()
+        if i + 2 < slices:
+            for copy in weight_copies(i + 2):
+                copy.start()
+        if i == 1:
+            gate.event(2)
+    for slot in range(2):
+        pltpu.make_async_copy(stage_n.at[slot], normed_out.at[:, pl.ds(0, cut)], n_sems.at[slot]).wait()
+
+    def gain_copy(off):
+        return pltpu.make_async_remote_copy(
+            src_ref=gain_buf, dst_ref=gain_recv.at[off - 1], send_sem=gain_send.at[off - 1],
+            recv_sem=gain_recv_sem.at[off - 1], device_id=z_at(off), device_id_type=MESH)
+
+    for off in (1, 2, 3):
+        gain_copy(off).start()
+    core_copy().wait_recv()
+    product(pair_buf, inner_prod, 1)
+    for m in range(2):
+        proj = proj_fin[...] * widened(modes[m, pl.ds(0, tokens), :], proj_fin.shape[1])
+        rows_out[pl.ds(m * mode_rows, span), :] = dot_f32(proj, act_b[...], TN)[:span].astype(low)
+    for off in (1, 2, 3):
+        gain_copy(off).wait_recv()
+    gain = gain_buf[0:1, :] + gain_recv[0, 0:1, :] + gain_recv[1, 0:1, :] + gain_recv[2, 0:1, :]
+    gains = [gain[:, k * channels:(k + 1) * channels] for k in range(width // channels)]
+    tail_rows = list(sums[::-1]) + [bias, bias0, bias1, extra[...]] + gains
+    used = taps + 3 + extra.shape[0] + len(gains)
+    tail_rows.append(jnp.zeros((32 - used, channels), jnp.float32))
+    rows_out[pl.ds(2 * mode_rows, 32), :] = jnp.concatenate(tail_rows, axis=0).astype(low)
+    for mode in range(2):
+        gate.quarter_copy(mode).wait_recv()
+        add_rows(gate_own.at[mode], half_buf.at[mode, 1], quarter_buf.at[mode], gate.side, 32)
+        gate.quarter_copy(mode).wait_send()
+        for k in range(2):
+            gate.half_copy(mode, k).wait_send()
+    for off in (1, 2, 3):
+        red_copy(off).wait_send()
+        all_copy(off).wait_send()
+        gain_copy(off).wait_send()
+    core_copy().wait_send()
+
+
+def middle(pre_grad, act_part, coeff, conv_sum, inner_x, act_b, rank_b, dt_proj, x_wide, conv_w, docs, modes,
+           gate_pair, normed_t, inv, extra, hidden, in_gate, in_inner):
+    tokens, channels = pre_grad.shape
+    width = hidden.shape[1]
+    low = jnp.bfloat16
+    side = normed_t.shape[0] // 4
+    cut = 512
+    mode_rows = x_wide.shape[1] - 96 + dt_proj.shape[1]
+    vmem, anywhere = pl.BlockSpec(memory_space=pltpu.VMEM), pl.BlockSpec(memory_space=pl.ANY)
+    return pl.pallas_call(
+        middle_kernel,
+        in_specs=[vmem] * 16 + [anywhere] * 3,
+        out_specs=[vmem, anywhere, vmem, anywhere, anywhere],
+        out_shape=[
+            jax.ShapeDtypeStruct((2 * mode_rows + 32, channels), low),
+            jax.ShapeDtypeStruct((tokens, width), low),
+            jax.ShapeDtypeStruct((2, side, channels), low),
+            jax.ShapeDtypeStruct((2, 4 * side, channels), low),
+            jax.ShapeDtypeStruct((2, 4 * side, channels), low),
+        ],
+        scratch_shapes=[
+            pltpu.VMEM((2, 4, cut, channels), low),
+            pltpu.VMEM((2 * tokens, channels), low),
+            pltpu.VMEM((2 * tokens, channels), low),
+            pltpu.VMEM((tokens + 8, channels), jnp.float32),
+            pltpu.VMEM((2, 2 * side, channels), low),
+            pltpu.VMEM((2, tokens, cut), low),
+            pltpu.VMEM((2, tokens, cut), low),
+            pltpu.VMEM((tokens, 2 * LANES), low),
+            pltpu.VMEM((3, tokens // 4, 2 * LANES), low),
+            pltpu.VMEM((tokens, 2 * LANES), low),
+            pltpu.VMEM((8, width), jnp.float32),
+            pltpu.VMEM((3, 8, width), jnp.float32),
+            pltpu.VMEM((2, 2, side, channels), low),
+            pltpu.VMEM((2, 2, side, channels), low),
+            pltpu.VMEM((2, side, channels), low),
+            DMA((2, 2)), DMA((2, 2)), DMA((2,)), DMA((2,)), DMA((2, 3)),
+            DMA((3,)), DMA((3,)), DMA((3,)), DMA((3,)), DMA((2,)), DMA((3,)), DMA((3,)),
+            DMA((2, 4)), DMA((2,)), DMA((2,)), DMA((2,)),
+        ],
+        cost_estimate=pl.CostEstimate(flops=27_000_000_000, bytes_accessed=60_000_000, transcendentals=1_000_000),
+        compiler_params=pltpu.CompilerParams(collective_id=3, has_side_effects=True, vmem_limit_bytes=61 * 1024 * 1024),
+        name="middle",
+    )(pre_grad, act_part, coeff, conv_sum, inner_x, act_b, rank_b, dt_proj, x_wide, conv_w, docs, modes,
+      gate_pair, normed_t, inv, extra, hidden, in_gate, in_inner)
+
+
+def split_tail(part, count):
+    lane = lax.broadcasted_iota(jnp.int32, part.shape, 1)
+    high = part.astype(jnp.bfloat16).astype(jnp.float32)
+    rest = pltpu.roll(part - high, count, axis=1)
+    return jnp.where(lane < count, high, jnp.where(lane < 2 * count, rest, 0.0)).astype(jnp.bfloat16)
+
+
+def join_tail(block, count):
+    return block + pltpu.roll(block, block.shape[1] - count, axis=1)
+
+
+def front_kernel(coeffs_wide, hidden, gain, conv_w, conv_b, docs, modes, x_wide, out_grad, view, out_proj,
+                 w_inner, w_gate, normed, inverse, conv_sum, inner_x, act_b, gate_z, gated_grad, rank_out, coeff_out,
+                 acc, view_buf, wide, stage, w_out, proj_buf, proj_recv, proj_fin,
+                 view_sems, stage_sems, out_sems, red_send, red_recv, all_send, all_recv):
+    tokens, width = hidden.shape
+    channels = conv_w.shape[1]
+    groups = channels // LANES
+    low = jnp.bfloat16
+    z = lax.axis_index("tensor")
+    share = tokens // 4
+    deep = stage.shape[2] // 2
+    turns = width // deep
+    block = 128
+
+    def z_at(off):
+        return {"tensor": (z + off) % 4}
+
+    barrier = pltpu.get_barrier_semaphore()
+    for off in (1, 2, 3):
+        pl.semaphore_signal(barrier, inc=1, device_id=z_at(off), device_id_type=MESH)
+
+    def view_copy(i, m):
+        tall = deep * 2 * groups
+        return pltpu.make_async_copy(view.at[m, pl.ds(pl.multiple_of(i * tall, tall), tall)], view_buf.at[i % 2, m],
+                                     view_sems.at[i % 2, m])
+
+    def stage_copy(i, half, m):
+        target = w_inner if half == 0 else w_gate
+        return pltpu.make_async_copy(stage.at[i % 2, half, pl.ds(m * deep, deep)],
+                                     target.at[m, pl.ds(pl.multiple_of(i * deep, deep), deep)], stage_sems.at[i % 2, half, m])
+
+    def out_copy(m):
+        return pltpu.make_async_copy(out_proj.at[m], w_out.at[m], out_sems.at[m])
+
+    for m in range(2):
+        view_copy(0, m).start()
+    for m in range(2):
+        view_copy(1, m).start()
+        out_copy(m).start()
+
+    def norm_block(i, nothing):
+        at = pl.ds(pl.multiple_of(i * block, block), block)
+        rows = hidden[at, :].astype(jnp.float32)
+        scale = lax.rsqrt(jnp.mean(rows * rows, axis=1, keepdims=True) + EPS)
+        inverse[at, :] = jnp.broadcast_to(scale, (block, LANES))
+        normed[at, :] = (rows * scale * gain[...]).astype(low)
+        return nothing
+
+    lax.fori_loop(0, tokens // block, norm_block, 0)
+    acc[0:8, :] = jnp.zeros((8, channels), jnp.float32)
+
+    def unpack(i):
+        for m in range(2):
+            wide[m] = view_buf[i % 2, m].astype(jnp.float32)
+            for half in range(2):
+                stage[i % 2, half, m * deep:(m + 1) * deep, :] = jnp.concatenate(
+                    [wide[m, pl.ds(g * 2 + half, deep, stride=2 * groups), :] for g in range(groups)], axis=1).astype(low)
+
+    def multiply(i, first):
+        columns = normed[:, pl.ds(pl.multiple_of(i * deep, deep), deep)]
+        left = jnp.concatenate([columns * widened(modes[0], deep), columns * widened(modes[1], deep)], axis=1)
+        for half in range(2):
+            product = dot_f32(left, stage[i % 2, half])
+            if half == 0:
+                acc[8:8 + tokens, :] = product if first else acc[8:8 + tokens, :] + product
+            else:
+                gate_z[...] = product if first else gate_z[...] + product
+
+    def turn(i):
+        for m in range(2):
+            view_copy(i, m).wait()
+        unpack(i)
+        for m in range(2):
+            for half in range(2):
+                stage_copy(i, half, m).start()
+
+    turn(0)
+    multiply(0, True)
+    for m in range(2):
+        view_copy(2, m).start()
+    turn(1)
+    for m in range(2):
+        view_copy(3, m).start()
+
+    def looped(i, nothing):
+        for m in range(2):
+            for half in range(2):
+                stage_copy(i, half, m).wait()
+        multiply(i + 1, False)
+        turn(i + 2)
+
+        @pl.when(i + 4 < turns)
+        def _():
+            for m in range(2):
+                view_copy(i + 4, m).start()
+        return nothing
+
+    lax.fori_loop(0, turns - 2, looped, 0)
+    multiply(turns - 1, False)
+    for i in (turns - 2, turns - 1):
+        for m in range(2):
+            for half in range(2):
+                stage_copy(i, half, m).wait()
+
+    taps = conv_w.shape[0]
+
+    def conv_block(i, nothing):
+        base = pl.multiple_of(i * block, block)
+        at = pl.ds(base, block)
+        rows = acc[pl.ds(base, block + 8), :]
+        doc = docs[at, :]
+        total = conv_b[...] + conv_w[taps - 1:taps, :] * rows[8:8 + block, :]
+        for offset in range(1, taps):
+            total = total + conv_w[taps - 1 - offset:taps - offset, :] * rows[8 - offset:8 - offset + block, :] * doc[:, offset:offset + 1]
+        conv_sum[at, :] = total
+        inner_x[at, :] = rows[8:8 + block, :]
+        active = (total * jax.nn.sigmoid(total)).astype(low)
+        act_b[at, :] = active
+        part = dot_f32(active * widened(modes[0, at, :], channels), x_wide[0], NT)
+        part = part + dot_f32(active * widened(modes[1, at, :], channels), x_wide[1], NT)
+        proj_buf[at, 0:LANES] = part[:, :LANES].astype(low)
+        proj_buf[at, LANES:2 * LANES] = split_tail(part[:, LANES:], coeffs_wide)
+        return nothing
+
+    lax.fori_loop(0, tokens // block, conv_block, 0)
+
+    def red_copy(off):
+        return pltpu.make_async_remote_copy(
+            src_ref=proj_buf.at[pl.ds(pl.multiple_of(((z + off) % 4) * share, share), share)], dst_ref=proj_recv.at[off - 1],
+            send_sem=red_send.at[off - 1], recv_sem=red_recv.at[off - 1], device_id=z_at(off), device_id_type=MESH)
+
+    mine = pl.ds(pl.multiple_of(z * share, share), share)
+
+    def all_copy(off):
+        return pltpu.make_async_remote_copy(
+            src_ref=proj_fin.at[mine], dst_ref=proj_fin.at[mine], send_sem=all_send.at[off - 1],
+            recv_sem=all_recv.at[off - 1], device_id=z_at(off), device_id_type=MESH)
+
+    pl.semaphore_wait(barrier, 3)
+    for off in (1, 2, 3):
+        red_copy(off).start()
+    third = tokens // 3
+
+    def grad_block(i):
+        at = pl.ds(i * third, third)
+        zero = dot_f32(out_grad[at, :], w_out[0], NT)
+        one = dot_f32(out_grad[at, :], w_out[1], NT)
+        gated_grad[at, :] = jnp.where(docs[at, 0:1] > 0.5, zero, one)
+
+    for m in range(2):
+        out_copy(m).wait()
+    grad_block(0)
+    for off in (1, 2, 3):
+        red_copy(off).wait_recv()
+    total = proj_buf[mine, :].astype(jnp.float32)
+    for k in range(3):
+        total = total + proj_recv[k].astype(jnp.float32)
+    proj_fin[mine, 0:LANES] = total[:, :LANES].astype(low)
+    proj_fin[mine, LANES:2 * LANES] = split_tail(join_tail(total[:, LANES:], coeffs_wide), coeffs_wide)
+    for off in (1, 2, 3):
+        all_copy(off).start()
+    grad_block(1)
+    grad_block(2)
+    for off in (1, 2, 3):
+        all_copy(off).wait_recv()
+    rank_out[...] = proj_fin[:, 0:LANES]
+    coeff_out[...] = join_tail(proj_fin[:, LANES:2 * LANES].astype(jnp.float32), coeffs_wide)
+    for off in (1, 2, 3):
+        red_copy(off).wait_send()
+        all_copy(off).wait_send()
+
+
+def front(hidden, gain, conv_w, conv_b, docs, modes, x_wide, out_grad, in_proj, out_proj, coeffs_wide):
+    tokens, width = hidden.shape
+    channels = conv_w.shape[1]
+    groups = channels // LANES
+    low, f32 = jnp.bfloat16, jnp.float32
+    view = in_proj.reshape(2, width, 2, groups, LANES).transpose(0, 1, 3, 2, 4).reshape(2, width * 2 * groups, LANES)
+    deep = 256
+    vmem, anywhere = pl.BlockSpec(memory_space=pltpu.VMEM), pl.BlockSpec(memory_space=pl.ANY)
+    shape = jax.ShapeDtypeStruct
+    return pl.pallas_call(
+        functools.partial(front_kernel, coeffs_wide),
+        in_specs=[vmem] * 8 + [anywhere] * 2,
+        out_specs=[anywhere] * 2 + [vmem] * 9,
+        out_shape=[
+            shape((2, width, channels), low), shape((2, width, channels), low), shape((tokens, width), low),
+            shape((tokens, LANES), f32), shape((tokens, channels), f32), shape((tokens, channels), f32),
+            shape((tokens, channels), low), shape((tokens, channels), f32), shape((tokens, channels), f32),
+            shape((tokens, LANES), low), shape((tokens, LANES), f32),
+        ],
+        scratch_shapes=[
+            pltpu.VMEM((tokens + 8, channels), f32),
+            pltpu.VMEM((2, 2, deep * 2 * groups, LANES), low),
+            pltpu.VMEM((2, deep * 2 * groups, LANES), f32),
+            pltpu.VMEM((2, 2, 2 * deep, channels), low),
+            pltpu.VMEM((2, channels, width), low),
+            pltpu.VMEM((tokens, 2 * LANES), low),
+            pltpu.VMEM((3, tokens // 4, 2 * LANES), low),
+            pltpu.VMEM((tokens, 2 * LANES), low),
+            DMA((2, 2)), DMA((2, 2, 2)), DMA((2,)), DMA((3,)), DMA((3,)), DMA((3,)), DMA((3,)),
+        ],
+        cost_estimate=pl.CostEstimate(flops=20_000_000_000, bytes_accessed=80_000_000, transcendentals=1_000_000),
+        compiler_params=pltpu.CompilerParams(collective_id=4, has_side_effects=True, vmem_limit_bytes=60 * 1024 * 1024),
+        name="front",
+    )(hidden, gain, conv_w, conv_b, docs, modes, x_wide, out_grad, view, out_proj)
+
+
+def finish_kernel(hidden, out_grad, inverse, gain, summed_out, normed_sum, output, input_grad):
+    rows = hidden[...].astype(jnp.float32)
+    output[...] = (rows + summed_out[...].astype(jnp.float32)).astype(output.dtype)
+    scale = inverse[:, 0:1]
+    scaled = normed_sum[...].astype(jnp.float32) * gain[...]
+    mean = jnp.mean(scaled * rows, axis=1, keepdims=True)
+    input_grad[...] = (out_grad[...].astype(jnp.float32) + scale * scaled - rows * (scale * scale * scale) * mean).astype(input_grad.dtype)
+
+
+def finish(hidden, out_grad, inverse, gain, summed_out, normed_sum):
+    tokens, width = hidden.shape
+    rows = 128
+    wide = pl.BlockSpec((rows, width), lambda i: (i, 0))
+    return pl.pallas_call(
+        finish_kernel,
+        grid=(tokens // rows,),
+        in_specs=[wide, wide, pl.BlockSpec((rows, LANES), lambda i: (i, 0)), pl.BlockSpec((1, width), lambda i: (0, 0)), wide, wide],
+        out_specs=[wide, wide],
+        out_shape=[jax.ShapeDtypeStruct((tokens, width), jnp.bfloat16)] * 2,
+        cost_estimate=pl.CostEstimate(flops=16 * tokens * width, bytes_accessed=12 * tokens * width, transcendentals=0),
+        name="finish_rows",
+    )(hidden, out_grad, inverse, gain, summed_out, normed_sum)
+
+
+def scan_backward_kernel(states, groups, rows, unroll, count, joined,
+                         bc_ref, pre_ref, act_ref, mixed_ref, keep_ref, alog_ref, skip_ref, h_ref, start_ref, *rest):
+    if joined:
+        prod_ref, part_ref, rest = rest[0], rest[1], rest[2:]
+    pgrad_ref, apart_ref, bcg_ref, sum_ref, skipsum_ref = rest[:5]
+    rest = rest[5:]
+    if joined:
+        shared_ref, res_ref, rest = rest[0], rest[1], rest[2:]
+    carry_ref, rate_scr, decay_scr, sk_scr, u_scr, dy_scr, w_scr, s_scr, p_scr, q_scr = rest[:10]
+    rest = rest[10:]
     chunk = pl.program_id(0)
-    count = pl.num_programs(0)
+    if joined:
+        line = LineSum(part_ref, res_ref, rest[0], rest[1], rest[2:7])
+        swapped = Exchange(prod_ref, shared_ref, *rest[7:10], rest[10:19])
+
+        @pl.when(chunk == 0)
+        def _():
+            line.load().start()
+            greet()
+            swapped.event(0)
+            line.begin()
+
+        for number, at in enumerate((2, 4, 7, 9, 11), start=1):
+            @pl.when(chunk == min(at, count - 1))
+            def _():
+                swapped.event(number)
+
+        for at in range(1, count):
+            @pl.when(chunk == at)
+            def _():
+                for turn in range(line.turns * (at - 1) // (count - 1), line.turns * at // (count - 1)):
+                    line.turn(turn)
 
     @pl.when(chunk == 0)
     def _():
         decay = -jnp.exp(alog_ref[...])
         decay_scr[...] = decay
         rate_scr[...] = decay * LOG2E
-        carry_scr[...] = jnp.zeros_like(carry_scr)
-        sum_scr[...] = jnp.zeros_like(sum_scr)
+        carry_ref[...] = jnp.zeros_like(carry_ref)
+        sum_ref[...] = jnp.zeros_like(sum_ref)
         skipsum_ref[...] = jnp.zeros_like(skipsum_ref)
 
     step = softplus(pre_ref[...])
@@ -154,7 +1016,7 @@
             fg = jnp.exp2(sk * rate_scr[n]) * g
             lg = fg * before(n)
             s = s + lg * decay_scr[n]
-            sum_scr[n] += lg * sk
+            sum_ref[n] += lg * sk
             new.append(fg)
         w_scr[pl.ds(at, groups), :] = w
         s_scr[pl.ds(at, groups), :] = s
@@ -169,10 +1031,10 @@
         t = rows - 1 - i
         return one(t, carried, lambda n: h_ref[t - 1, n])
 
-    last = lax.fori_loop(0, rows - 1, looped, tuple(carry_scr[n] for n in range(states)), unroll=unroll)
+    last = lax.fori_loop(0, rows - 1, looped, tuple(carry_ref[n] for n in range(states)), unroll=unroll)
     last = one(0, last, lambda n: start_ref[0, n])
     for n in range(states):
-        carry_scr[n] = last[n]
+        carry_ref[n] = last[n]
 
     ones = jnp.ones((16, LANES), jnp.bfloat16)
 
@@ -182,8 +1044,9 @@
         return nothing
 
     lax.fori_loop(0, rows, reduce_one, 0, unroll=4)
-    pick = (lax.broadcasted_iota(jnp.int32, (2 * states * groups, 2 * states), 0) // groups
-            == lax.broadcasted_iota(jnp.int32, (2 * states * groups, 2 * states), 1)).astype(jnp.float32).astype(jnp.bfloat16)
+    shape = (2 * states * groups, LANES)
+    pick = (lax.broadcasted_iota(jnp.int32, shape, 0) // groups == lax.broadcasted_iota(jnp.int32, shape, 1))
+    pick = pick.astype(jnp.float32).astype(jnp.bfloat16)
     q = q_scr[...]
     high = q.astype(jnp.bfloat16)
     low = (q - high.astype(jnp.float32)).astype(jnp.bfloat16)
@@ -194,23 +1057,36 @@
     pgrad_ref[...] = ((act * w + s) * jax.nn.sigmoid(pre_ref[...])).astype(pgrad_ref.dtype)
     apart_ref[...] = mixed * skip_ref[...] + step * w
 
-    @pl.when(chunk == count - 1)
-    def _():
-        ratesum_ref[...] = sum_scr[...] * decay_scr[...]
-
-
-def scan_backward(bc, pre, act, mixed, keep, a_log3, skip, h, starts, rows=64, unroll=3):
+    if joined:
+        @pl.when(chunk == count - 1)
+        def _():
+            swapped.event(6)
+            swapped.event(7)
+            line.finish()
+
+
+def scan_backward(bc, pre, act, mixed, keep, a_log3, skip, h, starts, product=None, z_part=None, rows=64, unroll=3, pieces=6):
     tokens, channels = pre.shape
     groups = channels // LANES
     states = a_log3.shape[0]
     count = tokens // rows
+    joined = product is not None
     wide = pl.BlockSpec((rows, channels), lambda i: (count - 1 - i, 0))
     whole3 = pl.BlockSpec((states, groups, LANES), lambda i: (0, 0, 0))
     row = pl.BlockSpec((1, channels), lambda i: (0, 0))
+    anywhere = pl.BlockSpec(memory_space=pl.ANY)
     small = lambda: pltpu.VMEM((states, groups, LANES), jnp.float32)
     long = lambda: pltpu.VMEM((rows * groups, LANES), jnp.float32)
-    return pl.pallas_call(
-        functools.partial(scan_backward_kernel, states, groups, rows, unroll),
+    extra, extra_shapes, extra_scratch = [], [], []
+    if joined:
+        side, depth = product.shape[1] // 4, product.shape[2]
+        part = z_part.reshape(2, pieces, tokens // 2 // pieces, z_part.shape[1])
+        extra = [product, part]
+        extra_shapes = [jax.ShapeDtypeStruct((2, 2, 4, side, depth), jnp.bfloat16), jax.ShapeDtypeStruct(part.shape, jnp.bfloat16)]
+        extra_scratch = LineSum.scratch(*part.shape[1:]) + Exchange.scratch(side, depth)
+    settings = dict(collective_id=2, has_side_effects=True) if joined else {}
+    outs = pl.pallas_call(
+        functools.partial(scan_backward_kernel, states, groups, rows, unroll, count, joined),
         grid=(count,),
         in_specs=[
             pl.BlockSpec((rows, 2 * states), lambda i: (count - 1 - i, 0), memory_space=pltpu.SMEM),
@@ -219,25 +1095,69 @@
             whole3, row,
             pl.BlockSpec((rows, states, groups, LANES), lambda i: (count - 1 - i, 0, 0, 0)),
             pl.BlockSpec((1, states, groups, LANES), lambda i: (count - 1 - i, 0, 0, 0)),
-        ],
-        out_specs=[
-            wide, wide,
-            pl.BlockSpec((rows, 2 * states), lambda i: (count - 1 - i, 0)),
-            whole3, row,
-        ],
+        ] + [anywhere] * len(extra),
+        out_specs=[wide, wide, pl.BlockSpec((rows, LANES), lambda i: (count - 1 - i, 0)), whole3, row]
+        + [anywhere] * len(extra),
         out_shape=[
             jax.ShapeDtypeStruct((tokens, channels), jnp.bfloat16),
             jax.ShapeDtypeStruct((tokens, channels), jnp.float32),
-            jax.ShapeDtypeStruct((tokens, 2 * states), jnp.float32),
+            jax.ShapeDtypeStruct((tokens, LANES), jnp.float32),
             jax.ShapeDtypeStruct((states, groups, LANES), jnp.float32),
             jax.ShapeDtypeStruct((1, channels), jnp.float32),
-        ],
-        scratch_shapes=[small(), small(), small(), small(), long(), long(), long(), long(), long(),
+        ] + extra_shapes,
+        scratch_shapes=[small(), small(), small(), long(), long(), long(), long(), long(),
                         pltpu.VMEM((rows, 2 * states * groups, LANES), jnp.bfloat16),
-                        pltpu.VMEM((rows, 2 * states * groups), jnp.float32)],
+                        pltpu.VMEM((rows, 2 * states * groups), jnp.float32)] + extra_scratch,
+        cost_estimate=pl.CostEstimate(flops=60 * tokens * channels * states,
+                                      bytes_accessed=4 * tokens * channels * states,
+                                      transcendentals=tokens * channels * states),
+        compiler_params=pltpu.CompilerParams(vmem_limit_bytes=52 * 1024 * 1024, **settings),
+        name="scan_backward",
+    )(bc, pre, act, mixed, keep, a_log3, skip, h, starts, *extra)
+    if joined:
+        outs = list(outs[:6]) + [outs[6].reshape(tokens, z_part.shape[1])]
+    return outs
+
+
+def writer_kernel(place, side, depth, where_ref, pieces_ref, *rest):
+    out_ref, wide_scr, sems = rest[-3:]
+    x, y, core = where_ref[0], where_ref[1], where_ref[2]
+    copies = []
+    for mode in range(2):
+        for owner in range(2):
+            c = core if owner == 0 else 1 - core
+            for k in range(4):
+                qx = x if k in (0, 1) else 1 - x
+                qy = y if k in (0, 2) else 1 - y
+                row = (qx * 2 + qy if mode == 0 else qy * 2 + qx) * side
+                at = (mode * 2 + owner) * 4 + k
+                wide_scr[at] = pieces_ref[mode, owner, k].astype(jnp.float32)
+                if place == "columns":
+                    target = out_ref.at[mode, pl.ds(pl.multiple_of(row, side), side),
+                                        pl.ds(pl.multiple_of(c * depth, depth), depth)]
+                else:
+                    target = out_ref.at[mode, pl.ds(pl.multiple_of(c * 4 * side + row, side), side), place, :]
+                copies.append(pltpu.make_async_copy(wide_scr.at[at], target, sems.at[at]))
+                copies[-1].start()
+    for copy in copies:
+        copy.wait()
+
+
+def write_out(place, shape, where, pieces, filled):
+    side, depth = pieces.shape[3:]
+    held = [] if filled is None else [filled]
+    return pl.pallas_call(
+        functools.partial(writer_kernel, place, side, depth),
+        in_specs=[pl.BlockSpec(memory_space=pltpu.SMEM), pl.BlockSpec(memory_space=pltpu.VMEM)]
+        + [pl.BlockSpec(memory_space=pl.ANY)] * len(held),
+        out_specs=pl.BlockSpec(memory_space=pl.ANY),
+        out_shape=jax.ShapeDtypeStruct(shape, jnp.float32),
+        input_output_aliases={2: 0} if held else {},
+        scratch_shapes=[pltpu.VMEM((16, side, depth), jnp.float32), pltpu.SemaphoreType.DMA((16,))],
+        cost_estimate=pl.CostEstimate(flops=16 * side * depth, bytes_accessed=16 * side * depth * 6, transcendentals=0),
         compiler_params=pltpu.CompilerParams(vmem_limit_bytes=48 * 1024 * 1024),
-        name="scan_backward",
-    )(bc, pre, act, mixed, keep, a_log3, skip, h, starts)
+        name="write_grads",
+    )(where, pieces, *held)
 
 
 def lagged(values, offset):
@@ -291,34 +1211,94 @@
     return (rows.astype(jnp.bfloat16), gain_terms)
 
 
-def shards(hidden_in, segment_ids, modality, norm_gain, in_proj, conv_weight, conv_bias, x_proj, dt_proj, dt_bias,
+def swap(values, distance):
+    return lax.ppermute(values, "dp", [(i, i ^ distance) for i in range(8)])
+
+
+CORE = 1
+
+
+def tie(values, *others):
+    return lax.optimization_barrier((values,) + others)[0]
+
+
+def z_sum(values, size, dtype=jnp.bfloat16):
+    distance = 1
+    while distance < size:
+        low = values.astype(dtype)
+        got = lax.ppermute(low, "tensor", [(i, i ^ distance) for i in range(size)])
+        values = low.astype(jnp.float32) + got.astype(jnp.float32)
+        distance *= 2
+    return values
+
+
+def shards(names, hidden_in, segment_ids, modality, norm_gain, in_proj, conv_weight, conv_bias, x_proj, dt_proj, dt_bias,
            a_log, skip_gain, out_proj, out_grad):
     tokens, model_width = hidden_in.shape
     conv_taps, channels = conv_weight.shape
     rank_dim = dt_proj.shape[1]
     state_dim = a_log.shape[0]
     groups = channels // LANES
+    ways = names["tensor"]
+    by_hand = names["dp"] == 8 and names["tensor"] == 4
     low = jnp.bfloat16
+    rank = lax.axis_index("dp")
+    core, x_at, y_at = rank % 2, (rank // 2) % 2, rank // 4
+    where = jnp.stack([x_at, y_at, core]).astype(jnp.int32)
+    half_width = model_width // 2
     first_mode = (modality == 0)[:, None]
-    hidden = hidden_in.astype(jnp.float32)
-    inverse = lax.rsqrt(jnp.mean(hidden * hidden, axis=1, keepdims=True) + EPS)
-    normed_b = (hidden * inverse * norm_gain).astype(low)
-    in_inner = in_proj[:, :, 0, :]
-    in_gate = in_proj[:, :, 1, :]
-    inner_x = pick_dot(normed_b, in_inner, first_mode)
-    gate_z = pick_dot(normed_b, in_gate, first_mode)
+    nothing = jnp.zeros((), low)
+    dims = (((0,), (0,)), ((), ()))
+
+    def col_half(values, which):
+        return lax.dynamic_slice_in_dim(values, which * half_width, half_width, 1)
+
+    def pair_half(values):
+        return jnp.concatenate([col_half(values, core), swap(col_half(values, 1 - core), CORE)], axis=0)
+
+    def pair_all(values):
+        return jnp.concatenate([values, swap(values, CORE)], axis=0)
+
+    def masked_products(left, right, modes, mask_left):
+        products = []
+        for chosen in (modes, jnp.logical_not(modes)):
+            one = jnp.where(chosen, left, nothing) if mask_left else left
+            two = right if mask_left else jnp.where(chosen, right, nothing)
+            products.append(lax.dot_general(one, two, dims, preferred_element_type=jnp.float32).astype(low))
+        return jnp.stack(products)
+
     same_doc = [jnp.ones((tokens, 1), jnp.float32)]
     for offset in range(1, conv_taps):
         earlier_seg = jnp.pad(segment_ids, (offset, 0), constant_values=-1)[:tokens]
         same_doc.append((earlier_seg == segment_ids).astype(jnp.float32)[:, None])
-    conv_sum = conv_bias + conv_weight[conv_taps - 1] * inner_x
-    for offset in range(1, conv_taps):
-        conv_sum = conv_sum + conv_weight[conv_taps - 1 - offset] * lagged(inner_x, offset) * same_doc[offset]
-    activated_b = jax.nn.silu(conv_sum).astype(low)
-    projected = lax.psum(pick_dot(activated_b, x_proj, first_mode), "tensor")
-    rank_b = projected[:, :rank_dim].astype(low)
-    coeffs = projected[:, rank_dim:]
-    gated_grad = pick_back(out_grad, out_proj, first_mode)
+    if by_hand:
+        modes_own = jnp.broadcast_to(jnp.stack([first_mode, jnp.logical_not(first_mode)]), (2, tokens, LANES)).astype(low)
+        x_wide = jnp.pad(jnp.swapaxes(x_proj, 1, 2), ((0, 0), (0, 96), (0, 0)))
+        facts = jnp.concatenate([first_mode.astype(jnp.float32)] + same_doc[1:], axis=1)
+        (in_inner, in_gate, normed_b, inverse, conv_sum, inner_x, activated_b, gate_z, gated_grad, rank_b, coeffs) = front(
+            hidden_in, norm_gain[None], conv_weight, conv_bias[None], facts, modes_own, x_wide, out_grad, in_proj, out_proj,
+            2 * state_dim)
+        coeffs = coeffs[:, :2 * state_dim]
+        sib_mode = swap(first_mode.astype(jnp.float32), CORE) > 0.5
+        pair_mode = jnp.concatenate([first_mode, sib_mode], axis=0)
+        normed_pair = pair_half(normed_b)
+        cotan_pair = pair_half(tie(out_grad, rank_b))
+    else:
+        hidden = hidden_in.astype(jnp.float32)
+        inverse = lax.rsqrt(jnp.mean(hidden * hidden, axis=1, keepdims=True) + EPS)
+        normed_b = (hidden * inverse * norm_gain).astype(low)
+        in_inner = in_proj[:, :, 0, :]
+        in_gate = in_proj[:, :, 1, :]
+        inner_x = pick_dot(normed_b, in_inner, first_mode)
+        conv_sum = conv_bias + conv_weight[conv_taps - 1] * inner_x
+        for offset in range(1, conv_taps):
+            conv_sum = conv_sum + conv_weight[conv_taps - 1 - offset] * lagged(inner_x, offset) * same_doc[offset]
+        activated_b = jax.nn.silu(conv_sum).astype(low)
+        projected = z_sum(pick_dot(activated_b, x_proj, first_mode), ways)
+        rank_b = projected[:, :rank_dim].astype(low)
+        coeffs = projected[:, rank_dim:]
+        gate_z = pick_dot(normed_b, in_gate, first_mode)
+        gated_grad = pick_back(out_grad, out_proj, first_mode)
     step_pre = pick_dot(rank_b, dt_proj, first_mode) + jnp.where(first_mode, dt_bias[0], dt_bias[1])
     keep = same_doc[1]
     a_log3 = a_log.reshape(state_dim, groups, LANES)
@@ -326,44 +1306,77 @@
     gated_b, gate_grad_b, mixed_grad, states, starts = scan_forward(
         coeffs, step_pre, activated_b, gate_z, gated_grad, keep, a_log3, skip_row)
     partial_out = pick_dot(gated_b, out_proj, first_mode).astype(low)
-    summed_out = lax.psum(partial_out, "tensor")
-    output = (hidden + summed_out.astype(jnp.float32)).astype(low)
-    cotan = out_grad.astype(jnp.float32)
-    out_proj_grad = weight_grads(gated_b, out_grad, first_mode).astype(low)
-    out_proj_grad = lax.psum(out_proj_grad, "dp").astype(jnp.float32)
-    gate_proj_grad = lax.psum(weight_grads(normed_b, gate_grad_b, first_mode).astype(low), "dp")
-    pre_grad_b, act_part, coeff_grad, a_log_grad, skip_grad = scan_backward(
-        coeffs, step_pre, activated_b, mixed_grad, keep, a_log3, skip_row, states, starts)
-    a_log_grad = a_log_grad.reshape(state_dim, channels)
-    pre_grad = pre_grad_b.astype(jnp.float32)
-    dt_bias_grad = jnp.stack([
-        jnp.sum(jnp.where(first_mode, pre_grad, 0.0), axis=0),
-        jnp.sum(jnp.where(first_mode, 0.0, pre_grad), axis=0)])
-    rank_part = pick_back(pre_grad_b, dt_proj, first_mode)
-    proj_grad = lax.psum(jnp.concatenate([rank_part, coeff_grad], axis=1), "tensor")
-    proj_grad_b = proj_grad.astype(low)
-    act_grad = act_part + pick_back(proj_grad_b, x_proj, first_mode)
-    sig_conv = jax.nn.sigmoid(conv_sum)
-    conv_grad = act_grad * sig_conv * (1.0 + conv_sum * (1.0 - sig_conv))
-    conv_bias_grad = jnp.sum(conv_grad, axis=0)
-    weight_rows = []
-    x_grad = jnp.zeros_like(inner_x)
-    for tap_index in range(conv_taps):
-        offset = conv_taps - 1 - tap_index
-        masked = conv_grad * same_doc[offset]
-        weight_rows.append(jnp.sum(masked * lagged(inner_x, offset), axis=0))
-        x_grad = x_grad + conv_weight[tap_index] * leading(masked, offset)
-    x_grad_b = x_grad.astype(low)
-    normed_part = pick_back(x_grad_b, in_inner, first_mode) + pick_back(gate_grad_b, in_gate, first_mode)
-    normed_grad = lax.psum(normed_part.astype(low), "tensor").astype(jnp.float32)
-    inner_proj_grad = lax.psum(weight_grads(normed_b, x_grad_b, first_mode).astype(low), "dp")
-    in_proj_grad = jnp.stack([inner_proj_grad, gate_proj_grad], axis=2).astype(jnp.float32)
-    input_grad, norm_gain_grad = finish_rows(normed_grad, hidden, inverse, cotan, norm_gain)
-    x_proj_grad = lax.psum(weight_grads(activated_b, proj_grad_b, first_mode).astype(low), "dp").astype(jnp.float32)
-    dt_proj_grad = lax.psum(weight_grads(rank_b, pre_grad_b, first_mode).astype(low), "dp").astype(jnp.float32)
-    rows = jnp.concatenate([jnp.stack(weight_rows), conv_bias_grad[None], dt_bias_grad, a_log_grad, skip_grad], axis=0)
-    rows = lax.psum(rows, "dp")
-    norm_gain_grad = lax.psum(norm_gain_grad, "dp")
+    if by_hand:
+        gated_pair = pair_all(gated_b)
+        ggrad_pair = pair_all(gate_grad_b)
+        out_product = masked_products(gated_pair, cotan_pair, pair_mode, True)
+        back = scan_backward(coeffs, step_pre, activated_b, mixed_grad, keep, a_log3, skip_row, states, starts,
+                             out_product, partial_out)
+        summed_out, out_shared = back[6], back[5]
+    else:
+        back = scan_backward(coeffs, step_pre, activated_b, mixed_grad, keep, a_log3, skip_row, states, starts)
+        summed_out = lax.psum(partial_out, "tensor")
+        out_proj_grad = lax.psum(weight_grads(gated_b, out_grad, first_mode).astype(low), "dp").astype(jnp.float32)
+        gate_proj_grad = lax.psum(weight_grads(normed_b, gate_grad_b, first_mode).astype(low), "dp")
+    pre_grad_b, act_part, coeff_grad, sums, skips = back[:5]
+    a_log_grad = sums.reshape(state_dim, channels) * -jnp.exp(a_log)
+    mode_rows = x_proj.shape[2] + rank_dim
+    if by_hand:
+        later = jnp.stack([same_doc[0]] + [leading(same_doc[k], k) for k in range(1, conv_taps)], axis=1)[:, :, 0]
+        modes = jnp.broadcast_to(jnp.stack([pair_mode, jnp.logical_not(pair_mode)]), (2, 2 * tokens, LANES)).astype(low)
+        row_facts = jnp.concatenate([inverse[:, :1], first_mode.astype(jnp.float32)], axis=1)
+        rows, normed_low, gate_own, inner_product, _ = middle(
+            pre_grad_b, act_part, coeff_grad, conv_sum, inner_x, activated_b, rank_b, dt_proj, x_wide, conv_weight, later, modes,
+            ggrad_pair, jnp.swapaxes(normed_pair, 0, 1), row_facts, jnp.concatenate([a_log_grad, skips], axis=0), hidden_in,
+            in_gate, in_inner)
+    else:
+        pre_grad = pre_grad_b.astype(jnp.float32)
+        dt_bias_grad = jnp.stack([
+            jnp.sum(jnp.where(first_mode, pre_grad, 0.0), axis=0),
+            jnp.sum(jnp.where(first_mode, 0.0, pre_grad), axis=0)])
+        rank_part = pick_back(pre_grad_b, dt_proj, first_mode)
+        proj_grad_b = z_sum(jnp.concatenate([rank_part, coeff_grad[:, :2 * state_dim]], axis=1), ways).astype(low)
+        act_grad = act_part + pick_back(proj_grad_b, x_proj, first_mode)
+        sig_conv = jax.nn.sigmoid(conv_sum)
+        conv_grad = act_grad * sig_conv * (1.0 + conv_sum * (1.0 - sig_conv))
+        conv_bias_grad = jnp.sum(conv_grad, axis=0)
+        weight_rows = []
+        x_grad = jnp.zeros_like(inner_x)
+        for tap_index in range(conv_taps):
+            offset = conv_taps - 1 - tap_index
+            masked = conv_grad * same_doc[offset]
+            weight_rows.append(jnp.sum(masked * lagged(inner_x, offset), axis=0))
+            x_grad = x_grad + conv_weight[tap_index] * leading(masked, offset)
+        x_grad_b = x_grad.astype(low)
+        normed_part = pick_back(x_grad_b, in_inner, first_mode) + pick_back(gate_grad_b, in_gate, first_mode)
+        gain_part = jnp.sum(normed_part * (hidden * inverse), axis=0).reshape(-1, channels)
+        gain_part = lax.psum(gain_part, "tensor")
+        small_modes = jnp.concatenate([
+            weight_grads(proj_grad_b, activated_b, first_mode), weight_grads(rank_b, pre_grad_b, first_mode)], axis=1)
+        rows = jnp.concatenate([small_modes.reshape(-1, channels), jnp.stack(weight_rows), conv_bias_grad[None], dt_bias_grad,
+                                a_log_grad, skips, gain_part], axis=0).astype(low)
+    summed_rows = lax.psum(rows, "dp")
+    if by_hand:
+        (gate_shared, inner_shared), normed_sum = tail_exchange([gate_own, inner_product], normed_low)
+
+        output, input_grad = finish(hidden_in, out_grad, inverse, norm_gain[None], summed_out, normed_sum)
+        where = tie(where, summed_rows)
+        out_proj_grad = write_out("columns", (2, channels, model_width), where, out_shared, None)
+        in_shape = (2, model_width, 2, channels)
+        in_proj_grad = write_out(1, in_shape, where, gate_shared, None)
+        in_proj_grad = write_out(0, in_shape, where, inner_shared, in_proj_grad)
+    else:
+        inner_proj_grad = lax.psum(weight_grads(normed_b, x_grad_b, first_mode).astype(low), "dp")
+        in_proj_grad = jnp.stack([inner_proj_grad, gate_proj_grad], axis=2).astype(jnp.float32)
+        normed_sum = lax.psum(normed_part.astype(low), "tensor")
+        output = (hidden + summed_out.astype(jnp.float32)).astype(low)
+        cotan = out_grad.astype(jnp.float32)
+        input_grad, _ = finish_rows(normed_sum.astype(jnp.float32), hidden, inverse, cotan, norm_gain)
+    summed_rows = summed_rows.astype(jnp.float32)
+    small_modes, rows = summed_rows[:2 * mode_rows].reshape(2, mode_rows, channels), summed_rows[2 * mode_rows:]
+    x_proj_grad = jnp.swapaxes(small_modes[:, :-rank_dim], 1, 2)
+    dt_proj_grad = small_modes[:, -rank_dim:]
+    norm_gain_grad = rows[conv_taps + 4 + state_dim:].reshape(-1)[:model_width]
     at = conv_taps + 1
     return (output, input_grad, norm_gain_grad, in_proj_grad, rows[:conv_taps], rows[conv_taps], x_proj_grad,
             dt_proj_grad, rows[at:at + 2], rows[at + 2:at + 2 + state_dim], rows[at + 2 + state_dim], out_proj_grad)
@@ -400,4 +1413,5 @@
         P("tensor"),
         P(None, "tensor", None),
     )
-    return jax.shard_map(shards, mesh=mesh, in_specs=in_specs, out_specs=out_specs, check_vma=False)
+    names = dict(mesh.shape)
+    return jax.shard_map(functools.partial(shards, names), mesh=mesh, in_specs=in_specs, out_specs=out_specs, check_vma=False)

time: 1010 us -> 564 us (0.56)
  waiting for transfers between devices: 507 us -> 0.03 us
  Pallas kernels: 103 us -> 454 us
  matrix products: 140 us -> 26.2 us
  other arithmetic: 83.8 us -> 16.9 us
  local copies, waits for them, and re-layouts: 102 us -> 42.1 us
  blocking collectives: 50.7 us -> 0 us
    psum x4 -> x1, waiting for transfers between devices: 507 us -> 0.01 us  [shards(): summed_rows = lax.psum(rows, 'dp')]
    pallas_call x0 -> x7, Pallas kernels: none -> 307 us  [the longest x1 133 us: tail_exchange(): pl.pallas_call(functools.partial(tail_kernel, count), in_specs=[anywhere]...]
    dot_general x20 -> x2, matrix products: 98.5 us -> 11.2 us  [masked_products(): lax.dot_general(one, two, dims, preferred_element_type=jnp.float32)]
    psum x2 -> x0, blocking collectives: 50.7 us -> none  [the longest x1 35.9 us: shards(): lax.psum(jnp.concatenate([rank_part, coeff_grad], axis=1), 'tensor')]
    convert_element_type x8 -> x4, other arithmetic: 50 us -> 0.35 us  [the longest x1 0.29 us: shards(): summed_rows = summed_rows.astype(jnp.float32)]
    unnamed x121 -> x48, local copies, waits for them, and re-layouts: 58.1 us -> 11.2 us
    pallas_call x1, Pallas kernels: 76.7 us -> 121 us  [scan_backward(): pl.pallas_call(functools.partial(scan_backward_kernel, states, groups, ro...]
    slice x3 -> x2, local copies, waits for them, and re-layouts: 34 us -> 2.64 us  [the longest x1 1.56 us: shards(): summed_rows[:2 * mode_rows].reshape(2, mode_rows, channels)]
  transfers between devices with their start and end apart: 4 -> 6, of which waited for: 3 -> 0; matrix products, arithmetic and copies ran while one was open for 13% -> 11% of each run, Pallas kernels for 0% -> 64%
where the time goes in v2:
time: 564 us; the launch traced here: 555 us
  Pallas kernels  454 us (80%)
  local copies, waits for them, and re-layouts  42.1 us (7%)
  matrix products  26.2 us (5%)
  other arithmetic  16.9 us (3%)
  between operations  14.9 us (3%)
    pallas_call x1, Pallas kernels, tail_exchange(): pl.pallas_call(functools.partial(tail_kernel, count), in_specs=[anywhere]...  133 us
    pallas_call x1, Pallas kernels, scan_backward(): pl.pallas_call(functools.partial(scan_backward_kernel, states, groups, ro...  121 us
    pallas_call x1, Pallas kernels, middle(): pl.pallas_call(middle_kernel, in_specs=[vmem] * 16 + [anywhere] * 3, out_...  69.6 us
    pallas_call x1, Pallas kernels, front(): pl.pallas_call(functools.partial(front_kernel, coeffs_wide), in_specs=[vm...  66.8 us
    pallas_call x3, Pallas kernels, write_out(): pl.pallas_call(functools.partial(writer_kernel, place, side, depth), in_s...  28.4 us
    pallas_call x1, Pallas kernels, scan_forward(): pl.pallas_call(functools.partial(scan_forward_kernel, states, groups, row...  26.1 us
  transfers between devices with their start and end apart: 6, of which 0 were waited for; matrix products, arithmetic and copies ran while one was open for 11% of the time, Pallas kernels for 64%

profile of v2, /device:TPU:0, one launch (start us, length us, event | category | flops | bytes accessed | tf_op | source)
XLA Modules:
  0.0 555.5 jit_solution(12436699931304700423)
XLA Ops:
  11.9 2.2 pad.31.x_wide
  16.3 66.8 %front.1 = (bf16[2,2048,1024]{2,1,0:T(8,128)(2,1)}, bf16[2,2048,1024]{2,1,0:T(8,128)(2,1)}, bf16[768,2048]{1,0:T(8,128)(2,1)}, f32[768,128]{1,0:T(8,128)}, f32[7...) custom-call(bf16[768,2048]{1,0:T(8,128)(2,1)} %hidden.5, ...), custom_call_target="tpu_custom_call" | custom-call | flops 20000000000 | bytes 80000000 | tf_op jit(solution)/shard_map/front/pallas_call | solution.py:902
  83.1 1.5 fusion.21
  84.7 2.4 select_add_fusion.pre_ref
  87.1 26.1 %scan_forward.1 = (bf16[768,1024]{1,0:T(8,128)(2,1)S(1)}, bf16[768,1024]{1,0:T(8,128)(2,1)}, f32[768,1024]{1,0:T(8,128)}, f32[768,16,8,128]{3,2,1,0:T(8,128)}, f32[12,16,8,128]{3,2,1,0:T(8,128)S(1)}) custom-call(f32[768,32]{1,0:T(8,128)S(1)} %bitcast.78, f32[768,1024]{1,0:T(8,128)} %select_add_fusion.pre_ref, ...), custom_call_target="tpu_custom_call" | custom-call | tf_op jit(solution)/shard_map/scan_forward/pallas_call | solution.py:83
  114.0 3.8 constant_dynamic-slice_fusion.3
  118.3 4.6 copy.88
  123.0 3.9 constant_dynamic-slice_fusion.1
  127.4 6.1 %fusion = bf16[768,2048]{1,0:T(8,128)(2,1)S(1)} fusion(bf16[768,1024]{1,0:T(8,128)(2,1)S(1)} %get-tuple-element.55, bf16[2,1024,2048]{2,1,0:T(8,128)(2,1)} %out_proj.1), kind=kOutput, calls=%fused_computation.2 | convolution fusion | flops 3221225472 | bytes 8912896 | tf_op jit(solution)/shard_map/dot_general | solution.py:1175
  133.5 5.0 select_convert_fusion
  141.6 1.3 constant_dynamic-update-slice_fusion.1
  145.4 1.2 fusion.37
  146.9 2.8 constant_dynamic-update-slice_fusion
  149.7 6.1 %convert_bitcast_fusion.1 = bf16[1,1024,1024]{2,1,0:T(8,128)(2,1)S(1)} fusion(bf16[768,1024]{1,0:T(8,128)(2,1)} %collective-permute-done.2, bf16[768,1024]{1,0:T(8,128)(2,1)S(1)} %copy-done.14, bf16[1536,1024]{1,0:T(8,128)(2,1)} %constant_dynamic-update-slice_fusion, pred[1536]{0:T(1024)(128)(4,1)S(1)} %get-tuple-element.93), kind=kOutput, calls=%fused_computation.19 | convolution fusion | flops 3230138368 | bytes 8390144 | tf_op jit(solution)/shard_map/dot_general | solution.py:1267
  155.8 5.1 convert_bitcast_fusion
  160.9 2.4 pad_maximum_fusion.rest_0_
  163.3 120.7 %scan_backward.1 = (bf16[768,1024]{1,0:T(8,128)(2,1)}, f32[768,1024]{1,0:T(8,128)}, f32[768,128]{1,0:T(8,128)S(1)}, f32[16,8,128]{2,1,0:T(8,128)S(1)}, f32[1,102...) custom-call(f32[768,32]{1,0:T(8,128)S(1)} %bitcast.79, ...), custom_call_target="tpu_custom_call" | custom-call | flops 754974720 | bytes 50331648 | tf_op jit(solution)/shard_map/scan_backward/pallas_call | solution.py:1088
  284.8 4.0 pad_maximum_fusion.2.gate_pair
  288.8 3.3 maximum_bitcast_fusion.normed_t
  292.1 1.4 broadcast_in_dim.106.modes
  293.5 69.6 %middle.1 = (bf16[608,1024]{1,0:T(8,128)(2,1)}, bf16[768,2048]{1,0:T(8,128)(2,1)}, bf16[2,256,1024]{2,1,0:T(8,128)(2,1)}, bf16[2,1024,1024]{2,1,0:T(8,128)(2,1)}, bf16[2,1024,1024]{2,1,0:T(8,128)(2,1)}) custom-call(bf16[768,1024]{1,0:T(8,128)(2,1)} %get-tuple-element.58.pre_grad, f32[768,1024]{1,0:T(8,128)} %get-tuple-element.59.act_part, ...), custom_call_target="tpu_custom_call" | custom-call | flops 27000000512 | bytes 60000000 | tf_op jit(solution)/shard_map/middle/pallas_call | solution.py:672
  363.2 2.2 copy-done
  365.4 1.9 copy-done.1
  367.3 1.3 copy-done.4
  368.5 132.9 %tail_exchange.1 = (bf16[2,2,4,256,1024]{4,3,2,1,0:T(8,128)(2,1)}, bf16[2,2,4,256,1024]{4,3,2,1,0:T(8,128)(2,1)}, bf16[2,12,32,2048]{3,2,1,0:T(8,128)(2,1)S(1)}) custom-call(bf16[2,256,1024]{2,1,0:T(8,128)(2,1)S(1)} %copy-done.4, bf16[2,1024,1024]{2,1,0:T(8,128)(2,1)S(1)} %copy-done, bf16[2,12,32,2048]{3,2,1,0:T(8,128)(2,1)S(1)} %bitcast.76), custom_call_target="tpu_custom_call" | custom-call | flops 100000000 | bytes 300000000 | tf_op jit(solution)/shard_map/tail_exchange/pallas_call | solution.py:418
  501.5 1.7 copy-done.2
  503.1 9.5 %finish_rows.1 = (bf16[768,2048]{1,0:T(8,128)(2,1)}, bf16[768,2048]{1,0:T(8,128)(2,1)}) custom-call(bf16[768,2048]{1,0:T(8,128)(2,1)} %hidden.5, bf16[768,2048]{1,0:T(8,128)(2,1)} %out_grad.3, f32[768,128]{1,0:T(8,128)} %get-tuple-element.46.inverse, f32[1,2048]{1,0:T(1,128)} %bitcast.98, bf16[768,2048]{1,0:T(8,128)(2,1)} %bitcast.88, bf16[768,2048]{1,0:T(8,128)(2,1)} %bitcast.77), custom_call_target="tpu_custom_call" | custom-call | flops 25165824 | bytes 18874368 | tf_op jit(solution)/shard_map/finish_rows/pallas_call | solution.py:942
  512.6 1.6 slice.108
  514.1 1.2 slice_bitcast_fusion
  516.4 9.4 %write_grads.5 = f32[2,1024,2048]{2,1,0:T(8,128)} custom-call(s32[3]{0:T(128)S(1)} %pad_add_fusion.1.where_ref, bf16[2,2,4,256,1024]{4,3,2,1,0:T(8,128)(2,1)} %get-tuple-element.79.pieces_ref), custom_call_target="tpu_custom_call" | custom-call | flops 4194304 | bytes 25165824 | tf_op jit(solution)/shard_map/write_grads/pallas_call | solution.py:1149
  525.9 9.5 %write_grads.3.rest_0_ = f32[2,2048,2,1024]{3,2,1,0:T(2,128)} custom-call(s32[3]{0:T(128)S(1)} %pad_add_fusion.1.where_ref, bf16[2,2,4,256,1024]{4,3,2,1,0:T(8,128)(2,1)} %get-tuple-element.78.pieces_ref), custom_call_target="tpu_custom_call" | custom-call | flops 4194304 | bytes 25165824 | tf_op jit(solution)/shard_map/write_grads/pallas_call | solution.py:1149
  536.3 9.4 %write_grads.4 = f32[2,2048,2,1024]{3,2,1,0:T(2,128)} custom-call(s32[3]{0:T(128)S(1)} %pad_add_fusion.1.where_ref, bf16[2,2,4,256,1024]{4,3,2,1,0:T(8,128)(2,1)} %get-tuple-element.77.pieces_ref, f32[2,2048,2,1024]{3,2,1,0:T(2,128)} %write_grads.3.rest_0_), custom_call_target="tpu_custom_call", output_to_operand_aliasing={{}: (2, {})} | custom-call | flops 4194304 | bytes 25165824 | tf_op jit(solution)/shard_map/write_grads/pallas_call | solution.py:1149
  (98 shorter events, 20.0 us)
Async XLA Ops:
  7.2 505.4 %all-reduce.9.cloned.1.call-start = ((), (), s32[]{:S(2)}) async-start(), calls=%async_computation | async-start | bytes 2490368 | tf_op jit(solution)/shard_map/psum | solution.py:1358
  8.2 137.2 %collective-permute-start = (f32[768,1]{1,0:T(8,128)S(1)}, f32[768,1]{1,0:T(8,128)}, u32[]{:S(2)}, u32[]{:S(2)}) collective-permute-start(f32[768,1]{1,0:T(8,128)S(1)} %convert_element_type.42), channel_id=1, source_target_pairs={{0,4},{4,0},{8,12},{12,8},{16,20},{20,16},{24,28},{28,24},{1,5},{5... | collective-permute-start | bytes 9224 | tf_op jit(solution)/shard_map/ppermute | solution.py:1215
  16.3 66.8 %copy-start.17 = (bf16[2,128,1024]{2,1,0:T(8,128)(2,1)S(1)}, bf16[2,128,1024]{2,1,0:T(8,128)(2,1)}, u32[]{:S(2)}) copy-start(bf16[2,128,1024]{2,1,0:T(8,128)(2,1)} %dt_proj.1) | copy-start | bytes 1572868
  83.1 1.6 copy-start.15
  84.7 2.4 copy-start.3
  84.7 2.4 copy-start.6
  113.1 0.9 copy-start.5
  114.0 32.9 %collective-permute-start.1 = (bf16[768,1024]{1,0:T(8,128)(2,1)S(1)}, bf16[768,1024]{1,0:T(8,128)(2,1)}, u32[]{:S(2)}, u32[]{:S(2)}) collective-permute-start(bf16[768,1024]{1,0:T(8,128)(2,1)S(1)} %get-tuple-element.55), channel_id=1, source_target_pairs={{0,4},{4,0},{8,12},{12,8},{16,20},{20,16},{24,28},{28,24},{1,5},{5... | collective-permute-start | bytes 4718600 | tf_op jit(solution)/shard_map/ppermute | solution.py:1215
  117.8 31.8 %collective-permute-start.2 = (bf16[768,1024]{1,0:T(8,128)(2,1)}, bf16[768,1024]{1,0:T(8,128)(2,1)}, u32[]{:S(2)}, u32[]{:S(2)}) collective-permute-start(bf16[768,1024]{1,0:T(8,128)(2,1)} %get-tuple-element.87), channel_id=1, source_target_pairs={{0,4},{4,0},{8,12},{12,8},{16,20},{20,16},{24,28},{28,24},{1,5},{5... | collective-permute-start | bytes 4718600 | tf_op jit(solution)/shard_map/ppermute | solution.py:1215
  118.3 166.5 %collective-permute-start.3 = (bf16[768,1024]{1,0:T(8,128)(2,1)}, bf16[768,1024]{1,0:T(8,128)(2,1)}, u32[]{:S(2)}, u32[]{:S(2)}) collective-permute-start(bf16[768,1024]{1,0:T(8,128)(2,1)} %get-tuple-element.63), channel_id=1, source_target_pairs={{0,4},{4,0},{8,12},{12,8},{16,20},{20,16},{24,28},{28,24},{1,5},{5... | collective-permute-start | bytes 4718600 | tf_op jit(solution)/shard_map/ppermute | solution.py:1215
  126.9 6.7 %slice-start = ((s8[8388608]{0:T(1024)(128)(4,1)}), s8[4194304]{0:T(1024)(128)(4,1)S(1)}, s32[]{:S(2)}) async-start(s8[8388608]{0:T(1024)(128)(4,1)} %bitcast.102), calls=%async_computation.1 | async-start | bytes 8388608
  126.9 6.7 %slice-start.1 = ((s8[8388608]{0:T(1024)(128)(4,1)}), s8[4194304]{0:T(1024)(128)(4,1)S(1)}, s32[]{:S(2)}) async-start(s8[8388608]{0:T(1024)(128)(4,1)} %bitcast.102), calls=%async_computation.2 | async-start | bytes 8388608
  126.9 161.9 %collective-permute-start.4 = (bf16[768,1024]{0,1:T(8,128)(2,1)}, bf16[768,1024]{0,1:T(8,128)(2,1)}, u32[]{:S(2)}, u32[]{:S(2)}) collective-permute-start(bf16[768,1024]{0,1:T(8,128)(2,1)} %get-tuple-element.85), channel_id=1, source_target_pairs={{0,4},{4,0},{8,12},{12,8},{16,20},{20,16},{24,28},{28,24},{1,5},{5... | collective-permute-start | bytes 4718600 | tf_op jit(solution)/shard_map/ppermute | solution.py:1215
  138.5 5.9 %copy-start.10 = (f32[768,128]{1,0:T(8,128)S(1)}, f32[768,128]{1,0:T(8,128)}, u32[]{:S(2)}) copy-start(f32[768,128]{1,0:T(8,128)} %get-tuple-element.46.inverse) | copy-start | bytes 1179652
  141.6 1.3 copy-start.11
  141.6 1.3 copy-start.12
  141.6 1.7 copy-start.13
  146.7 2.9 copy-start.14
  149.7 6.1 %copy-start.16 = (bf16[1536,1024]{1,0:T(8,128)(2,1)S(1)}, bf16[1536,1024]{1,0:T(8,128)(2,1)}, u32[]{:S(2)}) copy-start(bf16[1536,1024]{1,0:T(8,128)(2,1)} %constant_dynamic-update-slice_fusion) | copy-start | bytes 9437188
  163.3 120.7 %copy-start.18 = (f32[16,1024]{1,0:T(8,128)S(1)}, f32[16,1024]{1,0:T(8,128)}, u32[]{:S(2)}) copy-start(f32[16,1024]{1,0:T(8,128)} %param.24) | copy-start | bytes 196612
  284.0 4.8 copy-start.7
  284.8 4.0 copy-start.9
  363.2 2.2 copy-start
  365.4 1.9 copy-start.1
  367.2 1.3 copy-start.4
  501.4 1.7 copy-start.2
  525.9 9.5 %copy-start.8 = (bf16[608,1024]{1,0:T(8,128)(2,1)S(1)}, bf16[608,1024]{1,0:T(8,128)(2,1)}, u32[]{:S(2)}) copy-start(bf16[608,1024]{1,0:T(8,128)(2,1)} %all-reduce.9.cloned.1.call-done) | copy-start | bytes 3735556
Sparse Core Ops, SparseCore 0:
  363.2 63.3 all-reduce.8

commit v3 on v2

--- a/solution.py
+++ b/solution.py
@@ -29,11 +29,30 @@
         [scratch[pl.ds(g, rows, stride=groups), :] for g in range(groups)], axis=1)
 
 
-def scan_forward_kernel(states, groups, rows, unroll,
-                        bc_ref, pre_ref, act_ref, z_ref, gg_ref, keep_ref, alog_ref, skip_ref,
-                        gated_ref, ggrad_ref, mixed_ref, h_ref, start_ref,
-                        rate_scr, state_scr, sk_scr, u_scr, y_scr):
+def scan_forward_kernel(states, groups, rows, unroll, count, joined,
+                        bc_ref, pre_ref, act_ref, z_ref, gg_ref, keep_ref, alog_ref, skip_ref, mode_ref,
+                        gated_ref, ggrad_ref, mixed_ref, h_ref, start_ref, *rest):
     chunk = pl.program_id(0)
+    if joined:
+        split_ref, rate_scr, state_scr, sk_scr, u_scr, y_scr, gated_all, ggrad_all, send_sems, recv_sems, local_sems = rest
+        tokens = rows * count
+        to_core = place()[4]
+
+        def pair_copies(at, i):
+            source, target = ((gated_all, gated_ref), (ggrad_all, ggrad_ref))[i]
+            base = at * rows
+            return (pltpu.make_async_copy(source.at[pl.ds(base, rows)], target.at[pl.ds(base, rows)], local_sems.at[at, i]),
+                    pltpu.make_async_remote_copy(
+                        src_ref=source.at[pl.ds(base, rows)], dst_ref=target.at[pl.ds(tokens + base, rows)],
+                        send_sem=send_sems.at[at, i], recv_sem=recv_sems.at[at, i], device_id=to_core, device_id_type=MESH))
+
+        @pl.when(chunk == 0)
+        def _():
+            barrier = pltpu.get_barrier_semaphore()
+            pl.semaphore_signal(barrier, inc=1, device_id=to_core, device_id_type=MESH)
+            pl.semaphore_wait(barrier, 1)
+    else:
+        rate_scr, state_scr, sk_scr, u_scr, y_scr = rest
 
     @pl.when(chunk == 0)
     def _():
@@ -68,50 +87,76 @@
     gg = gg_ref[...].astype(jnp.float32)
     sig = jax.nn.sigmoid(z)
     silu = z * sig
-    gated_ref[...] = (mixed_out * silu).astype(gated_ref.dtype)
+    gated = mixed_out * silu
+    gate_grad = (gg * mixed_out * sig * (1.0 + z * (1.0 - sig))).astype(ggrad_ref.dtype)
     mixed_ref[...] = gg * silu
-    ggrad_ref[...] = (gg * mixed_out * sig * (1.0 + z * (1.0 - sig))).astype(ggrad_ref.dtype)
-
-
-def scan_forward(bc, pre, act, z, gg, keep, a_log3, skip, rows=64, unroll=4):
+    if joined:
+        channels = gated.shape[1]
+        first = mode_ref[...]
+        split_ref[:, 0:channels] = (gated * first).astype(split_ref.dtype)
+        split_ref[:, channels:2 * channels] = (gated * (1.0 - first)).astype(split_ref.dtype)
+        at = pl.ds(pl.multiple_of(chunk * rows, rows), rows)
+        gated_all[at, :] = gated.astype(gated_ref.dtype)
+        ggrad_all[at, :] = gate_grad
+        for k in range(count):
+            @pl.when(chunk == k)
+            def _():
+                for i in range(2):
+                    for copy in pair_copies(k, i):
+                        copy.start()
+
+        @pl.when(chunk == count - 1)
+        def _():
+            for k in range(count):
+                for i in range(2):
+                    for copy in pair_copies(k, i):
+                        copy.wait()
+    else:
+        gated_ref[...] = gated.astype(gated_ref.dtype)
+        ggrad_ref[...] = gate_grad
+
+
+def scan_forward(bc, pre, act, z, gg, keep, a_log3, skip, mode, joined, rows=64, unroll=4):
     tokens, channels = pre.shape
     groups = channels // LANES
     states = a_log3.shape[0]
     count = tokens // rows
     wide = pl.BlockSpec((rows, channels), lambda i: (i, 0))
+    thin = pl.BlockSpec((rows, 1), lambda i: (i, 0))
     whole3 = pl.BlockSpec((states, groups, LANES), lambda i: (0, 0, 0))
+    low, f32 = jnp.bfloat16, jnp.float32
+    long = lambda: pltpu.VMEM((rows * groups, LANES), f32)
+    small = lambda: pltpu.VMEM((states, groups, LANES), f32)
+    anywhere = pl.BlockSpec(memory_space=pl.ANY)
+    tall = 2 * tokens if joined else tokens
+    settings = dict(collective_id=5, has_side_effects=True) if joined else {}
     return pl.pallas_call(
-        functools.partial(scan_forward_kernel, states, groups, rows, unroll),
+        functools.partial(scan_forward_kernel, states, groups, rows, unroll, count, joined),
         grid=(count,),
         in_specs=[
             pl.BlockSpec((rows, 2 * states), lambda i: (i, 0), memory_space=pltpu.SMEM),
-            wide, wide, wide, wide,
-            pl.BlockSpec((rows, 1), lambda i: (i, 0)),
-            whole3,
-            pl.BlockSpec((1, channels), lambda i: (0, 0)),
+            wide, wide, wide, wide, thin, whole3,
+            pl.BlockSpec((1, channels), lambda i: (0, 0)), thin,
         ],
         out_specs=[
-            wide, wide, wide,
+            anywhere if joined else wide, anywhere if joined else wide, wide,
             pl.BlockSpec((rows, states, groups, LANES), lambda i: (i, 0, 0, 0)),
             pl.BlockSpec((1, states, groups, LANES), lambda i: (i, 0, 0, 0)),
-        ],
+        ] + ([pl.BlockSpec((rows, 2 * channels), lambda i: (i, 0))] if joined else []),
         out_shape=[
-            jax.ShapeDtypeStruct((tokens, channels), jnp.bfloat16),
-            jax.ShapeDtypeStruct((tokens, channels), jnp.bfloat16),
-            jax.ShapeDtypeStruct((tokens, channels), jnp.float32),
-            jax.ShapeDtypeStruct((tokens, states, groups, LANES), jnp.float32),
-            jax.ShapeDtypeStruct((count, states, groups, LANES), jnp.float32),
-        ],
-        scratch_shapes=[
-            pltpu.VMEM((states, groups, LANES), jnp.float32),
-            pltpu.VMEM((states, groups, LANES), jnp.float32),
-            pltpu.VMEM((rows * groups, LANES), jnp.float32),
-            pltpu.VMEM((rows * groups, LANES), jnp.float32),
-            pltpu.VMEM((rows * groups, LANES), jnp.float32),
-        ],
-        compiler_params=pltpu.CompilerParams(vmem_limit_bytes=48 * 1024 * 1024),
+            jax.ShapeDtypeStruct((tall, channels), low),
+            jax.ShapeDtypeStruct((tall, channels), low),
+            jax.ShapeDtypeStruct((tokens, channels), f32),
+            jax.ShapeDtypeStruct((tokens, states, groups, LANES), f32),
+            jax.ShapeDtypeStruct((count, states, groups, LANES), f32),
+        ] + ([jax.ShapeDtypeStruct((tokens, 2 * channels), low)] if joined else []),
+        scratch_shapes=[small(), small(), long(), long(), long()] + ([
+            pltpu.VMEM((tokens, channels), low), pltpu.VMEM((tokens, channels), low),
+            pltpu.SemaphoreType.DMA((count, 2)), pltpu.SemaphoreType.DMA((count, 2)), pltpu.SemaphoreType.DMA((count, 2)),
+        ] if joined else []),
+        compiler_params=pltpu.CompilerParams(vmem_limit_bytes=48 * 1024 * 1024, **settings),
         name="scan_forward",
-    )(bc, pre, act, z, gg, keep, a_log3, skip)
+    )(bc, pre, act, z, gg, keep, a_log3, skip, mode)
 
 
 MESH = pl.DeviceIdType.MESH
@@ -158,7 +203,8 @@
 class Exchange:
     def __init__(self, prod, out, held, half_buf, quarter_buf, sems, summed=None):
         self.summed = summed
-        self.prod, self.out, self.held, self.half_buf, self.quarter_buf = prod, out, held, half_buf, quarter_buf
+        self.prod, self.held, self.half_buf, self.quarter_buf = prod, held, half_buf, quarter_buf
+        self.out, self.own = out
         (self.half_send, self.half_recv, self.quarter_send, self.quarter_recv,
          self.share_send, self.share_recv, self.core_send, self.core_recv, self.local) = sems
         x, y, self.to_x, self.to_y, self.to_core = place()
@@ -180,12 +226,12 @@
 
     def half_copy(self, mode, k):
         return pltpu.make_async_remote_copy(
-            src_ref=self.prod.at[mode, self.rows(mode, k, False)], dst_ref=self.half_buf.at[mode, k],
+            src_ref=self.prod[mode].at[self.rows(mode, k, False)], dst_ref=self.half_buf.at[mode, k],
             send_sem=self.half_send.at[mode, k], recv_sem=self.half_recv.at[mode, k],
             device_id=self.ways[mode][0], device_id_type=MESH)
 
     def keep_copy(self, mode, k):
-        return pltpu.make_async_copy(self.prod.at[mode, self.rows(mode, k, True)], self.held.at[mode, k], self.local.at[mode, k])
+        return pltpu.make_async_copy(self.prod[mode].at[self.rows(mode, k, True)], self.held.at[mode, k], self.local.at[mode, k])
 
     def quarter_copy(self, mode):
         return pltpu.make_async_remote_copy(
@@ -210,7 +256,7 @@
             device_id=self.to_core, device_id_type=MESH)
 
     def out_copy(self, mode):
-        return pltpu.make_async_copy(self.held.at[mode, 1], self.out.at[mode, 0, 0], self.local.at[mode, 2])
+        return pltpu.make_async_copy(self.held.at[mode, 1], self.own.at[mode], self.local.at[mode, 2])
 
     def start_shares(self, mode):
         for k in ((1, 2) if mode == 0 else (2, 1)):
@@ -276,6 +322,196 @@
                 self.out_copy(mode).wait()
 
 
+class Share:
+    def __init__(self, own, out, sems):
+        self.own, self.out = own, out
+        self.share_send, self.share_recv, self.core_send, self.core_recv = sems
+        _, _, self.to_x, self.to_y, self.to_core = place()
+
+    @staticmethod
+    def scratch():
+        return [DMA((2, 4)), DMA((2, 4)), DMA((2, 4)), DMA((2, 4))]
+
+    def share_copy(self, mode, k):
+        if k == 3:
+            source, way = (self.out.at[mode, 0, 1], self.to_x) if mode == 0 else (self.out.at[mode, 0, 2], self.to_y)
+        else:
+            source, way = self.own.at[mode], self.to_y if k == 1 else self.to_x
+        return pltpu.make_async_remote_copy(
+            src_ref=source, dst_ref=self.out.at[mode, 0, k], send_sem=self.share_send.at[mode, k],
+            recv_sem=self.share_recv.at[mode, k], device_id=way, device_id_type=MESH)
+
+    def core_copy(self, mode, k):
+        return pltpu.make_async_remote_copy(
+            src_ref=self.own.at[mode] if k == 0 else self.out.at[mode, 0, k], dst_ref=self.out.at[mode, 1, k],
+            send_sem=self.core_send.at[mode, k], recv_sem=self.core_recv.at[mode, k],
+            device_id=self.to_core, device_id_type=MESH)
+
+    def event(self, number):
+        for mode in range(2):
+            early, late = (1, 2) if mode == 0 else (2, 1)
+            if number == 0:
+                self.share_copy(mode, early).start()
+                self.share_copy(mode, late).start()
+                self.core_copy(mode, 0).start()
+            elif number == 1:
+                self.share_copy(mode, early).wait_recv()
+                self.share_copy(mode, 3).start()
+                self.core_copy(mode, early).start()
+            elif number == 2:
+                self.share_copy(mode, late).wait_recv()
+                self.core_copy(mode, late).start()
+            elif number == 3:
+                self.share_copy(mode, 3).wait_recv()
+                self.core_copy(mode, 3).start()
+            else:
+                for k in range(1, 4):
+                    self.share_copy(mode, k).wait_send()
+                for k in range(4):
+                    self.core_copy(mode, k).wait_send()
+                    self.core_copy(mode, k).wait_recv()
+
+
+class Reduce(Exchange):
+    def __init__(self, prod, own, held, half_buf, quarter_buf, sems):
+        half_send, half_recv, quarter_send, quarter_recv, keep = sems
+        super().__init__(prod, (None, own), held, half_buf, quarter_buf,
+                         (half_send, half_recv, quarter_send, quarter_recv, None, None, None, None, keep))
+
+    @staticmethod
+    def scratch(side, depth):
+        low = jnp.bfloat16
+        return [pltpu.VMEM((2, 2, side, depth), low), pltpu.VMEM((2, 2, side, depth), low), pltpu.VMEM((2, side, depth), low),
+                DMA((2, 2)), DMA((2, 2)), DMA((2,)), DMA((2,)), DMA((2, 3))]
+
+    def last(self):
+        for mode in range(2):
+            self.quarter_copy(mode).wait_recv()
+            add_rows(self.held.at[mode, 1], self.half_buf.at[mode, 1], self.quarter_buf.at[mode], self.side, 32)
+            pltpu.make_async_copy(self.held.at[mode, 1], self.own.at[mode], self.local.at[mode, 2]).start()
+
+    def done(self):
+        for mode in range(2):
+            for k in range(2):
+                self.half_copy(mode, k).wait_send()
+            self.quarter_copy(mode).wait_send()
+            pltpu.make_async_copy(self.held.at[mode, 1], self.own.at[mode], self.local.at[mode, 2]).wait()
+
+
+class LineReduce:
+    def __init__(self, part, own, acc, red, sems):
+        red_send, red_recv, local = sems
+        self.line = LineSum(part, own, acc, red, (red_send, red_recv, None, None, local))
+
+    @staticmethod
+    def scratch(pieces, rows, width):
+        low = jnp.bfloat16
+        return [pltpu.VMEM((2, pieces, rows, width), low), pltpu.VMEM((2, pieces, rows, width), low),
+                DMA((2, pieces)), DMA((2, pieces)), DMA((2,))]
+
+    def step(self, c, half):
+        line = self.line
+        begins, ends = line.place_of(half)
+
+        @pl.when(jnp.logical_not(begins))
+        def _():
+            line.red_copy(half, c).wait_recv()
+            add_rows(line.acc.at[half, c], line.acc.at[half, c], line.red.at[half, c], line.rows, 16)
+
+            @pl.when(jnp.logical_not(ends))
+            def _():
+                line.red_copy(half, c).start()
+
+    def turn(self, turn):
+        line = self.line
+        at_end = (line.z == 0) | (line.z == 3)
+        if 0 <= turn - 2 < line.pieces:
+            self.step(turn - 2, line.near)
+        if 0 <= turn - 4 < line.pieces:
+            @pl.when(jnp.logical_not(at_end))
+            def _():
+                self.step(turn - 4, 1 - line.near)
+        if 0 <= turn - 6 < line.pieces:
+            @pl.when(at_end)
+            def _():
+                self.step(turn - 6, 1 - line.near)
+
+    def done(self):
+        line = self.line
+        for half in range(2):
+            begins, ends = line.place_of(half)
+
+            @pl.when(ends)
+            def _():
+                line.own(half).start()
+                line.own(half).wait()
+
+            @pl.when(jnp.logical_not(ends))
+            def _():
+                for c in range(line.pieces):
+                    line.red_copy(half, c).wait_send()
+
+
+class LineBack:
+    def __init__(self, res, sems):
+        self.res = res
+        self.send, self.recv = sems
+        self.z = lax.axis_index("tensor")
+        self.near = jnp.where(self.z < 2, 1, 0)
+        self.pieces = res.shape[1]
+
+    @staticmethod
+    def scratch(pieces):
+        return [DMA((2, pieces)), DMA((2, pieces))]
+
+    def place_of(self, half):
+        along = jnp.where(half == 0, 3 - self.z, self.z)
+        return along == 0, along == 3
+
+    def copy(self, half, c):
+        return pltpu.make_async_remote_copy(
+            src_ref=self.res.at[half, c], dst_ref=self.res.at[half, c], send_sem=self.send.at[half, c],
+            recv_sem=self.recv.at[half, c], device_id={"tensor": self.z - 2 * half + 1}, device_id_type=MESH)
+
+    def begin(self, pieces):
+        for half in range(2):
+            _, ends = self.place_of(half)
+
+            @pl.when(ends)
+            def _():
+                for c in pieces:
+                    self.copy(half, c).start()
+
+    def step(self, c, half):
+        begins, ends = self.place_of(half)
+
+        @pl.when(jnp.logical_not(ends | begins))
+        def _():
+            self.copy(half, c).wait_recv()
+            self.copy(half, c).start()
+
+    def some(self, pieces, far):
+        for c in pieces:
+            self.step(c, 1 - self.near if far else self.near)
+
+    def done(self):
+        for half in range(2):
+            begins, ends = self.place_of(half)
+
+            @pl.when(begins)
+            def _():
+                for c in range(self.pieces):
+                    self.copy(half, c).wait_recv()
+
+            @pl.when(jnp.logical_not(begins))
+            def _():
+                for c in range(self.pieces):
+                    self.copy(half, c).wait_send()
+
+
+AHEAD = 2
+
+
 class LineSum:
     def __init__(self, part, res, acc, red, sems):
         self.part, self.res, self.acc, self.red = part, res, acc, red
@@ -311,14 +547,13 @@
     def own(self, half):
         return pltpu.make_async_copy(self.acc.at[half], self.res.at[half], self.local.at[1])
 
-    def begin(self):
-        self.load().wait()
+    def begin(self, pieces):
         for half in range(2):
             begins, _ = self.place_of(half)
 
             @pl.when(begins)
             def _():
-                for c in range(self.pieces):
+                for c in pieces:
                     self.red_copy(half, c).start()
 
     def reduce_step(self, c, half):
@@ -340,16 +575,15 @@
     def back_step(self, c, half):
         begins, ends = self.place_of(half)
 
-        @pl.when(jnp.logical_not(ends))
+        @pl.when(jnp.logical_not(ends | begins))
         def _():
             self.back_copy(half, c, self.res.at[half, c]).wait_recv()
-
-            @pl.when(jnp.logical_not(begins))
-            def _():
-                self.back_copy(half, c, self.res.at[half, c]).start()
+            self.back_copy(half, c, self.res.at[half, c]).start()
 
     def turn(self, turn):
         near, far = self.near, 1 - self.near
+        if turn + AHEAD < self.pieces:
+            self.begin((turn + AHEAD,))
         if turn < self.pieces:
             self.reduce_step(turn, near)
         if 1 <= turn <= self.pieces:
@@ -369,6 +603,11 @@
                 self.own(half).start()
                 self.own(half).wait()
 
+            @pl.when(begins)
+            def _():
+                for c in range(self.pieces):
+                    self.back_copy(half, c, self.res.at[half, c]).wait_recv()
+
             @pl.when(jnp.logical_not(ends))
             def _():
                 for c in range(self.pieces):
@@ -382,20 +621,17 @@
 
 def tail_kernel(count, *refs):
     prods, part = refs[:count], refs[count]
-    outs, res = refs[count + 1:2 * count + 1], refs[2 * count + 1]
-    scr = refs[2 * count + 2:]
+    outs, res, owns = refs[count + 1:2 * count + 1], refs[2 * count + 1], refs[2 * count + 2:3 * count + 2]
+    scr = refs[3 * count + 2:]
     line = LineSum(part, res, scr[0], scr[1], scr[2:7])
-    swaps = [Exchange(prods[i], outs[i], *scr[7 + 12 * i:10 + 12 * i], scr[10 + 12 * i:19 + 12 * i]) for i in range(count)]
-    swaps[0].summed = True
+    swaps = [Exchange([prods[i].at[0], prods[i].at[1]], (outs[i], owns[i]), *scr[7 + 12 * i:10 + 12 * i], scr[10 + 12 * i:19 + 12 * i]) for i in range(count)]
     line.load().start()
-    swaps[0].event(8)
     greet()
-    swaps[1].event(0)
-    swaps[0].event(9)
-    line.begin()
+    swaps[0].event(0)
+    line.load().wait()
+    line.begin(range(AHEAD))
     last = line.turns
-    plan = {4: [(1, 1)], 6: [(0, 4)], 8: [(1, 2)], 10: [(0, 5)], 12: [(1, 3)], 15: [(0, 6)], 17: [(1, 4)], 20: [(1, 5)],
-            24: [(1, 6)]}
+    plan = {3: [(0, 1)], 5: [(0, 2)], 9: [(0, 3)], 13: [(0, 4)], 17: [(0, 5)], 21: [(0, 6)]}
     for turn in range(last):
         line.turn(turn)
         for which, number in plan.get(turn, []):
@@ -407,7 +643,7 @@
 
 def tail_exchange(products, normed_part, pieces=12):
     count = len(products)
-    side, depth = products[0].shape[1:]
+    side, depth = products[0].shape[1] // 4, products[0].shape[2]
     tokens, width = normed_part.shape
     part = normed_part.reshape(2, pieces, tokens // 2 // pieces, width)
     low = jnp.bfloat16
@@ -418,14 +654,15 @@
     outs = pl.pallas_call(
         functools.partial(tail_kernel, count),
         in_specs=[anywhere] * (count + 1),
-        out_specs=[anywhere] * (count + 1),
-        out_shape=[jax.ShapeDtypeStruct((2, 2, 4, side, depth), low)] * count + [jax.ShapeDtypeStruct(part.shape, low)],
+        out_specs=[anywhere] * (2 * count + 1),
+        out_shape=[jax.ShapeDtypeStruct((2, 2, 4, side, depth), low)] * count + [jax.ShapeDtypeStruct(part.shape, low)]
+        + [jax.ShapeDtypeStruct((2, side, depth), low)] * count,
         scratch_shapes=scratch,
         cost_estimate=pl.CostEstimate(flops=100_000_000, bytes_accessed=300_000_000, transcendentals=0),
         compiler_params=pltpu.CompilerParams(collective_id=1, has_side_effects=True, vmem_limit_bytes=40 * 1024 * 1024),
         name="tail_exchange",
     )(*products, part)
-    return outs[:count], outs[count].reshape(tokens, width)
+    return outs[:count], outs[count + 1:], outs[count].reshape(tokens, width)
 
 
 NT = (((1,), (1,)), ((), ()))
@@ -441,20 +678,20 @@
 
 
 def middle_kernel(pre_grad, act_part, coeff, conv_sum, inner_x, act_b, rank_b, dt_proj, x_wide, conv_w, docs, modes,
-                  gate_pair, normed_t, inv, extra, hidden, in_gate, in_inner,
-                  rows_out, normed_out, gate_own, inner_prod, gate_prod,
+                  gate_grads, normed_t, inv, extra, hidden, in_gate, in_inner, out_own, gate_own, z_own,
+                  rows_out, normed_out, inner_prod, out_shared, gate_shared, z_res,
                   w_buf, mask_buf, pair_buf, conv_buf, stage, stage_n, hid_buf, proj_buf, proj_recv, proj_fin, gain_buf, gain_recv,
-                  held, half_buf, quarter_buf,
-                  half_send, half_recv, quarter_send, quarter_recv, keep_sems,
-                  red_send, red_recv, all_send, all_recv, core_sems, gain_send, gain_recv_sem, w_sems, stage_sems, n_sems, hid_sems):
+                  red_send, red_recv, all_send, all_recv, core_sems, gain_send, gain_recv_sem, w_sems, stage_sems, n_sems, hid_sems,
+                  *share_sems):
     tokens, channels = pre_grad.shape
     low = jnp.bfloat16
     rank_dim = dt_proj.shape[1]
     z = lax.axis_index("tensor")
     x, y, to_x, to_y, to_core = place()
     share = tokens // 4
-    gate = Exchange(gate_prod, None, held, half_buf, quarter_buf,
-                    (half_send, half_recv, quarter_send, quarter_recv, None, None, None, None, keep_sems))
+    outs = Share(out_own, out_shared, share_sems[0:4])
+    gate = Share(gate_own, gate_shared, share_sems[4:8])
+    back = LineBack(z_res, share_sems[8:10])
     width = hidden.shape[1]
     slices = width // w_buf.shape[2]
     cut = w_buf.shape[2]
@@ -501,6 +738,7 @@
 
     for off in (1, 2, 3):
         red_copy(off).start()
+    outs.event(0)
 
     def product(pair, target, number):
         pair_tokens = pair.shape[0]
@@ -522,9 +760,6 @@
         for slot in range(2):
             pltpu.make_async_copy(stage.at[slot], target.at[0, pl.ds(0, tall)], stage_sems.at[slot]).wait()
 
-    product(gate_pair, gate_prod, 0)
-    gate.event(0)
-
     for off in (1, 2, 3):
         red_copy(off).wait_recv()
     mine = pl.ds(pl.multiple_of(z * share, share), share)
@@ -555,6 +790,7 @@
     bias0, bias1 = lax.fori_loop(0, tokens // block, dt_sums, (none_row, none_row))
     for off in (1, 2, 3):
         all_copy(off).wait_recv()
+    back.begin((0, 1))
 
     def act_block(i, bias):
         at = pl.ds(pl.multiple_of(i * block, block), block)
@@ -570,7 +806,10 @@
 
     conv_buf[pl.ds(tokens, 8), :] = jnp.zeros((8, channels), jnp.float32)
     bias = lax.fori_loop(0, tokens // block, act_block, none_row)
-    gate.event(1)
+    outs.event(1)
+    gate.event(0)
+    back.some((0,), True)
+    back.begin((2,))
     taps = conv_w.shape[0]
     thin = 64
 
@@ -597,6 +836,8 @@
             send_sem=core_sems.at[0], recv_sem=core_sems.at[1], device_id=to_core, device_id_type=MESH)
 
     core_copy().start()
+    back.some((1,), True)
+    back.begin((3,))
 
     for i in range(slices):
         slot = i % 2
@@ -609,7 +850,7 @@
 
         def normed_rows(j, gain, slot=slot):
             at = pl.ds(pl.multiple_of(j * third, third), third)
-            gate_grad, grad = gate_pair[at, :], pair_buf[at, :]
+            gate_grad, grad = gate_grads[at, :], pair_buf[at, :]
             zero = dot_f32(gate_grad, w_buf[slot, 0], NT) + dot_f32(grad, w_buf[slot, 2], NT)
             one = dot_f32(gate_grad, w_buf[slot, 1], NT) + dot_f32(grad, w_buf[slot, 3], NT)
             picked = jnp.where(inv[at, 1:2] > 0.5, zero, one)
@@ -622,8 +863,21 @@
         if i + 2 < slices:
             for copy in weight_copies(i + 2):
                 copy.start()
-        if i == 1:
-            gate.event(2)
+        if i == 0:
+            back.some((2,), True)
+            back.some((0,), False)
+            back.begin((4,))
+        elif i == 1:
+            back.some((3,), True)
+            back.some((1,), False)
+            back.begin((5,))
+        elif i == 2:
+            outs.event(2)
+            back.some((4,), True)
+            back.some((2,), False)
+        elif i == 3:
+            back.some((5,), True)
+            back.some((3,), False)
     for slot in range(2):
         pltpu.make_async_copy(stage_n.at[slot], normed_out.at[:, pl.ds(0, cut)], n_sems.at[slot]).wait()
 
@@ -636,6 +890,9 @@
         gain_copy(off).start()
     core_copy().wait_recv()
     product(pair_buf, inner_prod, 1)
+    back.some((4, 5), False)
+    gate.event(1)
+    outs.event(3)
     for m in range(2):
         proj = proj_fin[...] * widened(modes[m, pl.ds(0, tokens), :], proj_fin.shape[1])
         rows_out[pl.ds(m * mode_rows, span), :] = dot_f32(proj, act_b[...], TN)[:span].astype(low)
@@ -647,12 +904,11 @@
     used = taps + 3 + extra.shape[0] + len(gains)
     tail_rows.append(jnp.zeros((32 - used, channels), jnp.float32))
     rows_out[pl.ds(2 * mode_rows, 32), :] = jnp.concatenate(tail_rows, axis=0).astype(low)
-    for mode in range(2):
-        gate.quarter_copy(mode).wait_recv()
-        add_rows(gate_own.at[mode], half_buf.at[mode, 1], quarter_buf.at[mode], gate.side, 32)
-        gate.quarter_copy(mode).wait_send()
-        for k in range(2):
-            gate.half_copy(mode, k).wait_send()
+    gate.event(2)
+    gate.event(3)
+    outs.event(4)
+    gate.event(4)
+    back.done()
     for off in (1, 2, 3):
         red_copy(off).wait_send()
         all_copy(off).wait_send()
@@ -661,7 +917,7 @@
 
 
 def middle(pre_grad, act_part, coeff, conv_sum, inner_x, act_b, rank_b, dt_proj, x_wide, conv_w, docs, modes,
-           gate_pair, normed_t, inv, extra, hidden, in_gate, in_inner):
+           gate_grads, normed_t, inv, extra, hidden, in_gate, in_inner, out_own, gate_own, z_own):
     tokens, channels = pre_grad.shape
     width = hidden.shape[1]
     low = jnp.bfloat16
@@ -671,14 +927,15 @@
     vmem, anywhere = pl.BlockSpec(memory_space=pltpu.VMEM), pl.BlockSpec(memory_space=pl.ANY)
     return pl.pallas_call(
         middle_kernel,
-        in_specs=[vmem] * 16 + [anywhere] * 3,
-        out_specs=[vmem, anywhere, vmem, anywhere, anywhere],
+        in_specs=[vmem] * 16 + [anywhere] * 6,
+        out_specs=[vmem] + [anywhere] * 5,
         out_shape=[
             jax.ShapeDtypeStruct((2 * mode_rows + 32, channels), low),
             jax.ShapeDtypeStruct((tokens, width), low),
-            jax.ShapeDtypeStruct((2, side, channels), low),
             jax.ShapeDtypeStruct((2, 4 * side, channels), low),
-            jax.ShapeDtypeStruct((2, 4 * side, channels), low),
+            jax.ShapeDtypeStruct((2, 2, 4) + out_own.shape[1:], low),
+            jax.ShapeDtypeStruct((2, 2, 4) + gate_own.shape[1:], low),
+            jax.ShapeDtypeStruct(z_own.shape, low),
         ],
         scratch_shapes=[
             pltpu.VMEM((2, 4, cut, channels), low),
@@ -693,18 +950,15 @@
             pltpu.VMEM((tokens, 2 * LANES), low),
             pltpu.VMEM((8, width), jnp.float32),
             pltpu.VMEM((3, 8, width), jnp.float32),
-            pltpu.VMEM((2, 2, side, channels), low),
-            pltpu.VMEM((2, 2, side, channels), low),
-            pltpu.VMEM((2, side, channels), low),
-            DMA((2, 2)), DMA((2, 2)), DMA((2,)), DMA((2,)), DMA((2, 3)),
             DMA((3,)), DMA((3,)), DMA((3,)), DMA((3,)), DMA((2,)), DMA((3,)), DMA((3,)),
             DMA((2, 4)), DMA((2,)), DMA((2,)), DMA((2,)),
-        ],
+        ] + Share.scratch() + Share.scratch() + LineBack.scratch(z_own.shape[1]),
+        input_output_aliases={21: 5},
         cost_estimate=pl.CostEstimate(flops=27_000_000_000, bytes_accessed=60_000_000, transcendentals=1_000_000),
         compiler_params=pltpu.CompilerParams(collective_id=3, has_side_effects=True, vmem_limit_bytes=61 * 1024 * 1024),
         name="middle",
     )(pre_grad, act_part, coeff, conv_sum, inner_x, act_b, rank_b, dt_proj, x_wide, conv_w, docs, modes,
-      gate_pair, normed_t, inv, extra, hidden, in_gate, in_inner)
+      gate_grads, normed_t, inv, extra, hidden, in_gate, in_inner, out_own, gate_own, z_own)
 
 
 def split_tail(part, count):
@@ -719,9 +973,10 @@
 
 
 def front_kernel(coeffs_wide, hidden, gain, conv_w, conv_b, docs, modes, x_wide, out_grad, view, out_proj,
-                 w_inner, w_gate, normed, inverse, conv_sum, inner_x, act_b, gate_z, gated_grad, rank_out, coeff_out,
+                 w_inner, w_gate, normed_pair, cotan_pair, modes_pair,
+                 normed, inverse, conv_sum, inner_x, act_b, gate_z, gated_grad, rank_out, coeff_out,
                  acc, view_buf, wide, stage, w_out, proj_buf, proj_recv, proj_fin,
-                 view_sems, stage_sems, out_sems, red_send, red_recv, all_send, all_recv):
+                 view_sems, stage_sems, out_sems, red_send, red_recv, all_send, all_recv, pair_send, pair_recv, pair_local):
     tokens, width = hidden.shape
     channels = conv_w.shape[1]
     groups = channels // LANES
@@ -738,6 +993,22 @@
     barrier = pltpu.get_barrier_semaphore()
     for off in (1, 2, 3):
         pl.semaphore_signal(barrier, inc=1, device_id=z_at(off), device_id_type=MESH)
+    core, to_core = lax.axis_index("dp") % 2, place()[4]
+    pl.semaphore_signal(barrier, inc=1, device_id=to_core, device_id_type=MESH)
+
+    def half_of(ref, which):
+        return ref.at[:, pl.ds(pl.multiple_of(which * (width // 2), width // 2), width // 2)]
+
+    own_rows, other_rows = pl.ds(0, tokens), pl.ds(tokens, tokens)
+    pairs = ((half_of(normed, core), half_of(normed, 1 - core), normed_pair.at[own_rows], normed_pair.at[other_rows]),
+             (half_of(out_grad, core), half_of(out_grad, 1 - core), cotan_pair.at[own_rows], cotan_pair.at[other_rows]),
+             (modes, modes, modes_pair.at[:, own_rows], modes_pair.at[:, other_rows]))
+
+    def pair_copies(i):
+        mine, theirs, here, there = pairs[i]
+        return (pltpu.make_async_copy(mine, here, pair_local.at[i]),
+                pltpu.make_async_remote_copy(src_ref=theirs, dst_ref=there, send_sem=pair_send.at[i], recv_sem=pair_recv.at[i],
+                                             device_id=to_core, device_id_type=MESH))
 
     def view_copy(i, m):
         tall = deep * 2 * groups
@@ -856,9 +1127,12 @@
             src_ref=proj_fin.at[mine], dst_ref=proj_fin.at[mine], send_sem=all_send.at[off - 1],
             recv_sem=all_recv.at[off - 1], device_id=z_at(off), device_id_type=MESH)
 
-    pl.semaphore_wait(barrier, 3)
+    pl.semaphore_wait(barrier, 4)
     for off in (1, 2, 3):
         red_copy(off).start()
+    for i in range(3):
+        for copy in pair_copies(i):
+            copy.start()
     third = tokens // 3
 
     def grad_block(i):
@@ -888,6 +1162,9 @@
     for off in (1, 2, 3):
         red_copy(off).wait_send()
         all_copy(off).wait_send()
+    for i in range(3):
+        for copy in pair_copies(i):
+            copy.wait()
 
 
 def front(hidden, gain, conv_w, conv_b, docs, modes, x_wide, out_grad, in_proj, out_proj, coeffs_wide):
@@ -902,9 +1179,10 @@
     return pl.pallas_call(
         functools.partial(front_kernel, coeffs_wide),
         in_specs=[vmem] * 8 + [anywhere] * 2,
-        out_specs=[anywhere] * 2 + [vmem] * 9,
+        out_specs=[anywhere] * 5 + [vmem] * 9,
         out_shape=[
-            shape((2, width, channels), low), shape((2, width, channels), low), shape((tokens, width), low),
+            shape((2, width, channels), low), shape((2, width, channels), low), shape((2 * tokens, width // 2), low),
+            shape((2 * tokens, width // 2), low), shape((2, 2 * tokens, LANES), low), shape((tokens, width), low),
             shape((tokens, LANES), f32), shape((tokens, channels), f32), shape((tokens, channels), f32),
             shape((tokens, channels), low), shape((tokens, channels), f32), shape((tokens, channels), f32),
             shape((tokens, LANES), low), shape((tokens, LANES), f32),
@@ -918,7 +1196,7 @@
             pltpu.VMEM((tokens, 2 * LANES), low),
             pltpu.VMEM((3, tokens // 4, 2 * LANES), low),
             pltpu.VMEM((tokens, 2 * LANES), low),
-            DMA((2, 2)), DMA((2, 2, 2)), DMA((2,)), DMA((3,)), DMA((3,)), DMA((3,)), DMA((3,)),
+            DMA((2, 2)), DMA((2, 2, 2)), DMA((2,)), DMA((3,)), DMA((3,)), DMA((3,)), DMA((3,)), DMA((3,)), DMA((3,)), DMA((3,)),
         ],
         cost_estimate=pl.CostEstimate(flops=20_000_000_000, bytes_accessed=80_000_000, transcendentals=1_000_000),
         compiler_params=pltpu.CompilerParams(collective_id=4, has_side_effects=True, vmem_limit_bytes=60 * 1024 * 1024),
@@ -953,35 +1231,45 @@
 def scan_backward_kernel(states, groups, rows, unroll, count, joined,
                          bc_ref, pre_ref, act_ref, mixed_ref, keep_ref, alog_ref, skip_ref, h_ref, start_ref, *rest):
     if joined:
-        prod_ref, part_ref, rest = rest[0], rest[1], rest[2:]
+        prods, part_ref, rest = rest[:4], rest[4], rest[5:]
     pgrad_ref, apart_ref, bcg_ref, sum_ref, skipsum_ref = rest[:5]
     rest = rest[5:]
     if joined:
-        shared_ref, res_ref, rest = rest[0], rest[1], rest[2:]
+        out_own, gate_own, z_own, rest = rest[0], rest[1], rest[2], rest[3:]
     carry_ref, rate_scr, decay_scr, sk_scr, u_scr, dy_scr, w_scr, s_scr, p_scr, q_scr = rest[:10]
     rest = rest[10:]
     chunk = pl.program_id(0)
     if joined:
-        line = LineSum(part_ref, res_ref, rest[0], rest[1], rest[2:7])
-        swapped = Exchange(prod_ref, shared_ref, *rest[7:10], rest[10:19])
+        line = LineReduce(part_ref, z_own, rest[0], rest[1], rest[2:5])
+        outs = Reduce(prods[:2], out_own, *rest[5:8], rest[8:13])
+        gate = Reduce(prods[2:], gate_own, *rest[13:16], rest[16:21])
 
         @pl.when(chunk == 0)
         def _():
-            line.load().start()
+            line.line.load().start()
             greet()
-            swapped.event(0)
-            line.begin()
-
-        for number, at in enumerate((2, 4, 7, 9, 11), start=1):
-            @pl.when(chunk == min(at, count - 1))
-            def _():
-                swapped.event(number)
+            outs.event(0)
+            line.line.load().wait()
+            line.line.begin((0,))
 
         for at in range(1, count):
             @pl.when(chunk == at)
             def _():
-                for turn in range(line.turns * (at - 1) // (count - 1), line.turns * at // (count - 1)):
-                    line.turn(turn)
+                if at < line.line.pieces:
+                    line.line.begin((at,))
+                if at == 2:
+                    outs.event(1)
+                elif at == 3:
+                    gate.event(0)
+                elif at == 5:
+                    outs.event(2)
+                elif at == 6:
+                    outs.last()
+                elif at == 8:
+                    gate.event(1)
+                elif at == 10:
+                    gate.event(2)
+                line.turn(at)
 
     @pl.when(chunk == 0)
     def _():
@@ -1060,17 +1348,18 @@
     if joined:
         @pl.when(chunk == count - 1)
         def _():
-            swapped.event(6)
-            swapped.event(7)
-            line.finish()
-
-
-def scan_backward(bc, pre, act, mixed, keep, a_log3, skip, h, starts, product=None, z_part=None, rows=64, unroll=3, pieces=6):
+            gate.last()
+            outs.done()
+            gate.done()
+            line.done()
+
+
+def scan_backward(bc, pre, act, mixed, keep, a_log3, skip, h, starts, products=None, z_part=None, rows=64, unroll=3, pieces=6):
     tokens, channels = pre.shape
     groups = channels // LANES
     states = a_log3.shape[0]
     count = tokens // rows
-    joined = product is not None
+    joined = products is not None
     wide = pl.BlockSpec((rows, channels), lambda i: (count - 1 - i, 0))
     whole3 = pl.BlockSpec((states, groups, LANES), lambda i: (0, 0, 0))
     row = pl.BlockSpec((1, channels), lambda i: (0, 0))
@@ -1079,11 +1368,11 @@
     long = lambda: pltpu.VMEM((rows * groups, LANES), jnp.float32)
     extra, extra_shapes, extra_scratch = [], [], []
     if joined:
-        side, depth = product.shape[1] // 4, product.shape[2]
+        side, depth = products[0].shape[0] // 4, products[0].shape[1]
         part = z_part.reshape(2, pieces, tokens // 2 // pieces, z_part.shape[1])
-        extra = [product, part]
-        extra_shapes = [jax.ShapeDtypeStruct((2, 2, 4, side, depth), jnp.bfloat16), jax.ShapeDtypeStruct(part.shape, jnp.bfloat16)]
-        extra_scratch = LineSum.scratch(*part.shape[1:]) + Exchange.scratch(side, depth)
+        extra = list(products) + [part]
+        extra_shapes = [jax.ShapeDtypeStruct((2, side, depth), jnp.bfloat16)] * 2 + [jax.ShapeDtypeStruct(part.shape, jnp.bfloat16)]
+        extra_scratch = LineReduce.scratch(*part.shape[1:]) + Reduce.scratch(side, depth) + Reduce.scratch(side, depth)
     settings = dict(collective_id=2, has_side_effects=True) if joined else {}
     outs = pl.pallas_call(
         functools.partial(scan_backward_kernel, states, groups, rows, unroll, count, joined),
@@ -1097,7 +1386,7 @@
             pl.BlockSpec((1, states, groups, LANES), lambda i: (count - 1 - i, 0, 0, 0)),
         ] + [anywhere] * len(extra),
         out_specs=[wide, wide, pl.BlockSpec((rows, LANES), lambda i: (count - 1 - i, 0)), whole3, row]
-        + [anywhere] * len(extra),
+        + [anywhere] * len(extra_shapes),
         out_shape=[
             jax.ShapeDtypeStruct((tokens, channels), jnp.bfloat16),
             jax.ShapeDtypeStruct((tokens, channels), jnp.float32),
@@ -1114,12 +1403,10 @@
         compiler_params=pltpu.CompilerParams(vmem_limit_bytes=52 * 1024 * 1024, **settings),
         name="scan_backward",
     )(bc, pre, act, mixed, keep, a_log3, skip, h, starts, *extra)
-    if joined:
-        outs = list(outs[:6]) + [outs[6].reshape(tokens, z_part.shape[1])]
     return outs
 
 
-def writer_kernel(place, side, depth, where_ref, pieces_ref, *rest):
+def writer_kernel(place, side, depth, where_ref, pieces_ref, own_ref, *rest):
     out_ref, wide_scr, sems = rest[-3:]
     x, y, core = where_ref[0], where_ref[1], where_ref[2]
     copies = []
@@ -1131,7 +1418,8 @@
                 qy = y if k in (0, 2) else 1 - y
                 row = (qx * 2 + qy if mode == 0 else qy * 2 + qx) * side
                 at = (mode * 2 + owner) * 4 + k
-                wide_scr[at] = pieces_ref[mode, owner, k].astype(jnp.float32)
+                piece = own_ref[mode] if owner == 0 and k == 0 else pieces_ref[mode, owner, k]
+                wide_scr[at] = piece.astype(jnp.float32)
                 if place == "columns":
                     target = out_ref.at[mode, pl.ds(pl.multiple_of(row, side), side),
                                         pl.ds(pl.multiple_of(c * depth, depth), depth)]
@@ -1143,21 +1431,21 @@
         copy.wait()
 
 
-def write_out(place, shape, where, pieces, filled):
+def write_out(place, shape, where, pieces, own, filled):
     side, depth = pieces.shape[3:]
     held = [] if filled is None else [filled]
     return pl.pallas_call(
         functools.partial(writer_kernel, place, side, depth),
-        in_specs=[pl.BlockSpec(memory_space=pltpu.SMEM), pl.BlockSpec(memory_space=pltpu.VMEM)]
+        in_specs=[pl.BlockSpec(memory_space=pltpu.SMEM), pl.BlockSpec(memory_space=pltpu.VMEM), pl.BlockSpec(memory_space=pltpu.VMEM)]
         + [pl.BlockSpec(memory_space=pl.ANY)] * len(held),
         out_specs=pl.BlockSpec(memory_space=pl.ANY),
         out_shape=jax.ShapeDtypeStruct(shape, jnp.float32),
-        input_output_aliases={2: 0} if held else {},
+        input_output_aliases={3: 0} if held else {},
         scratch_shapes=[pltpu.VMEM((16, side, depth), jnp.float32), pltpu.SemaphoreType.DMA((16,))],
         cost_estimate=pl.CostEstimate(flops=16 * side * depth, bytes_accessed=16 * side * depth * 6, transcendentals=0),
         compiler_params=pltpu.CompilerParams(vmem_limit_bytes=48 * 1024 * 1024),
         name="write_grads",
-    )(where, pieces, *held)
+    )(where, pieces, own, *held)
 
 
 def lagged(values, offset):
@@ -1250,15 +1538,6 @@
     nothing = jnp.zeros((), low)
     dims = (((0,), (0,)), ((), ()))
 
-    def col_half(values, which):
-        return lax.dynamic_slice_in_dim(values, which * half_width, half_width, 1)
-
-    def pair_half(values):
-        return jnp.concatenate([col_half(values, core), swap(col_half(values, 1 - core), CORE)], axis=0)
-
-    def pair_all(values):
-        return jnp.concatenate([values, swap(values, CORE)], axis=0)
-
     def masked_products(left, right, modes, mask_left):
         products = []
         for chosen in (modes, jnp.logical_not(modes)):
@@ -1275,14 +1554,10 @@
         modes_own = jnp.broadcast_to(jnp.stack([first_mode, jnp.logical_not(first_mode)]), (2, tokens, LANES)).astype(low)
         x_wide = jnp.pad(jnp.swapaxes(x_proj, 1, 2), ((0, 0), (0, 96), (0, 0)))
         facts = jnp.concatenate([first_mode.astype(jnp.float32)] + same_doc[1:], axis=1)
-        (in_inner, in_gate, normed_b, inverse, conv_sum, inner_x, activated_b, gate_z, gated_grad, rank_b, coeffs) = front(
+        (in_inner, in_gate, normed_pair, cotan_pair, modes, _, inverse, conv_sum, inner_x, activated_b, gate_z, gated_grad, rank_b, coeffs) = front(
             hidden_in, norm_gain[None], conv_weight, conv_bias[None], facts, modes_own, x_wide, out_grad, in_proj, out_proj,
             2 * state_dim)
         coeffs = coeffs[:, :2 * state_dim]
-        sib_mode = swap(first_mode.astype(jnp.float32), CORE) > 0.5
-        pair_mode = jnp.concatenate([first_mode, sib_mode], axis=0)
-        normed_pair = pair_half(normed_b)
-        cotan_pair = pair_half(tie(out_grad, rank_b))
     else:
         hidden = hidden_in.astype(jnp.float32)
         inverse = lax.rsqrt(jnp.mean(hidden * hidden, axis=1, keepdims=True) + EPS)
@@ -1303,17 +1578,21 @@
     keep = same_doc[1]
     a_log3 = a_log.reshape(state_dim, groups, LANES)
     skip_row = skip_gain[None]
-    gated_b, gate_grad_b, mixed_grad, states, starts = scan_forward(
-        coeffs, step_pre, activated_b, gate_z, gated_grad, keep, a_log3, skip_row)
-    partial_out = pick_dot(gated_b, out_proj, first_mode).astype(low)
+    forward = scan_forward(coeffs, step_pre, activated_b, gate_z, gated_grad, keep, a_log3, skip_row,
+                           first_mode.astype(jnp.float32), by_hand)
+    gated_b, gate_grad_b, mixed_grad, states, starts = forward[:5]
     if by_hand:
-        gated_pair = pair_all(gated_b)
-        ggrad_pair = pair_all(gate_grad_b)
-        out_product = masked_products(gated_pair, cotan_pair, pair_mode, True)
+        masks = [modes[m, :, :1] for m in range(2)]
+        products = [lax.dot_general(gated_b * masks[m], cotan_pair, dims, preferred_element_type=jnp.float32).astype(low)
+                    for m in range(2)]
+        products += [lax.dot_general(normed_pair, gate_grad_b * masks[m], dims, preferred_element_type=jnp.float32).astype(low)
+                     for m in range(2)]
+        partial_out = jnp.dot(forward[5], out_proj.reshape(2 * channels, model_width), preferred_element_type=jnp.float32).astype(low)
         back = scan_backward(coeffs, step_pre, activated_b, mixed_grad, keep, a_log3, skip_row, states, starts,
-                             out_product, partial_out)
-        summed_out, out_shared = back[6], back[5]
+                             products, partial_out)
+        out_own, gate_own, z_own = back[5:]
     else:
+        partial_out = pick_dot(gated_b, out_proj, first_mode).astype(low)
         back = scan_backward(coeffs, step_pre, activated_b, mixed_grad, keep, a_log3, skip_row, states, starts)
         summed_out = lax.psum(partial_out, "tensor")
         out_proj_grad = lax.psum(weight_grads(gated_b, out_grad, first_mode).astype(low), "dp").astype(jnp.float32)
@@ -1323,12 +1602,12 @@
     mode_rows = x_proj.shape[2] + rank_dim
     if by_hand:
         later = jnp.stack([same_doc[0]] + [leading(same_doc[k], k) for k in range(1, conv_taps)], axis=1)[:, :, 0]
-        modes = jnp.broadcast_to(jnp.stack([pair_mode, jnp.logical_not(pair_mode)]), (2, 2 * tokens, LANES)).astype(low)
         row_facts = jnp.concatenate([inverse[:, :1], first_mode.astype(jnp.float32)], axis=1)
-        rows, normed_low, gate_own, inner_product, _ = middle(
+        rows, normed_low, inner_product, out_shared, gate_shared, z_res = middle(
             pre_grad_b, act_part, coeff_grad, conv_sum, inner_x, activated_b, rank_b, dt_proj, x_wide, conv_weight, later, modes,
-            ggrad_pair, jnp.swapaxes(normed_pair, 0, 1), row_facts, jnp.concatenate([a_log_grad, skips], axis=0), hidden_in,
-            in_gate, in_inner)
+            gate_grad_b[:tokens], jnp.swapaxes(normed_pair, 0, 1), row_facts, jnp.concatenate([a_log_grad, skips], axis=0),
+            hidden_in, in_gate, in_inner, out_own, gate_own, z_own)
+        summed_out = z_res.reshape(tokens, model_width)
     else:
         pre_grad = pre_grad_b.astype(jnp.float32)
         dt_bias_grad = jnp.stack([
@@ -1357,14 +1636,14 @@
                                 a_log_grad, skips, gain_part], axis=0).astype(low)
     summed_rows = lax.psum(rows, "dp")
     if by_hand:
-        (gate_shared, inner_shared), normed_sum = tail_exchange([gate_own, inner_product], normed_low)
+        (inner_shared,), (inner_own,), normed_sum = tail_exchange([inner_product], normed_low)
 
         output, input_grad = finish(hidden_in, out_grad, inverse, norm_gain[None], summed_out, normed_sum)
         where = tie(where, summed_rows)
-        out_proj_grad = write_out("columns", (2, channels, model_width), where, out_shared, None)
+        out_proj_grad = write_out("columns", (2, channels, model_width), where, out_shared, out_own, None)
         in_shape = (2, model_width, 2, channels)
-        in_proj_grad = write_out(1, in_shape, where, gate_shared, None)
-        in_proj_grad = write_out(0, in_shape, where, inner_shared, in_proj_grad)
+        in_proj_grad = write_out(1, in_shape, where, gate_shared, gate_own, None)
+        in_proj_grad = write_out(0, in_shape, where, inner_shared, inner_own, in_proj_grad)
     else:
         inner_proj_grad = lax.psum(weight_grads(normed_b, x_grad_b, first_mode).astype(low), "dp")
         in_proj_grad = jnp.stack([inner_proj_grad, gate_proj_grad], axis=2).astype(jnp.float32)

time: 564 us -> 523 us (0.927)
  Pallas kernels: 454 us -> 429 us
  local copies, waits for them, and re-layouts: 42.1 us -> 29.5 us
  other arithmetic: 16.9 us -> 4.74 us
  matrix products: 26.2 us -> 36.2 us
    pallas_call x1, Pallas kernels: 121 us -> 87.4 us  [scan_backward(): pl.pallas_call(functools.partial(scan_backward_kernel, states, groups, ro...]
    dot_general x2 -> x5, matrix products: 11.2 us -> 33.3 us  [the longest x1 11.8 us: shards(): jnp.dot(forward[5], out_proj.reshape(2 * channels, model_width), preferre...]
    pallas_call x1, Pallas kernels: 69.6 us -> 87.8 us  [middle(): pl.pallas_call(middle_kernel, in_specs=[vmem] * 16 + [anywhere] * 6, out_...]
    pallas_call x1, Pallas kernels: 133 us -> 118 us  [tail_exchange(): pl.pallas_call(functools.partial(tail_kernel, count), in_specs=[anywhere]...]
    dynamic_slice x2 -> x0, local copies, waits for them, and re-layouts: 7.73 us -> none  [col_half(): return lax.dynamic_slice_in_dim(values, which * half_width, half_width, 1)]
    dot_general x2 -> x1, matrix products: 8.44 us -> 2.37 us  [pick_dot(): jnp.dot(left_side, weights[1], preferred_element_type=jnp.float32)]
    dot_general x2 -> x1, matrix products: 6.5 us -> 0.56 us  [pick_dot(): jnp.dot(left_side, weights[0], preferred_element_type=jnp.float32)]
  transfers between devices with their start and end apart: 6 -> 1, of which waited for: 0 -> 0; matrix products, arithmetic and copies ran while one was open for 11% -> 0% of each run, Pallas kernels for 64% -> 25%
where the time goes in v3:
time: 523 us; the launch traced here: 514 us
  Pallas kernels  429 us (82%)
  matrix products  36.2 us (7%)
  local copies, waits for them, and re-layouts  29.5 us (6%)
  between operations  14.8 us (3%)
    pallas_call x1, Pallas kernels, tail_exchange(): pl.pallas_call(functools.partial(tail_kernel, count), in_specs=[anywhere]...  118 us
    pallas_call x1, Pallas kernels, middle(): pl.pallas_call(middle_kernel, in_specs=[vmem] * 16 + [anywhere] * 6, out_...  87.8 us
    pallas_call x1, Pallas kernels, scan_backward(): pl.pallas_call(functools.partial(scan_backward_kernel, states, groups, ro...  87.4 us
    pallas_call x1, Pallas kernels, front(): pl.pallas_call(functools.partial(front_kernel, coeffs_wide), in_specs=[vm...  66.6 us
    pallas_call x1, Pallas kernels, scan_forward(): pl.pallas_call(functools.partial(scan_forward_kernel, states, groups, row...  31.5 us
    pallas_call x3, Pallas kernels, write_out(): pl.pallas_call(functools.partial(writer_kernel, place, side, depth), in_s...  28.3 us
    dot_general x1, matrix products, shards(): jnp.dot(forward[5], out_proj.reshape(2 * channels, model_width), preferre...  11.8 us
    dot_general x2, matrix products, shards(): lax.dot_general(normed_pair, gate_grad_b * masks[m], dims, preferred_elem...  11.6 us
  transfers between devices with their start and end apart: 1, of which 0 were waited for; matrix products, arithmetic and copies ran while one was open for 0% of the time, Pallas kernels for 25%

profile of v3, /device:TPU:0, one launch (start us, length us, event | category | flops | bytes accessed | tf_op | source)
XLA Modules:
  0.0 514.4 jit_solution(6300100295178703392)
XLA Ops:
  7.9 0.9 fusion.29
  9.5 0.8 fusion.38
  10.3 0.9 copy.75
  11.2 0.9 copy.66.docs
  12.1 2.2 pad.31.x_wide
  14.3 1.0 broadcast_in_dim.63.modes
  15.3 66.6 %front.1 = (bf16[2,2048,1024]{2,1,0:T(8,128)(2,1)}, bf16[2,2048,1024]{2,1,0:T(8,128)(2,1)}, bf16[1536,1024]{1,0:T(8,128)(2,1)}, bf16[1536,1024]{1,0:T(8,128)(2,1...) custom-call(bf16[768,2048]{1,0:T(8,128)(2,1)} %hidden.5, ...), custom_call_target="tpu_custom_call" | custom-call | flops 20000000000 | bytes 80000000 | tf_op jit(solution)/shard_map/front/pallas_call | solution.py:1179
  81.9 1.4 slice_reduce_fusion
  83.3 4.7 copy.73
  88.6 2.4 select_add_fusion.pre_ref
  91.0 31.5 %scan_forward.1 = (bf16[1536,1024]{1,0:T(8,128)(2,1)}, bf16[1536,1024]{1,0:T(8,128)(2,1)}, f32[768,1024]{1,0:T(8,128)}, f32[768,16,8,128]{3,2,1,0:T(8,128)}, f32...) custom-call(f32[768,32]{1,0:T(8,128)S(1)} %bitcast.64, f32[768,1024]{1,0:T(8,128)} %select_add_fusion.pre_ref, ...), custom_call_target="tpu_custom_call" | custom-call | tf_op jit(solution)/shard_map/scan_forward/pallas_call | solution.py:133
  122.5 3.0 slice.97.gate_grads
  125.6 6.8 %fusion.14.rest_2_ = bf16[1024,1024]{1,0:T(8,128)(2,1)} fusion(bf16[1536,1024]{1,0:T(8,128)(2,1)S(1)} %copy-done.11, bf16[1536,1024]{1,0:T(8,128)(2,1)} %get-tuple-element.64, bf16[1536]{0:T(1024)(128)(2,1)S(1)} %get-tuple-element.91), kind=kOutput, calls=%fused_computation.12 | convolution fusion | flops 3223846912 | bytes 8391680 | tf_op jit(solution)/shard_map/dot_general | solution.py:1588
  132.4 4.8 fusion.8.rest_0_
  137.2 5.0 fusion.11.rest_1_
  142.2 4.8 fusion.17.rest_3_
  147.6 0.9 pad_maximum_fusion.inv
  148.5 11.8 %convolution_convert_fusion = bf16[768,2048]{1,0:T(8,128)(2,1)} fusion(bf16[768,2048]{1,0:T(8,128)(2,1)} %get-tuple-element.65, bf16[2048,2048]{1,0:T(8,128)(2,1)} %bitcast.87), kind=kOutput, calls=%fused_computation | convolution fusion | flops 6444023808 | bytes 14680064 | tf_op jit(solution)/shard_map/dot_general | solution.py:1590
  160.4 87.4 %scan_backward.1 = (bf16[768,1024]{1,0:T(8,128)(2,1)}, f32[768,1024]{1,0:T(8,128)}, f32[768,128]{1,0:T(8,128)S(1)}, f32[16,8,128]{2,1,0:T(8,128)S(1)}, f32[1,102...) custom-call(f32[768,32]{1,0:T(8,128)S(1)} %bitcast.65, ...), custom_call_target="tpu_custom_call" | custom-call | flops 754974720 | bytes 50331648 | tf_op jit(solution)/shard_map/scan_backward/pallas_call | solution.py:1377
  249.3 1.1 maximum_bitcast_fusion.docs
  250.4 87.8 %middle.1 = (bf16[608,1024]{1,0:T(8,128)(2,1)}, bf16[768,2048]{1,0:T(8,128)(2,1)}, bf16[2,1024,1024]{2,1,0:T(8,128)(2,1)}, bf16[2,2,4,256,1024]{4,3,2,1,0:T(8,12...) custom-call(bf16[768,1024]{1,0:T(8,128)(2,1)} %get-tuple-element.66., ...), custom_call_target="tpu_custom_call", output_to_operand_aliasing={{5}: (21, {})} | custom-call | flops 27000000512 | bytes 60000000 | tf_op jit(solution)/shard_map/middle/pallas_call | solution.py:928
  338.3 2.2 copy-done.1
  340.5 1.9 copy-done.2
  342.4 117.7 %tail_exchange.1 = (bf16[2,2,4,256,1024]{4,3,2,1,0:T(8,128)(2,1)}, bf16[2,12,32,2048]{3,2,1,0:T(8,128)(2,1)S(1)}, bf16[2,256,1024]{2,1,0:T(8,128)(2,1)S(1)}) custom-call(bf16[2,1024,1024]{2,1,0:T(8,128)(2,1)S(1)} %copy-done.1, bf16[2,12,32,2048]{3,2,1,0:T(8,128)(2,1)S(1)} %bitcast.62), custom_call_target="tpu_custom_call" | custom-call | flops 100000000 | bytes 300000000 | tf_op jit(solution)/shard_map/tail_exchange/pallas_call | solution.py:654
  460.1 1.7 copy-done.3
  461.7 9.7 %finish_rows.1 = (bf16[768,2048]{1,0:T(8,128)(2,1)}, bf16[768,2048]{1,0:T(8,128)(2,1)}) custom-call(bf16[768,2048]{1,0:T(8,128)(2,1)} %hidden.5, bf16[768,2048]{1,0:T(8,128)(2,1)} %out_grad.3, f32[768,128]{1,0:T(8,128)} %get-tuple-element.51.inverse, f32[1,2048]{1,0:T(1,128)} %bitcast.83, bf16[768,2048]{1,0:T(8,128)(2,1)} %bitcast.74, bf16[768,2048]{1,0:T(8,128)(2,1)} %bitcast.63), custom_call_target="tpu_custom_call" | custom-call | flops 25165824 | bytes 18874368 | tf_op jit(solution)/shard_map/finish_rows/pallas_call | solution.py:1220
  471.5 1.5 slice.112
  473.1 1.1 slice.114
  474.2 1.2 slice_bitcast_fusion
  476.3 9.5 %write_grads.5 = f32[2,1024,2048]{2,1,0:T(8,128)} custom-call(s32[3]{0:T(128)S(1)} %pad_add_fusion.where_ref, bf16[2,2,4,256,1024]{4,3,2,1,0:T(8,128)(2,1)} %get-tuple-element.89.pieces_ref, bf16[2,256,1024]{2,1,0:T(8,128)(2,1)S(1)} %copy-done.6), custom_call_target="tpu_custom_call" | custom-call | flops 4194304 | bytes 25165824 | tf_op jit(solution)/shard_map/write_grads/pallas_call | solution.py:1437
  485.8 9.4 %write_grads.3.rest_0_ = f32[2,2048,2,1024]{3,2,1,0:T(2,128)} custom-call(s32[3]{0:T(128)S(1)} %pad_add_fusion.where_ref, bf16[2,2,4,256,1024]{4,3,2,1,0:T(8,128)(2,1)} %get-tuple-element.88.pieces_ref, bf16[2,256,1024]{2,1,0:T(8,128)(2,1)S(1)} %copy-done.5), custom_call_target="tpu_custom_call" | custom-call | flops 4194304 | bytes 25165824 | tf_op jit(solution)/shard_map/write_grads/pallas_call | solution.py:1437
  495.3 9.4 %write_grads.4 = f32[2,2048,2,1024]{3,2,1,0:T(2,128)} custom-call(s32[3]{0:T(128)S(1)} %pad_add_fusion.where_ref, bf16[2,2,4,256,1024]{4,3,2,1,0:T(8,128)(2,1)} %get-tuple-element.86.pieces_ref, bf16[2,256,1024]{2,1,0:T(8,128)(2,1)S(1)} %get-tuple-element.87.own_ref, f32[2,2048,2,1024]{3,2,1,0:T(2,128)} %write_grads.3.rest_0_), custom_call_target="tpu_custom_call", output_to_operand_aliasing={{}: (3, {})} | custom-call | flops 4194304 | bytes 25165824 | tf_op jit(solution)/shard_map/write_grads/pallas_call | solution.py:1437
  (68 shorter events, 7.4 us)
Async XLA Ops:
  7.2 464.4 %all-reduce.9.cloned.1.call-start = ((), (), s32[]{:S(2)}) async-start(), calls=%async_computation | async-start | bytes 2490368 | tf_op jit(solution)/shard_map/psum | solution.py:1637
  83.3 4.7 copy-start.13
  83.3 4.7 copy-start.15
  88.6 2.4 copy-start
  88.6 2.4 copy-start.4
  88.6 2.4 copy-start.8
  122.5 9.8 %copy-start.7 = (f32[12,16,8,128]{3,2,1,0:T(8,128)}, f32[12,16,8,128]{3,2,1,0:T(8,128)S(1)}, u32[]{:S(2)}) copy-start(f32[12,16,8,128]{3,2,1,0:T(8,128)S(1)} %get-tuple-element.59.start_ref) | copy-start | bytes 2359300
  122.5 3.0 copy-start.11
  125.6 6.8 %copy-start.17 = (bf16[1536,1024]{1,0:T(8,128)(2,1)S(1)}, bf16[1536,1024]{1,0:T(8,128)(2,1)}, u32[]{:S(2)}) copy-start(bf16[1536,1024]{1,0:T(8,128)(2,1)} %get-tuple-element.60) | copy-start | bytes 9437188
  125.6 6.8 %copy-start.18 = (bf16[1536,1024]{1,0:T(8,128)(2,1)S(1)}, bf16[1536,1024]{1,0:T(8,128)(2,1)}, u32[]{:S(2)}) copy-start(bf16[1536,1024]{1,0:T(8,128)(2,1)} %get-tuple-element.62) | copy-start | bytes 9437188
  137.2 5.0 copy-start.14
  142.2 5.4 %copy-start.12 = (f32[768,128]{1,0:T(8,128)S(1)}, f32[768,128]{1,0:T(8,128)}, u32[]{:S(2)}) copy-start(f32[768,128]{1,0:T(8,128)} %get-tuple-element.51.inverse) | copy-start | bytes 1179652
  160.4 88.2 %copy-start.16 = (f32[16,1024]{1,0:T(8,128)S(1)}, f32[16,1024]{1,0:T(8,128)}, u32[]{:S(2)}) copy-start(f32[16,1024]{1,0:T(8,128)} %param.24) | copy-start | bytes 196612
  247.8 0.7 copy-start.9
  338.3 2.2 copy-start.1
  340.5 1.9 copy-start.2
  460.1 1.7 copy-start.3
  473.1 2.3 copy-start.10
  474.2 2.1 copy-start.6
  476.3 9.5 %copy-start.5 = (bf16[2,256,1024]{2,1,0:T(8,128)(2,1)S(1)}, bf16[2,256,1024]{2,1,0:T(8,128)(2,1)}, u32[]{:S(2)}) copy-start(bf16[2,256,1024]{2,1,0:T(8,128)(2,1)} %get-tuple-element.76.gate_own.own_ref) | copy-start | bytes 3145732
Sparse Core Ops, SparseCore 0:
  338.4 67.8 all-reduce.8

commit v4 on v3

--- a/solution.py
+++ b/solution.py
@@ -1204,28 +1204,201 @@
     )(hidden, gain, conv_w, conv_b, docs, modes, x_wide, out_grad, view, out_proj)
 
 
-def finish_kernel(hidden, out_grad, inverse, gain, summed_out, normed_sum, output, input_grad):
-    rows = hidden[...].astype(jnp.float32)
-    output[...] = (rows + summed_out[...].astype(jnp.float32)).astype(output.dtype)
-    scale = inverse[:, 0:1]
-    scaled = normed_sum[...].astype(jnp.float32) * gain[...]
-    mean = jnp.mean(scaled * rows, axis=1, keepdims=True)
-    input_grad[...] = (out_grad[...].astype(jnp.float32) + scale * scaled - rows * (scale * scale * scale) * mean).astype(input_grad.dtype)
-
-
-def finish(hidden, out_grad, inverse, gain, summed_out, normed_sum):
+def products_kernel(gated, cotan, normed, gate, modes, split, weights,
+                    out0, out1, gate0, gate1, partial, normed_t,
+                    left_buf, right_buf, mode_buf, split_buf, w_buf, turned, mask_buf, stage, stage_wide,
+                    load_sems, w_sems, stage_sems, wide_sems, turned_sem):
+    pair_tokens, channels = left_buf.shape[1:]
+    tokens, deep = split_buf.shape
+    low = jnp.bfloat16
+    block = 128
+    loads = [pltpu.make_async_copy(source, target, load_sems.at[i]) for i, (source, target) in enumerate((
+        (gated, left_buf.at[0]), (cotan, right_buf.at[0]), (modes, mode_buf), (normed, left_buf.at[1]), (gate, right_buf.at[1]),
+        (split, split_buf)))]
+    for copy in loads:
+        copy.start()
+    half = w_buf.shape[0] // 2
+    w_loads = [pltpu.make_async_copy(weights.at[m], w_buf.at[pl.ds(m * half, half)], w_sems.at[m]) for m in range(2)]
+    for copy in w_loads:
+        copy.start()
+    tall = stage.shape[1]
+    turns = channels // tall
+    flights = [None, None]
+
+    def turn_left(which):
+        def body(i, nothing):
+            at = pl.ds(pl.multiple_of(i * block, block), block)
+            turned[at, :] = left_buf[which, :, at].T
+            return nothing
+        lax.fori_loop(0, channels // block, body, 0)
+
+    def multiply(which, targets):
+        for m in range(2):
+            def mask_rows(i, nothing):
+                at = pl.ds(pl.multiple_of(i * block, block), block)
+                mask_buf[at, :] = right_buf[which, at, :] * widened(mode_buf[m, at, :], channels)
+                return nothing
+            lax.fori_loop(0, pair_tokens // block, mask_rows, 0)
+            for j in range(turns):
+                slot = (m * turns + j) % 2
+                if flights[slot] is not None:
+                    flights[slot].wait()
+                stage[slot] = dot_f32(turned[pl.ds(j * tall, tall), :], mask_buf[...]).astype(low)
+                flights[slot] = pltpu.make_async_copy(stage.at[slot], targets[m].at[pl.ds(j * tall, tall)], stage_sems.at[slot])
+                flights[slot].start()
+
+    for copy in loads[:3]:
+        copy.wait()
+    turn_left(0)
+    multiply(0, (out0, out1))
+    for copy in loads[3:5]:
+        copy.wait()
+    turn_left(1)
+    out_turned = pltpu.make_async_copy(turned, normed_t, turned_sem)
+    out_turned.start()
+    multiply(1, (gate0, gate1))
+    loads[5].wait()
+    for copy in w_loads:
+        copy.wait()
+    part = stage_wide.shape[1]
+    wide_flights = [None, None]
+    for j in range(tokens // part):
+        slot = j % 2
+        if wide_flights[slot] is not None:
+            wide_flights[slot].wait()
+        stage_wide[slot] = dot_f32(split_buf[pl.ds(j * part, part), :], w_buf[...]).astype(low)
+        wide_flights[slot] = pltpu.make_async_copy(stage_wide.at[slot], partial.at[pl.ds(j * part, part)], wide_sems.at[slot])
+        wide_flights[slot].start()
+    for copy in flights + wide_flights + [out_turned]:
+        copy.wait()
+
+
+def make_products(gated, cotan, normed, gate, modes, split, weights):
+    pair_tokens, channels = gated.shape
+    tokens, deep = split.shape
+    width = weights.shape[2]
+    low = jnp.bfloat16
+    anywhere = pl.BlockSpec(memory_space=pl.ANY)
+    square = jax.ShapeDtypeStruct((channels, channels), low)
+    return pl.pallas_call(
+        products_kernel,
+        in_specs=[anywhere] * 7,
+        out_specs=[anywhere] * 6,
+        out_shape=[square] * 4 + [jax.ShapeDtypeStruct((tokens, width), low), jax.ShapeDtypeStruct((channels, pair_tokens), low)],
+        scratch_shapes=[
+            pltpu.VMEM((2, pair_tokens, channels), low), pltpu.VMEM((2, pair_tokens, channels), low),
+            pltpu.VMEM((2, pair_tokens, LANES), low), pltpu.VMEM((tokens, deep), low), pltpu.VMEM((deep, width), low),
+            pltpu.VMEM((channels, pair_tokens), low), pltpu.VMEM((pair_tokens, channels), low),
+            pltpu.VMEM((2, channels // 2, channels), low), pltpu.VMEM((2, tokens // 3, width), low),
+            DMA((6,)), DMA((2,)), DMA((2,)), DMA((2,)), DMA,
+        ],
+        cost_estimate=pl.CostEstimate(flops=20_000_000_000, bytes_accessed=45_000_000, transcendentals=0),
+        compiler_params=pltpu.CompilerParams(vmem_limit_bytes=56 * 1024 * 1024),
+        name="products",
+    )(gated, cotan, normed, gate, modes, split, weights)
+
+
+def final_kernel(side, depth, where_ref, out_shared, out_own, gate_shared, gate_own, inner_shared, inner_own,
+                 hidden, out_grad, inverse, gain, summed_out, normed_sum,
+                 out_ref, in_ref, output, input_grad,
+                 narrow, wide, row_in, row_out, in_sems, out_sems, row_in_sems, row_out_sems):
+    x, y, core = where_ref[0], where_ref[1], where_ref[2]
+    low, f32 = jnp.bfloat16, jnp.float32
+    block = row_in.shape[2]
+    jobs = []
+    for which, (shared, own) in enumerate(((out_shared, out_own), (gate_shared, gate_own), (inner_shared, inner_own))):
+        for mode in range(2):
+            for owner in range(2):
+                c = core if owner == 0 else 1 - core
+                for k in range(4):
+                    qx = x if k in (0, 1) else 1 - x
+                    qy = y if k in (0, 2) else 1 - y
+                    row = (qx * 2 + qy if mode == 0 else qy * 2 + qx) * side
+                    if which == 0:
+                        target = out_ref.at[mode, pl.ds(pl.multiple_of(row, side), side),
+                                            pl.ds(pl.multiple_of(c * depth, depth), depth)]
+                    else:
+                        target = in_ref.at[mode, pl.ds(pl.multiple_of(c * 4 * side + row, side), side), 2 - which, :]
+                    source = own.at[mode] if owner == 0 and k == 0 else shared.at[mode, owner, k]
+                    jobs.append((source, target))
+    slots = narrow.shape[0]
+    loads = [pltpu.make_async_copy(jobs[i][0], narrow.at[i % slots], in_sems.at[i % slots]) for i in range(len(jobs))]
+    stores = [pltpu.make_async_copy(wide.at[i % slots], jobs[i][1], out_sems.at[i % slots]) for i in range(len(jobs))]
+    count = hidden.shape[0] // block
+
+    def row_loads(i):
+        at = pl.ds(i * block, block)
+        return [pltpu.make_async_copy(ref.at[at], row_in.at[i % 2, j], row_in_sems.at[i % 2, j])
+                for j, ref in enumerate((hidden, out_grad, summed_out, normed_sum))]
+
+    def row_stores(i):
+        at = pl.ds(i * block, block)
+        return [pltpu.make_async_copy(row_out.at[i % 2, j], ref.at[at], row_out_sems.at[i % 2, j])
+                for j, ref in enumerate((output, input_grad))]
+
+    for copy in row_loads(0) + row_loads(1):
+        copy.start()
+    for i in range(slots):
+        loads[i].start()
+    per = -(-len(jobs) // count)
+    for i in range(count):
+        for copy in row_loads(i):
+            copy.wait()
+        if i >= 2:
+            for copy in row_stores(i - 2):
+                copy.wait()
+        rows = row_in[i % 2, 0].astype(f32)
+        scale = inverse[pl.ds(i * block, block), 0:1]
+        scaled = row_in[i % 2, 3].astype(f32) * gain[...]
+        mean = jnp.mean(scaled * rows, axis=1, keepdims=True)
+        row_out[i % 2, 0] = (rows + row_in[i % 2, 2].astype(f32)).astype(low)
+        row_out[i % 2, 1] = (row_in[i % 2, 1].astype(f32) + scale * scaled - rows * (scale * scale * scale) * mean).astype(low)
+        for copy in row_stores(i):
+            copy.start()
+        if i + 2 < count:
+            for copy in row_loads(i + 2):
+                copy.start()
+        for p in range(i * per, min((i + 1) * per, len(jobs))):
+            loads[p].wait()
+            if p >= slots:
+                stores[p - slots].wait()
+            wide[p % slots] = narrow[p % slots].astype(f32)
+            stores[p].start()
+            if p + slots < len(jobs):
+                loads[p + slots].start()
+    for p in range(len(jobs) - slots, len(jobs)):
+        stores[p].wait()
+    for i in (count - 2, count - 1):
+        for copy in row_stores(i):
+            copy.wait()
+
+
+def final(where, out_shared, out_own, gate_shared, gate_own, inner_shared, inner_own, hidden, out_grad, inverse, gain,
+          summed_out, normed_sum):
+    side, depth = out_own.shape[1:]
     tokens, width = hidden.shape
-    rows = 128
-    wide = pl.BlockSpec((rows, width), lambda i: (i, 0))
+    channels = 4 * side
+    low, f32 = jnp.bfloat16, jnp.float32
+    anywhere, vmem = pl.BlockSpec(memory_space=pl.ANY), pl.BlockSpec(memory_space=pltpu.VMEM)
+    block, slots = 128, 6
     return pl.pallas_call(
-        finish_kernel,
-        grid=(tokens // rows,),
-        in_specs=[wide, wide, pl.BlockSpec((rows, LANES), lambda i: (i, 0)), pl.BlockSpec((1, width), lambda i: (0, 0)), wide, wide],
-        out_specs=[wide, wide],
-        out_shape=[jax.ShapeDtypeStruct((tokens, width), jnp.bfloat16)] * 2,
-        cost_estimate=pl.CostEstimate(flops=16 * tokens * width, bytes_accessed=12 * tokens * width, transcendentals=0),
-        name="finish_rows",
-    )(hidden, out_grad, inverse, gain, summed_out, normed_sum)
+        functools.partial(final_kernel, side, depth),
+        in_specs=[pl.BlockSpec(memory_space=pltpu.SMEM)] + [anywhere] * 8 + [vmem] * 2 + [anywhere] * 2,
+        out_specs=[anywhere] * 4,
+        out_shape=[
+            jax.ShapeDtypeStruct((2, channels, width), f32), jax.ShapeDtypeStruct((2, width, 2, channels), f32),
+            jax.ShapeDtypeStruct((tokens, width), low), jax.ShapeDtypeStruct((tokens, width), low),
+        ],
+        scratch_shapes=[
+            pltpu.VMEM((slots, side, depth), low), pltpu.VMEM((slots, side, depth), f32),
+            pltpu.VMEM((2, 4, block, width), low), pltpu.VMEM((2, 2, block, width), low),
+            DMA((slots,)), DMA((slots,)), DMA((2, 4)), DMA((2, 2)),
+        ],
+        cost_estimate=pl.CostEstimate(flops=50_000_000, bytes_accessed=91_000_000, transcendentals=0),
+        compiler_params=pltpu.CompilerParams(vmem_limit_bytes=40 * 1024 * 1024),
+        name="final_rows",
+    )(where, out_shared, out_own, gate_shared, gate_own, inner_shared, inner_own, hidden, out_grad, inverse, gain,
+      summed_out, normed_sum)
 
 
 def scan_backward_kernel(states, groups, rows, unroll, count, joined,
@@ -1406,48 +1579,6 @@
     return outs
 
 
-def writer_kernel(place, side, depth, where_ref, pieces_ref, own_ref, *rest):
-    out_ref, wide_scr, sems = rest[-3:]
-    x, y, core = where_ref[0], where_ref[1], where_ref[2]
-    copies = []
-    for mode in range(2):
-        for owner in range(2):
-            c = core if owner == 0 else 1 - core
-            for k in range(4):
-                qx = x if k in (0, 1) else 1 - x
-                qy = y if k in (0, 2) else 1 - y
-                row = (qx * 2 + qy if mode == 0 else qy * 2 + qx) * side
-                at = (mode * 2 + owner) * 4 + k
-                piece = own_ref[mode] if owner == 0 and k == 0 else pieces_ref[mode, owner, k]
-                wide_scr[at] = piece.astype(jnp.float32)
-                if place == "columns":
-                    target = out_ref.at[mode, pl.ds(pl.multiple_of(row, side), side),
-                                        pl.ds(pl.multiple_of(c * depth, depth), depth)]
-                else:
-                    target = out_ref.at[mode, pl.ds(pl.multiple_of(c * 4 * side + row, side), side), place, :]
-                copies.append(pltpu.make_async_copy(wide_scr.at[at], target, sems.at[at]))
-                copies[-1].start()
-    for copy in copies:
-        copy.wait()
-
-
-def write_out(place, shape, where, pieces, own, filled):
-    side, depth = pieces.shape[3:]
-    held = [] if filled is None else [filled]
-    return pl.pallas_call(
-        functools.partial(writer_kernel, place, side, depth),
-        in_specs=[pl.BlockSpec(memory_space=pltpu.SMEM), pl.BlockSpec(memory_space=pltpu.VMEM), pl.BlockSpec(memory_space=pltpu.VMEM)]
-        + [pl.BlockSpec(memory_space=pl.ANY)] * len(held),
-        out_specs=pl.BlockSpec(memory_space=pl.ANY),
-        out_shape=jax.ShapeDtypeStruct(shape, jnp.float32),
-        input_output_aliases={3: 0} if held else {},
-        scratch_shapes=[pltpu.VMEM((16, side, depth), jnp.float32), pltpu.SemaphoreType.DMA((16,))],
-        cost_estimate=pl.CostEstimate(flops=16 * side * depth, bytes_accessed=16 * side * depth * 6, transcendentals=0),
-        compiler_params=pltpu.CompilerParams(vmem_limit_bytes=48 * 1024 * 1024),
-        name="write_grads",
-    )(where, pieces, own, *held)
-
-
 def lagged(values, offset):
     padding = [(offset, 0)] + [(0, 0)] * (values.ndim - 1)
     return jnp.pad(values, padding)[: values.shape[0]]
@@ -1533,7 +1664,6 @@
     rank = lax.axis_index("dp")
     core, x_at, y_at = rank % 2, (rank // 2) % 2, rank // 4
     where = jnp.stack([x_at, y_at, core]).astype(jnp.int32)
-    half_width = model_width // 2
     first_mode = (modality == 0)[:, None]
     nothing = jnp.zeros((), low)
     dims = (((0,), (0,)), ((), ()))
@@ -1582,12 +1712,8 @@
                            first_mode.astype(jnp.float32), by_hand)
     gated_b, gate_grad_b, mixed_grad, states, starts = forward[:5]
     if by_hand:
-        masks = [modes[m, :, :1] for m in range(2)]
-        products = [lax.dot_general(gated_b * masks[m], cotan_pair, dims, preferred_element_type=jnp.float32).astype(low)
-                    for m in range(2)]
-        products += [lax.dot_general(normed_pair, gate_grad_b * masks[m], dims, preferred_element_type=jnp.float32).astype(low)
-                     for m in range(2)]
-        partial_out = jnp.dot(forward[5], out_proj.reshape(2 * channels, model_width), preferred_element_type=jnp.float32).astype(low)
+        made = make_products(gated_b, cotan_pair, normed_pair, gate_grad_b, modes, forward[5], out_proj)
+        products, partial_out, normed_t = made[:4], made[4], made[5]
         back = scan_backward(coeffs, step_pre, activated_b, mixed_grad, keep, a_log3, skip_row, states, starts,
                              products, partial_out)
         out_own, gate_own, z_own = back[5:]
@@ -1605,7 +1731,7 @@
         row_facts = jnp.concatenate([inverse[:, :1], first_mode.astype(jnp.float32)], axis=1)
         rows, normed_low, inner_product, out_shared, gate_shared, z_res = middle(
             pre_grad_b, act_part, coeff_grad, conv_sum, inner_x, activated_b, rank_b, dt_proj, x_wide, conv_weight, later, modes,
-            gate_grad_b[:tokens], jnp.swapaxes(normed_pair, 0, 1), row_facts, jnp.concatenate([a_log_grad, skips], axis=0),
+            gate_grad_b, normed_t, row_facts, jnp.concatenate([a_log_grad, skips], axis=0),
             hidden_in, in_gate, in_inner, out_own, gate_own, z_own)
         summed_out = z_res.reshape(tokens, model_width)
     else:
@@ -1638,12 +1764,9 @@
     if by_hand:
         (inner_shared,), (inner_own,), normed_sum = tail_exchange([inner_product], normed_low)
 
-        output, input_grad = finish(hidden_in, out_grad, inverse, norm_gain[None], summed_out, normed_sum)
-        where = tie(where, summed_rows)
-        out_proj_grad = write_out("columns", (2, channels, model_width), where, out_shared, out_own, None)
-        in_shape = (2, model_width, 2, channels)
-        in_proj_grad = write_out(1, in_shape, where, gate_shared, gate_own, None)
-        in_proj_grad = write_out(0, in_shape, where, inner_shared, inner_own, in_proj_grad)
+        out_proj_grad, in_proj_grad, output, input_grad = final(
+            tie(where, summed_rows), out_shared, out_own, gate_shared, gate_own, inner_shared, inner_own,
+            hidden_in, out_grad, inverse, norm_gain[None], summed_out, normed_sum)
     else:
         inner_proj_grad = lax.psum(weight_grads(normed_b, x_grad_b, first_mode).astype(low), "dp")
         in_proj_grad = jnp.stack([inner_proj_grad, gate_proj_grad], axis=2).astype(jnp.float32)

time: 523 us -> 501 us (0.958)
  matrix products: 36.2 us -> 3.91 us
  Pallas kernels: 429 us -> 447 us
  local copies, waits for them, and re-layouts: 29.5 us -> 21.7 us
    dot_general x5 -> x0, matrix products: 33.3 us -> none  [the longest x1 11.8 us: shards(): jnp.dot(forward[5], out_proj.reshape(2 * channels, model_width), preferre...]
    pallas_call x4 -> x2, Pallas kernels: 38.1 us -> 57 us  [the longest x1 29.1 us: make_products(): pl.pallas_call(products_kernel, in_specs=[anywhere] * 7, out_specs=[anywh...]
  transfers between devices with their start and end apart: 1 -> 1, of which waited for: 0 -> 0; matrix products, arithmetic and copies ran while one was open for 0% -> 0% of each run, Pallas kernels for 25% -> 24%
where the time goes in v4:
time: 501 us; the launch traced here: 493 us
  Pallas kernels  447 us (89%)
  local copies, waits for them, and re-layouts  21.7 us (4%)
  between operations  14.8 us (3%)
    pallas_call x1, Pallas kernels, tail_exchange(): pl.pallas_call(functools.partial(tail_kernel, count), in_specs=[anywhere]...  117 us
    pallas_call x1, Pallas kernels, middle(): pl.pallas_call(middle_kernel, in_specs=[vmem] * 16 + [anywhere] * 6, out_...  88 us
    pallas_call x1, Pallas kernels, scan_backward(): pl.pallas_call(functools.partial(scan_backward_kernel, states, groups, ro...  87.4 us
    pallas_call x1, Pallas kernels, front(): pl.pallas_call(functools.partial(front_kernel, coeffs_wide), in_specs=[vm...  66.4 us
    pallas_call x1, Pallas kernels, scan_forward(): pl.pallas_call(functools.partial(scan_forward_kernel, states, groups, row...  31.3 us
    pallas_call x1, Pallas kernels, make_products(): pl.pallas_call(products_kernel, in_specs=[anywhere] * 7, out_specs=[anywh...  29.1 us
    pallas_call x1, Pallas kernels, final(): pl.pallas_call(functools.partial(final_kernel, side, depth), in_specs=[pl...  27.8 us
  transfers between devices with their start and end apart: 1, of which 0 were waited for; matrix products, arithmetic and copies ran while one was open for 0% of the time, Pallas kernels for 24%

profile of v4, /device:TPU:0, one launch (start us, length us, event | category | flops | bytes accessed | tf_op | source)
XLA Modules:
  0.0 492.7 jit_solution(13337226653231041366)
XLA Ops:
  7.2 0.7 fusion.12
  7.9 0.9 fusion.5
  9.5 0.9 copy.61.docs
  10.5 0.8 fusion.14
  11.2 0.9 copy.69
  12.1 2.2 pad.31.x_wide
  14.3 1.0 broadcast_in_dim.63.modes
  15.3 66.4 %front.1 = (bf16[2,2048,1024]{2,1,0:T(8,128)(2,1)}, bf16[2,2048,1024]{2,1,0:T(8,128)(2,1)}, bf16[1536,1024]{1,0:T(8,128)(2,1)}, bf16[1536,1024]{1,0:T(8,128)(2,1...) custom-call(bf16[768,2048]{1,0:T(8,128)(2,1)} %hidden.5, ...), custom_call_target="tpu_custom_call" | custom-call | flops 20000000000 | bytes 80000000 | tf_op jit(solution)/shard_map/front/pallas_call | solution.py:1179
  81.8 1.5 fusion.1
  83.3 2.4 select_add_fusion.pre_ref
  85.7 31.3 %scan_forward.1 = (bf16[1536,1024]{1,0:T(8,128)(2,1)}, bf16[1536,1024]{1,0:T(8,128)(2,1)}, f32[768,1024]{1,0:T(8,128)}, f32[768,16,8,128]{3,2,1,0:T(8,128)}, f32...) custom-call(f32[768,32]{1,0:T(8,128)S(1)} %bitcast.57, f32[768,1024]{1,0:T(8,128)} %select_add_fusion.pre_ref, ...), custom_call_target="tpu_custom_call" | custom-call | tf_op jit(solution)/shard_map/scan_forward/pallas_call | solution.py:133
  117.1 0.9 copy-done.11
  118.0 29.1 %products.1 = (bf16[1024,1024]{1,0:T(8,128)(2,1)}, bf16[1024,1024]{1,0:T(8,128)(2,1)}, bf16[1024,1024]{1,0:T(8,128)(2,1)}, bf16[1024,1024]{1,0:T(8,128)(2,1)}, b...) custom-call(bf16[1536,1024]{1,0:T(8,128)(2,1)} %get-tuple-element.67.gated, ...), custom_call_target="tpu_custom_call" | custom-call | flops 20000000000 | bytes 45000000 | tf_op jit(solution)/shard_map/products/pallas_call | solution.py:1283
  147.1 87.4 %scan_backward.1 = (bf16[768,1024]{1,0:T(8,128)(2,1)}, f32[768,1024]{1,0:T(8,128)}, f32[768,128]{1,0:T(8,128)S(1)}, f32[16,8,128]{2,1,0:T(8,128)S(1)}, f32[1,102...) custom-call(f32[768,32]{1,0:T(8,128)S(1)} %bitcast.58, ...), custom_call_target="tpu_custom_call" | custom-call | flops 754974720 | bytes 50331648 | tf_op jit(solution)/shard_map/scan_backward/pallas_call | solution.py:1550
  234.6 0.9 pad_maximum_fusion.inv
  236.1 0.7 pad_maximum_fusion.1.extra
  236.8 1.1 maximum_bitcast_fusion.docs
  237.9 88.0 %middle.1 = (bf16[608,1024]{1,0:T(8,128)(2,1)}, bf16[768,2048]{1,0:T(8,128)(2,1)}, bf16[2,1024,1024]{2,1,0:T(8,128)(2,1)}, bf16[2,2,4,256,1024]{4,3,2,1,0:T(8,12...) custom-call(bf16[768,1024]{1,0:T(8,128)(2,1)} %get-tuple-element.78., ...), custom_call_target="tpu_custom_call", output_to_operand_aliasing={{5}: (21, {})} | custom-call | flops 27000000512 | bytes 60000000 | tf_op jit(solution)/shard_map/middle/pallas_call | solution.py:928
  326.0 2.2 copy-done.1
  328.2 1.9 copy-done.4
  330.1 117.2 %tail_exchange.1 = (bf16[2,2,4,256,1024]{4,3,2,1,0:T(8,128)(2,1)}, bf16[2,12,32,2048]{3,2,1,0:T(8,128)(2,1)S(1)}, bf16[2,256,1024]{2,1,0:T(8,128)(2,1)S(1)}) custom-call(bf16[2,1024,1024]{2,1,0:T(8,128)(2,1)S(1)} %copy-done.1, bf16[2,12,32,2048]{3,2,1,0:T(8,128)(2,1)S(1)} %bitcast.54), custom_call_target="tpu_custom_call" | custom-call | flops 100000000 | bytes 300000000 | tf_op jit(solution)/shard_map/tail_exchange/pallas_call | solution.py:654
  447.3 1.6 copy-done.6
  449.1 1.7 slice.100
  450.8 1.2 slice_bitcast_fusion
  452.0 1.1 slice.102
  453.4 0.6 copy.74
  454.0 0.5 copy-done.2
  455.1 27.8 %final_rows.1 = (f32[2,1024,2048]{2,1,0:T(8,128)}, f32[2,2048,2,1024]{3,2,1,0:T(2,128)}, bf16[768,2048]{1,0:T(8,128)(2,1)}, bf16[768,2048]{1,0:T(8,128)(2,1)}) custom-call(s32[3]{0:T(128)S(1)} %pad_add_fusion.where_ref, bf16[2,2,4,256,1024]{4,3,2,1,0:T(8,128)(2,1)} %get-tuple-element.94.out_shared, bf16[2,256,1024]{2,1,0:T(8,128)(2,1)S(1)} %copy-done.9, ...), custom_call_target="tpu_custom_call" | custom-call | flops 50000000 | bytes 91000000 | tf_op jit(solution)/shard_map/final_rows/pallas_call | solution.py:1384
  482.9 0.6 slice.104
  483.6 0.6 slice.98
  484.2 0.6 fusion.13
  484.8 0.6 slice.103
  (58 shorter events, 2.3 us)
Async XLA Ops:
  7.2 441.9 %all-reduce.9.cloned.1.call-start = ((), (), s32[]{:S(2)}) async-start(), calls=%async_computation | async-start | bytes 2490368 | tf_op jit(solution)/shard_map/psum | solution.py:1763
  15.3 66.4 %copy-start.17 = (bf16[2,128,1024]{2,1,0:T(8,128)(2,1)S(1)}, bf16[2,128,1024]{2,1,0:T(8,128)(2,1)}, u32[]{:S(2)}) copy-start(bf16[2,128,1024]{2,1,0:T(8,128)(2,1)} %dt_proj.1) | copy-start | bytes 1572868
  81.7 1.6 copy-start.16
  83.3 2.4 copy-start
  83.3 2.4 copy-start.7
  83.3 2.4 copy-start.12
  117.1 0.9 copy-start.11
  147.1 87.5 %copy-start.18 = (f32[16,1024]{1,0:T(8,128)S(1)}, f32[16,1024]{1,0:T(8,128)}, u32[]{:S(2)}) copy-start(f32[16,1024]{1,0:T(8,128)} %param.24) | copy-start | bytes 196612
  147.1 87.5 %copy-start.8 = (f32[768,128]{1,0:T(8,128)S(1)}, f32[768,128]{1,0:T(8,128)}, u32[]{:S(2)}) copy-start(f32[768,128]{1,0:T(8,128)} %get-tuple-element.84.inverse) | copy-start | bytes 1179652
  234.6 3.3 copy-start.14
  326.0 2.2 copy-start.1
  328.2 1.9 copy-start.4
  447.3 1.7 copy-start.6
  449.1 4.0 copy-start.15
  449.1 4.9 %copy-start.5 = (bf16[2,6,64,2048]{3,2,1,0:T(8,128)(2,1)S(1)}, bf16[2,6,64,2048]{3,2,1,0:T(8,128)(2,1)}, u32[]{:S(2)}) copy-start(bf16[2,6,64,2048]{3,2,1,0:T(8,128)(2,1)} %get-tuple-element.100) | copy-start | bytes 9437188
  450.8 3.2 copy-start.3
  452.0 2.6 copy-start.2
  452.0 2.8 copy-start.9
  452.0 3.1 copy-start.10
  452.0 3.1 copy-start.13
Sparse Core Ops, SparseCore 0:
  326.1 67.7 all-reduce.8

commit v5 on v4

--- a/solution.py
+++ b/solution.py
@@ -116,7 +116,7 @@
         ggrad_ref[...] = gate_grad
 
 
-def scan_forward(bc, pre, act, z, gg, keep, a_log3, skip, mode, joined, rows=64, unroll=4):
+def scan_forward(bc, pre, act, z, gg, keep, a_log3, skip, mode, joined, rows=64, unroll=8):
     tokens, channels = pre.shape
     groups = channels // LANES
     states = a_log3.shape[0]
@@ -509,7 +509,7 @@
                     self.copy(half, c).wait_send()
 
 
-AHEAD = 2
+AHEAD = 4
 
 
 class LineSum:
@@ -659,7 +659,7 @@
         + [jax.ShapeDtypeStruct((2, side, depth), low)] * count,
         scratch_shapes=scratch,
         cost_estimate=pl.CostEstimate(flops=100_000_000, bytes_accessed=300_000_000, transcendentals=0),
-        compiler_params=pltpu.CompilerParams(collective_id=1, has_side_effects=True, vmem_limit_bytes=40 * 1024 * 1024),
+        compiler_params=pltpu.CompilerParams(collective_id=1, has_side_effects=True, vmem_limit_bytes=60 * 1024 * 1024),
         name="tail_exchange",
     )(*products, part)
     return outs[:count], outs[count + 1:], outs[count].reshape(tokens, width)
@@ -974,17 +974,18 @@
 
 def front_kernel(coeffs_wide, hidden, gain, conv_w, conv_b, docs, modes, x_wide, out_grad, view, out_proj,
                  w_inner, w_gate, normed_pair, cotan_pair, modes_pair,
-                 normed, inverse, conv_sum, inner_x, act_b, gate_z, gated_grad, rank_out, coeff_out,
-                 acc, view_buf, wide, stage, w_out, proj_buf, proj_recv, proj_fin,
-                 view_sems, stage_sems, out_sems, red_send, red_recv, all_send, all_recv, pair_send, pair_recv, pair_local):
+                 inverse, conv_sum_out, inner_x_out, act_out, gate_z_out, gated_grad, rank_out, coeff_out,
+                 normed, conv_sum, act_b, gate_z, acc, view_a, view_b, wide, stage_a, stage_b, w_out, proj_buf, proj_recv, proj_fin,
+                 view_sems, stage_sems, out_sems, red_send, red_recv, all_send, all_recv, pair_send, pair_recv, pair_local, early_sems):
     tokens, width = hidden.shape
     channels = conv_w.shape[1]
     groups = channels // LANES
     low = jnp.bfloat16
     z = lax.axis_index("tensor")
     share = tokens // 4
-    deep = stage.shape[2] // 2
+    deep = stage_a.shape[1] // 2
     turns = width // deep
+    views, stages = (view_a, view_b), (stage_a, stage_b)
     block = 128
 
     def z_at(off):
@@ -1010,23 +1011,23 @@
                 pltpu.make_async_remote_copy(src_ref=theirs, dst_ref=there, send_sem=pair_send.at[i], recv_sem=pair_recv.at[i],
                                              device_id=to_core, device_id_type=MESH))
 
-    def view_copy(i, m):
+    def view_copy(i, slot, m):
         tall = deep * 2 * groups
-        return pltpu.make_async_copy(view.at[m, pl.ds(pl.multiple_of(i * tall, tall), tall)], view_buf.at[i % 2, m],
-                                     view_sems.at[i % 2, m])
-
-    def stage_copy(i, half, m):
+        return pltpu.make_async_copy(view.at[m, pl.ds(pl.multiple_of(i * tall, tall), tall)], views[slot].at[m],
+                                     view_sems.at[slot, m])
+
+    def stage_copy(i, slot, half, m):
         target = w_inner if half == 0 else w_gate
-        return pltpu.make_async_copy(stage.at[i % 2, half, pl.ds(m * deep, deep)],
-                                     target.at[m, pl.ds(pl.multiple_of(i * deep, deep), deep)], stage_sems.at[i % 2, half, m])
+        return pltpu.make_async_copy(stages[slot].at[half, pl.ds(m * deep, deep)],
+                                     target.at[m, pl.ds(pl.multiple_of(i * deep, deep), deep)], stage_sems.at[slot, half, m])
 
     def out_copy(m):
         return pltpu.make_async_copy(out_proj.at[m], w_out.at[m], out_sems.at[m])
 
+    for slot in range(2):
+        for m in range(2):
+            view_copy(slot, slot, m).start()
     for m in range(2):
-        view_copy(0, m).start()
-    for m in range(2):
-        view_copy(1, m).start()
         out_copy(m).start()
 
     def norm_block(i, nothing):
@@ -1040,58 +1041,69 @@
     lax.fori_loop(0, tokens // block, norm_block, 0)
     acc[0:8, :] = jnp.zeros((8, channels), jnp.float32)
 
-    def unpack(i):
+    def unpack(slot):
         for m in range(2):
-            wide[m] = view_buf[i % 2, m].astype(jnp.float32)
+            wide[m] = views[slot][m].astype(jnp.float32)
             for half in range(2):
-                stage[i % 2, half, m * deep:(m + 1) * deep, :] = jnp.concatenate(
+                stages[slot][half, m * deep:(m + 1) * deep, :] = jnp.concatenate(
                     [wide[m, pl.ds(g * 2 + half, deep, stride=2 * groups), :] for g in range(groups)], axis=1).astype(low)
 
-    def multiply(i, first):
+    def multiply(i, slot, first):
         columns = normed[:, pl.ds(pl.multiple_of(i * deep, deep), deep)]
         left = jnp.concatenate([columns * widened(modes[0], deep), columns * widened(modes[1], deep)], axis=1)
         for half in range(2):
-            product = dot_f32(left, stage[i % 2, half])
+            product = dot_f32(left, stages[slot][half])
             if half == 0:
                 acc[8:8 + tokens, :] = product if first else acc[8:8 + tokens, :] + product
             else:
                 gate_z[...] = product if first else gate_z[...] + product
 
-    def turn(i):
+    def arrive(i, slot):
         for m in range(2):
-            view_copy(i, m).wait()
-        unpack(i)
+            view_copy(i, slot, m).wait()
+
+    def depart(i, slot):
         for m in range(2):
             for half in range(2):
-                stage_copy(i, half, m).start()
-
-    turn(0)
-    multiply(0, True)
-    for m in range(2):
-        view_copy(2, m).start()
-    turn(1)
-    for m in range(2):
-        view_copy(3, m).start()
-
-    def looped(i, nothing):
+                stage_copy(i, slot, half, m).start()
+
+    def departed(i, slot):
         for m in range(2):
             for half in range(2):
-                stage_copy(i, half, m).wait()
-        multiply(i + 1, False)
-        turn(i + 2)
-
-        @pl.when(i + 4 < turns)
-        def _():
-            for m in range(2):
-                view_copy(i + 4, m).start()
+                stage_copy(i, slot, half, m).wait()
+
+    def fetch(i, slot):
+        for m in range(2):
+            view_copy(i, slot, m).start()
+
+    arrive(0, 0)
+    unpack(0)
+    depart(0, 0)
+    fetch(2, 0)
+    arrive(1, 1)
+    multiply(0, 0, True)
+    unpack(1)
+    depart(1, 1)
+    fetch(3, 1)
+
+    def looped(j, nothing):
+        for slot in range(2):
+            i = 2 * j + slot
+            departed(i, slot)
+            arrive(i + 2, slot)
+            multiply(i + 1, 1 - slot, False)
+            unpack(slot)
+            depart(i + 2, slot)
+
+            @pl.when(i + 4 < turns)
+            def _():
+                fetch(i + 4, slot)
         return nothing
 
-    lax.fori_loop(0, turns - 2, looped, 0)
-    multiply(turns - 1, False)
-    for i in (turns - 2, turns - 1):
-        for m in range(2):
-            for half in range(2):
-                stage_copy(i, half, m).wait()
+    lax.fori_loop(0, turns // 2 - 1, looped, 0)
+    multiply(turns - 1, 1, False)
+    departed(turns - 2, 0)
+    departed(turns - 1, 1)
 
     taps = conv_w.shape[0]
 
@@ -1104,7 +1116,6 @@
         for offset in range(1, taps):
             total = total + conv_w[taps - 1 - offset:taps - offset, :] * rows[8 - offset:8 - offset + block, :] * doc[:, offset:offset + 1]
         conv_sum[at, :] = total
-        inner_x[at, :] = rows[8:8 + block, :]
         active = (total * jax.nn.sigmoid(total)).astype(low)
         act_b[at, :] = active
         part = dot_f32(active * widened(modes[0, at, :], channels), x_wide[0], NT)
@@ -1130,6 +1141,10 @@
     pl.semaphore_wait(barrier, 4)
     for off in (1, 2, 3):
         red_copy(off).start()
+    early = [pltpu.make_async_copy(source, target, early_sems.at[i]) for i, (source, target) in enumerate((
+        (conv_sum, conv_sum_out), (acc.at[pl.ds(8, tokens)], inner_x_out), (act_b, act_out), (gate_z, gate_z_out)))]
+    for copy in early:
+        copy.start()
     for i in range(3):
         for copy in pair_copies(i):
             copy.start()
@@ -1165,6 +1180,8 @@
     for i in range(3):
         for copy in pair_copies(i):
             copy.wait()
+    for copy in early:
+        copy.wait()
 
 
 def front(hidden, gain, conv_w, conv_b, docs, modes, x_wide, out_grad, in_proj, out_proj, coeffs_wide):
@@ -1179,24 +1196,26 @@
     return pl.pallas_call(
         functools.partial(front_kernel, coeffs_wide),
         in_specs=[vmem] * 8 + [anywhere] * 2,
-        out_specs=[anywhere] * 5 + [vmem] * 9,
+        out_specs=[anywhere] * 5 + [vmem] + [anywhere] * 4 + [vmem] * 3,
         out_shape=[
             shape((2, width, channels), low), shape((2, width, channels), low), shape((2 * tokens, width // 2), low),
-            shape((2 * tokens, width // 2), low), shape((2, 2 * tokens, LANES), low), shape((tokens, width), low),
+            shape((2 * tokens, width // 2), low), shape((2, 2 * tokens, LANES), low),
             shape((tokens, LANES), f32), shape((tokens, channels), f32), shape((tokens, channels), f32),
             shape((tokens, channels), low), shape((tokens, channels), f32), shape((tokens, channels), f32),
             shape((tokens, LANES), low), shape((tokens, LANES), f32),
         ],
         scratch_shapes=[
+            pltpu.VMEM((tokens, width), low), pltpu.VMEM((tokens, channels), f32), pltpu.VMEM((tokens, channels), low),
+            pltpu.VMEM((tokens, channels), f32),
             pltpu.VMEM((tokens + 8, channels), f32),
-            pltpu.VMEM((2, 2, deep * 2 * groups, LANES), low),
+            pltpu.VMEM((2, deep * 2 * groups, LANES), low), pltpu.VMEM((2, deep * 2 * groups, LANES), low),
             pltpu.VMEM((2, deep * 2 * groups, LANES), f32),
-            pltpu.VMEM((2, 2, 2 * deep, channels), low),
+            pltpu.VMEM((2, 2 * deep, channels), low), pltpu.VMEM((2, 2 * deep, channels), low),
             pltpu.VMEM((2, channels, width), low),
             pltpu.VMEM((tokens, 2 * LANES), low),
             pltpu.VMEM((3, tokens // 4, 2 * LANES), low),
             pltpu.VMEM((tokens, 2 * LANES), low),
-            DMA((2, 2)), DMA((2, 2, 2)), DMA((2,)), DMA((3,)), DMA((3,)), DMA((3,)), DMA((3,)), DMA((3,)), DMA((3,)), DMA((3,)),
+            DMA((2, 2)), DMA((2, 2, 2)), DMA((2,)), DMA((3,)), DMA((3,)), DMA((3,)), DMA((3,)), DMA((3,)), DMA((3,)), DMA((3,)), DMA((4,)),
         ],
         cost_estimate=pl.CostEstimate(flops=20_000_000_000, bytes_accessed=80_000_000, transcendentals=1_000_000),
         compiler_params=pltpu.CompilerParams(collective_id=4, has_side_effects=True, vmem_limit_bytes=60 * 1024 * 1024),
@@ -1293,15 +1312,15 @@
             DMA((6,)), DMA((2,)), DMA((2,)), DMA((2,)), DMA,
         ],
         cost_estimate=pl.CostEstimate(flops=20_000_000_000, bytes_accessed=45_000_000, transcendentals=0),
-        compiler_params=pltpu.CompilerParams(vmem_limit_bytes=56 * 1024 * 1024),
+        compiler_params=pltpu.CompilerParams(vmem_limit_bytes=60 * 1024 * 1024),
         name="products",
     )(gated, cotan, normed, gate, modes, split, weights)
 
 
 def final_kernel(side, depth, where_ref, out_shared, out_own, gate_shared, gate_own, inner_shared, inner_own,
-                 hidden, out_grad, inverse, gain, summed_out, normed_sum,
-                 out_ref, in_ref, output, input_grad,
-                 narrow, wide, row_in, row_out, in_sems, out_sems, row_in_sems, row_out_sems):
+                 hidden, out_grad, inverse, gain, summed_rows, summed_out, normed_sum,
+                 out_ref, in_ref, output, input_grad, x_grad, dt_grad, *rest):
+    row_grads, (narrow, wide, row_in, row_out, in_sems, out_sems, row_in_sems, row_out_sems) = rest[:-8], rest[-8:]
     x, y, core = where_ref[0], where_ref[1], where_ref[2]
     low, f32 = jnp.bfloat16, jnp.float32
     block = row_in.shape[2]
@@ -1340,6 +1359,16 @@
         copy.start()
     for i in range(slots):
         loads[i].start()
+    span, rank_dim = x_grad.shape[1], dt_grad.shape[1]
+    for m in range(2):
+        base = m * (span + rank_dim)
+        x_grad[m] = summed_rows[base:base + span, :].astype(f32)
+        dt_grad[m] = summed_rows[base + span:base + span + rank_dim, :].astype(f32)
+    tail_rows = summed_rows[2 * (span + rank_dim):, :].astype(f32)
+    at = 0
+    for ref in row_grads:
+        ref[...] = tail_rows[at:at + ref.shape[0], :]
+        at += ref.shape[0]
     per = -(-len(jobs) // count)
     for i in range(count):
         for copy in row_loads(i):
@@ -1374,7 +1403,7 @@
 
 
 def final(where, out_shared, out_own, gate_shared, gate_own, inner_shared, inner_own, hidden, out_grad, inverse, gain,
-          summed_out, normed_sum):
+          summed_rows, rank_dim, row_counts, summed_out, normed_sum):
     side, depth = out_own.shape[1:]
     tokens, width = hidden.shape
     channels = 4 * side
@@ -1383,22 +1412,24 @@
     block, slots = 128, 6
     return pl.pallas_call(
         functools.partial(final_kernel, side, depth),
-        in_specs=[pl.BlockSpec(memory_space=pltpu.SMEM)] + [anywhere] * 8 + [vmem] * 2 + [anywhere] * 2,
-        out_specs=[anywhere] * 4,
+        in_specs=[pl.BlockSpec(memory_space=pltpu.SMEM)] + [anywhere] * 8 + [vmem] * 3 + [anywhere] * 2,
+        out_specs=[anywhere] * 4 + [vmem] * (2 + len(row_counts)),
         out_shape=[
             jax.ShapeDtypeStruct((2, channels, width), f32), jax.ShapeDtypeStruct((2, width, 2, channels), f32),
             jax.ShapeDtypeStruct((tokens, width), low), jax.ShapeDtypeStruct((tokens, width), low),
-        ],
+            jax.ShapeDtypeStruct((2, (summed_rows.shape[0] - 32) // 2 - rank_dim, channels), f32),
+            jax.ShapeDtypeStruct((2, rank_dim, channels), f32),
+        ] + [jax.ShapeDtypeStruct((n, channels), f32) for n in row_counts],
         scratch_shapes=[
             pltpu.VMEM((slots, side, depth), low), pltpu.VMEM((slots, side, depth), f32),
             pltpu.VMEM((2, 4, block, width), low), pltpu.VMEM((2, 2, block, width), low),
             DMA((slots,)), DMA((slots,)), DMA((2, 4)), DMA((2, 2)),
         ],
         cost_estimate=pl.CostEstimate(flops=50_000_000, bytes_accessed=91_000_000, transcendentals=0),
-        compiler_params=pltpu.CompilerParams(vmem_limit_bytes=40 * 1024 * 1024),
+        compiler_params=pltpu.CompilerParams(vmem_limit_bytes=60 * 1024 * 1024),
         name="final_rows",
     )(where, out_shared, out_own, gate_shared, gate_own, inner_shared, inner_own, hidden, out_grad, inverse, gain,
-      summed_out, normed_sum)
+      summed_rows, summed_out, normed_sum)
 
 
 def scan_backward_kernel(states, groups, rows, unroll, count, joined,
@@ -1527,7 +1558,7 @@
             line.done()
 
 
-def scan_backward(bc, pre, act, mixed, keep, a_log3, skip, h, starts, products=None, z_part=None, rows=64, unroll=3, pieces=6):
+def scan_backward(bc, pre, act, mixed, keep, a_log3, skip, h, starts, products=None, z_part=None, rows=64, unroll=7, pieces=6):
     tokens, channels = pre.shape
     groups = channels // LANES
     states = a_log3.shape[0]
@@ -1684,7 +1715,7 @@
         modes_own = jnp.broadcast_to(jnp.stack([first_mode, jnp.logical_not(first_mode)]), (2, tokens, LANES)).astype(low)
         x_wide = jnp.pad(jnp.swapaxes(x_proj, 1, 2), ((0, 0), (0, 96), (0, 0)))
         facts = jnp.concatenate([first_mode.astype(jnp.float32)] + same_doc[1:], axis=1)
-        (in_inner, in_gate, normed_pair, cotan_pair, modes, _, inverse, conv_sum, inner_x, activated_b, gate_z, gated_grad, rank_b, coeffs) = front(
+        (in_inner, in_gate, normed_pair, cotan_pair, modes, inverse, conv_sum, inner_x, activated_b, gate_z, gated_grad, rank_b, coeffs) = front(
             hidden_in, norm_gain[None], conv_weight, conv_bias[None], facts, modes_own, x_wide, out_grad, in_proj, out_proj,
             2 * state_dim)
         coeffs = coeffs[:, :2 * state_dim]
@@ -1764,9 +1795,13 @@
     if by_hand:
         (inner_shared,), (inner_own,), normed_sum = tail_exchange([inner_product], normed_low)
 
-        out_proj_grad, in_proj_grad, output, input_grad = final(
-            tie(where, summed_rows), out_shared, out_own, gate_shared, gate_own, inner_shared, inner_own,
-            hidden_in, out_grad, inverse, norm_gain[None], summed_out, normed_sum)
+        (out_proj_grad, in_proj_grad, output, input_grad, x_rows, dt_proj_grad, conv_weight_grad, conv_row, dt_bias_grad,
+         a_log_grad, skip_row, gain_rows) = final(
+            where, out_shared, out_own, gate_shared, gate_own, inner_shared, inner_own,
+            hidden_in, out_grad, inverse, norm_gain[None], summed_rows, rank_dim, (conv_taps, 1, 2, state_dim, 1, model_width // channels),
+            summed_out, normed_sum)
+        x_proj_grad = jnp.swapaxes(x_rows, 1, 2)
+        conv_bias_grad, skip_grad, norm_gain_grad = conv_row[0], skip_row[0], gain_rows.reshape(-1)
     else:
         inner_proj_grad = lax.psum(weight_grads(normed_b, x_grad_b, first_mode).astype(low), "dp")
         in_proj_grad = jnp.stack([inner_proj_grad, gate_proj_grad], axis=2).astype(jnp.float32)
@@ -1774,14 +1809,16 @@
         output = (hidden + summed_out.astype(jnp.float32)).astype(low)
         cotan = out_grad.astype(jnp.float32)
         input_grad, _ = finish_rows(normed_sum.astype(jnp.float32), hidden, inverse, cotan, norm_gain)
-    summed_rows = summed_rows.astype(jnp.float32)
-    small_modes, rows = summed_rows[:2 * mode_rows].reshape(2, mode_rows, channels), summed_rows[2 * mode_rows:]
-    x_proj_grad = jnp.swapaxes(small_modes[:, :-rank_dim], 1, 2)
-    dt_proj_grad = small_modes[:, -rank_dim:]
-    norm_gain_grad = rows[conv_taps + 4 + state_dim:].reshape(-1)[:model_width]
-    at = conv_taps + 1
-    return (output, input_grad, norm_gain_grad, in_proj_grad, rows[:conv_taps], rows[conv_taps], x_proj_grad,
-            dt_proj_grad, rows[at:at + 2], rows[at + 2:at + 2 + state_dim], rows[at + 2 + state_dim], out_proj_grad)
+        summed_rows = summed_rows.astype(jnp.float32)
+        small_modes, rows = summed_rows[:2 * mode_rows].reshape(2, mode_rows, channels), summed_rows[2 * mode_rows:]
+        x_proj_grad = jnp.swapaxes(small_modes[:, :-rank_dim], 1, 2)
+        dt_proj_grad = small_modes[:, -rank_dim:]
+        norm_gain_grad = rows[conv_taps + 4 + state_dim:].reshape(-1)[:model_width]
+        at = conv_taps + 1
+        conv_weight_grad, conv_bias_grad, dt_bias_grad = rows[:conv_taps], rows[conv_taps], rows[at:at + 2]
+        a_log_grad, skip_grad = rows[at + 2:at + 2 + state_dim], rows[at + 2 + state_dim]
+    return (output, input_grad, norm_gain_grad, in_proj_grad, conv_weight_grad, conv_bias_grad, x_proj_grad,
+            dt_proj_grad, dt_bias_grad, a_log_grad, skip_grad, out_proj_grad)
 
 
 def solution(mesh):

time: 501 us -> 488 us (0.974)
  local copies, waits for them, and re-layouts: 21.7 us -> 9.9 us
    pallas_call x1, Pallas kernels: 27.8 us -> 33.9 us  [final(): pl.pallas_call(functools.partial(final_kernel, side, depth), in_specs=[pl...]
    unnamed x41 -> x20, local copies, waits for them, and re-layouts: 9.19 us -> 3.8 us
    slice x6 -> x0, local copies, waits for them, and re-layouts: 5.23 us -> none  [the longest x1 1.69 us: shards(): summed_rows[:2 * mode_rows].reshape(2, mode_rows, channels)]
where the time goes in v5:
time: 488 us; the launch traced here: 482 us
  Pallas kernels  449 us (92%)
  between operations  14.8 us (3%)
  local copies, waits for them, and re-layouts  9.9 us (2%)
  other arithmetic  4.93 us (1%)
    pallas_call x1, Pallas kernels, tail_exchange(): pl.pallas_call(functools.partial(tail_kernel, count), in_specs=[anywhere]...  117 us
    pallas_call x1, Pallas kernels, middle(): pl.pallas_call(middle_kernel, in_specs=[vmem] * 16 + [anywhere] * 6, out_...  88.9 us
    pallas_call x1, Pallas kernels, scan_backward(): pl.pallas_call(functools.partial(scan_backward_kernel, states, groups, ro...  86.5 us
    pallas_call x1, Pallas kernels, front(): pl.pallas_call(functools.partial(front_kernel, coeffs_wide), in_specs=[vm...  63 us
    pallas_call x1, Pallas kernels, final(): pl.pallas_call(functools.partial(final_kernel, side, depth), in_specs=[pl...  33.9 us
    pallas_call x1, Pallas kernels, scan_forward(): pl.pallas_call(functools.partial(scan_forward_kernel, states, groups, row...  30.7 us
    pallas_call x1, Pallas kernels, make_products(): pl.pallas_call(products_kernel, in_specs=[anywhere] * 7, out_specs=[anywh...  28.9 us
  transfers between devices with their start and end apart: 1, of which 0 were waited for; matrix products, arithmetic and copies ran while one was open for 0% of the time, Pallas kernels for 24%

profile of v5, /device:TPU:0, one launch (start us, length us, event | category | flops | bytes accessed | tf_op | source)
XLA Modules:
  0.0 482.5 jit_solution(16662820209085344649)
XLA Ops:
  7.2 0.0 all-reduce.9.cloned.1.call-start
  7.2 0.7 fusion.12
  7.9 0.9 fusion.5
  8.8 0.2 copy.62.keep_ref
  9.0 0.1 fusion.8
  9.1 0.2 copy.63.mode_ref
  9.3 0.1 fusion.9
  9.4 0.1 fusion.10
  9.5 0.9 copy.61.docs
  10.5 0.8 fusion.13
  11.2 0.9 copy.69
  12.1 2.2 pad.31.x_wide
  14.3 1.0 broadcast_in_dim.63.modes
  15.3 63.0 %front.1 = (bf16[2,2048,1024]{2,1,0:T(8,128)(2,1)}, bf16[2,2048,1024]{2,1,0:T(8,128)(2,1)}, bf16[1536,1024]{1,0:T(8,128)(2,1)}, bf16[1536,1024]{1,0:T(8,128)(2,1...) custom-call(bf16[768,2048]{1,0:T(8,128)(2,1)} %hidden.5, ...), custom_call_target="tpu_custom_call" | custom-call | flops 20000000000 | bytes 80000000 | tf_op jit(solution)/shard_map/front/pallas_call | solution.py:1196
  78.4 1.5 fusion.1
  80.0 2.4 select_add_fusion.pre_ref
  82.4 30.7 %scan_forward.1 = (bf16[1536,1024]{1,0:T(8,128)(2,1)}, bf16[1536,1024]{1,0:T(8,128)(2,1)}, f32[768,1024]{1,0:T(8,128)}, f32[768,16,8,128]{3,2,1,0:T(8,128)}, f32...) custom-call(f32[768,32]{1,0:T(8,128)S(1)} %bitcast.51, f32[768,1024]{1,0:T(8,128)} %select_add_fusion.pre_ref, ...), custom_call_target="tpu_custom_call" | custom-call | tf_op jit(solution)/shard_map/scan_forward/pallas_call | solution.py:133
  113.1 0.9 copy-done.2
  114.0 28.9 %products.1 = (bf16[1024,1024]{1,0:T(8,128)(2,1)}, bf16[1024,1024]{1,0:T(8,128)(2,1)}, bf16[1024,1024]{1,0:T(8,128)(2,1)}, bf16[1024,1024]{1,0:T(8,128)(2,1)}, b...) custom-call(bf16[1536,1024]{1,0:T(8,128)(2,1)} %get-tuple-element.74.gated, ...), custom_call_target="tpu_custom_call" | custom-call | flops 20000000000 | bytes 45000000 | tf_op jit(solution)/shard_map/products/pallas_call | solution.py:1302
  142.9 86.5 %scan_backward.1 = (bf16[768,1024]{1,0:T(8,128)(2,1)}, f32[768,1024]{1,0:T(8,128)}, f32[768,128]{1,0:T(8,128)S(1)}, f32[16,8,128]{2,1,0:T(8,128)S(1)}, f32[1,102...) custom-call(f32[768,32]{1,0:T(8,128)S(1)} %bitcast.52, ...), custom_call_target="tpu_custom_call" | custom-call | flops 754974720 | bytes 50331648 | tf_op jit(solution)/shard_map/scan_backward/pallas_call | solution.py:1581
  229.5 0.7 copy-done.4
  230.2 0.9 pad_maximum_fusion.inv
  231.1 0.2 copy.65
  231.3 0.2 copy.66
  231.5 0.2 copy.67
  231.7 0.7 pad_maximum_fusion.1.extra
  232.4 1.1 maximum_bitcast_fusion.docs
  233.5 88.9 %middle.1 = (bf16[608,1024]{1,0:T(8,128)(2,1)}, bf16[768,2048]{1,0:T(8,128)(2,1)}, bf16[2,1024,1024]{2,1,0:T(8,128)(2,1)}, bf16[2,2,4,256,1024]{4,3,2,1,0:T(8,12...) custom-call(bf16[768,1024]{1,0:T(8,128)(2,1)} %get-tuple-element.85., ...), custom_call_target="tpu_custom_call", output_to_operand_aliasing={{5}: (21, {})} | custom-call | flops 27000000512 | bytes 60000000 | tf_op jit(solution)/shard_map/middle/pallas_call | solution.py:928
  322.5 116.9 %tail_exchange.1 = (bf16[2,2,4,256,1024]{4,3,2,1,0:T(8,128)(2,1)}, bf16[2,12,32,2048]{3,2,1,0:T(8,128)(2,1)}, bf16[2,256,1024]{2,1,0:T(8,128)(2,1)}) custom-call(bf16[2,1024,1024]{2,1,0:T(8,128)(2,1)} %get-tuple-element.101.refs_0_, bf16[2,12,32,2048]{3,2,1,0:T(8,128)(2,1)} %bitcast.58), custom_call_target="tpu_custom_call" | custom-call | flops 100000000 | bytes 300000000 | tf_op jit(solution)/shard_map/tail_exchange/pallas_call | solution.py:654
  439.5 0.6 pad_add_fusion.where_ref
  440.0 33.9 %final_rows.1 = (f32[2,1024,2048]{2,1,0:T(8,128)}, f32[2,2048,2,1024]{3,2,1,0:T(2,128)}, bf16[768,2048]{1,0:T(8,128)(2,1)}, bf16[768,2048]{1,0:T(8,128)(2,1)}, f...) custom-call(s32[3]{0:T(128)} %pad_add_fusion.where_ref, ...), custom_call_target="tpu_custom_call" | custom-call | flops 50000000 | bytes 91000000 | tf_op jit(solution)/shard_map/final_rows/pallas_call | solution.py:1413
  473.9 1.3 copy.74
  (29 shorter events, 0.2 us)
Async XLA Ops:
  7.2 432.9 %all-reduce.9.cloned.1.call-start = ((), (), s32[]{:S(2)}) async-start(), calls=%async_computation | async-start | bytes 2490368 | tf_op jit(solution)/shard_map/psum | solution.py:1794
  15.3 63.1 %copy-start.7 = (bf16[2,128,1024]{2,1,0:T(8,128)(2,1)S(1)}, bf16[2,128,1024]{2,1,0:T(8,128)(2,1)}, u32[]{:S(2)}) copy-start(bf16[2,128,1024]{2,1,0:T(8,128)(2,1)} %dt_proj.1) | copy-start | bytes 1572868
  78.4 1.6 copy-start.6
  79.9 2.4 copy-start
  79.9 2.4 copy-start.1
  80.0 2.4 copy-start.3
  113.1 0.9 copy-start.2
  142.9 87.3 %copy-start.8 = (f32[16,1024]{1,0:T(8,128)S(1)}, f32[16,1024]{1,0:T(8,128)}, u32[]{:S(2)}) copy-start(f32[16,1024]{1,0:T(8,128)} %param.24) | copy-start | bytes 196612
  142.9 87.3 %copy-start.5 = (f32[768,128]{1,0:T(8,128)S(1)}, f32[768,128]{1,0:T(8,128)}, u32[]{:S(2)}) copy-start(f32[768,128]{1,0:T(8,128)} %get-tuple-element.91.inverse) | copy-start | bytes 1179652
  229.4 0.7 copy-start.4
Sparse Core Ops, SparseCore 0:
  322.6 67.9 all-reduce.8

commit v6 on v5

--- a/solution.py
+++ b/solution.py
@@ -31,10 +31,13 @@
 
 def scan_forward_kernel(states, groups, rows, unroll, count, joined,
                         bc_ref, pre_ref, act_ref, z_ref, gg_ref, keep_ref, alog_ref, skip_ref, mode_ref,
-                        gated_ref, ggrad_ref, mixed_ref, h_ref, start_ref, *rest):
+                        *rest):
     chunk = pl.program_id(0)
     if joined:
-        split_ref, rate_scr, state_scr, sk_scr, u_scr, y_scr, gated_all, ggrad_all, send_sems, recv_sems, local_sems = rest
+        dt_ref, dt_bias_ref, rest = rest[0], rest[1], rest[2:]
+    gated_ref, ggrad_ref, mixed_ref, h_ref, start_ref, *rest = rest
+    if joined:
+        pre_out, split_ref, rate_scr, state_scr, sk_scr, u_scr, y_scr, gated_all, ggrad_all, send_sems, recv_sems, local_sems = rest
         tokens = rows * count
         to_core = place()[4]
 
@@ -59,7 +62,16 @@
         rate_scr[...] = jnp.exp(alog_ref[...]) * (-LOG2E)
         state_scr[...] = jnp.zeros_like(state_scr)
 
-    step = softplus(pre_ref[...])
+    if joined:
+        ranks, first = pre_ref[...], mode_ref[...]
+        ranks_0 = (ranks.astype(jnp.float32) * first).astype(ranks.dtype)
+        pre = (jnp.dot(ranks_0, dt_ref[0], preferred_element_type=jnp.float32)
+               + jnp.dot(ranks - ranks_0, dt_ref[1], preferred_element_type=jnp.float32))
+        pre = pre + (first * dt_bias_ref[0:1, :] + (1.0 - first) * dt_bias_ref[1:2, :])
+        pre_out[...] = pre
+    else:
+        pre = pre_ref[...]
+    step = softplus(pre)
     act = act_ref[...].astype(jnp.float32)
     spread_rows(u_scr, step * act, groups)
     spread_rows(sk_scr, jnp.where(keep_ref[...] > 0.0, step, BIG), groups)
@@ -116,8 +128,8 @@
         ggrad_ref[...] = gate_grad
 
 
-def scan_forward(bc, pre, act, z, gg, keep, a_log3, skip, mode, joined, rows=64, unroll=8):
-    tokens, channels = pre.shape
+def scan_forward(bc, pre, act, z, gg, keep, a_log3, skip, mode, joined, dt=(), rows=64, unroll=8):
+    tokens, channels = act.shape
     groups = channels // LANES
     states = a_log3.shape[0]
     count = tokens // rows
@@ -135,28 +147,28 @@
         grid=(count,),
         in_specs=[
             pl.BlockSpec((rows, 2 * states), lambda i: (i, 0), memory_space=pltpu.SMEM),
-            wide, wide, wide, wide, thin, whole3,
+            pl.BlockSpec((rows, pre.shape[1]), lambda i: (i, 0)), wide, wide, wide, thin, whole3,
             pl.BlockSpec((1, channels), lambda i: (0, 0)), thin,
-        ],
+        ] + [pl.BlockSpec(v.shape, lambda i, n=v.ndim: (0,) * n) for v in dt],
         out_specs=[
             anywhere if joined else wide, anywhere if joined else wide, wide,
             pl.BlockSpec((rows, states, groups, LANES), lambda i: (i, 0, 0, 0)),
             pl.BlockSpec((1, states, groups, LANES), lambda i: (i, 0, 0, 0)),
-        ] + ([pl.BlockSpec((rows, 2 * channels), lambda i: (i, 0))] if joined else []),
+        ] + ([wide, pl.BlockSpec((rows, 2 * channels), lambda i: (i, 0))] if joined else []),
         out_shape=[
             jax.ShapeDtypeStruct((tall, channels), low),
             jax.ShapeDtypeStruct((tall, channels), low),
             jax.ShapeDtypeStruct((tokens, channels), f32),
             jax.ShapeDtypeStruct((tokens, states, groups, LANES), f32),
             jax.ShapeDtypeStruct((count, states, groups, LANES), f32),
-        ] + ([jax.ShapeDtypeStruct((tokens, 2 * channels), low)] if joined else []),
+        ] + ([jax.ShapeDtypeStruct((tokens, channels), f32), jax.ShapeDtypeStruct((tokens, 2 * channels), low)] if joined else []),
         scratch_shapes=[small(), small(), long(), long(), long()] + ([
             pltpu.VMEM((tokens, channels), low), pltpu.VMEM((tokens, channels), low),
             pltpu.SemaphoreType.DMA((count, 2)), pltpu.SemaphoreType.DMA((count, 2)), pltpu.SemaphoreType.DMA((count, 2)),
         ] if joined else []),
         compiler_params=pltpu.CompilerParams(vmem_limit_bytes=48 * 1024 * 1024, **settings),
         name="scan_forward",
-    )(bc, pre, act, z, gg, keep, a_log3, skip, mode)
+    )(bc, pre, act, z, gg, keep, a_log3, skip, mode, *dt)
 
 
 MESH = pl.DeviceIdType.MESH
@@ -519,7 +531,7 @@
         self.z = lax.axis_index("tensor")
         self.near = jnp.where(self.z < 2, 1, 0)
         self.pieces, self.rows = acc.shape[1], acc.shape[2]
-        self.turns = 2 * self.pieces + 2
+        self.turns = self.pieces + 8
 
     @staticmethod
     def scratch(pieces, rows, width):
@@ -588,11 +600,10 @@
             self.reduce_step(turn, near)
         if 1 <= turn <= self.pieces:
             self.reduce_step(turn - 1, far)
-        back = turn - self.pieces
-        if 0 <= back < self.pieces:
-            self.back_step(back, far)
-        if 1 <= back <= self.pieces:
-            self.back_step(back - 1, near)
+        if 0 <= turn - 6 < self.pieces:
+            self.back_step(turn - 6, far)
+        if 0 <= turn - 8 < self.pieces:
+            self.back_step(turn - 8, near)
 
     def finish(self):
         for half in range(2):
@@ -631,7 +642,7 @@
     line.load().wait()
     line.begin(range(AHEAD))
     last = line.turns
-    plan = {3: [(0, 1)], 5: [(0, 2)], 9: [(0, 3)], 13: [(0, 4)], 17: [(0, 5)], 21: [(0, 6)]}
+    plan = {4: [(0, 1)], 7: [(0, 2)], 10: [(0, 3)], 12: [(0, 4)], 15: [(0, 5)], 19: [(0, 6)]}
     for turn in range(last):
         line.turn(turn)
         for which, number in plan.get(turn, []):
@@ -1735,15 +1746,19 @@
         coeffs = projected[:, rank_dim:]
         gate_z = pick_dot(normed_b, in_gate, first_mode)
         gated_grad = pick_back(out_grad, out_proj, first_mode)
-    step_pre = pick_dot(rank_b, dt_proj, first_mode) + jnp.where(first_mode, dt_bias[0], dt_bias[1])
+    step_pre, dt = rank_b, (dt_proj, dt_bias)
+    if not by_hand:
+        step_pre = pick_dot(rank_b, dt_proj, first_mode) + jnp.where(first_mode, dt_bias[0], dt_bias[1])
+        dt = ()
     keep = same_doc[1]
     a_log3 = a_log.reshape(state_dim, groups, LANES)
     skip_row = skip_gain[None]
     forward = scan_forward(coeffs, step_pre, activated_b, gate_z, gated_grad, keep, a_log3, skip_row,
-                           first_mode.astype(jnp.float32), by_hand)
+                           first_mode.astype(jnp.float32), by_hand, dt)
     gated_b, gate_grad_b, mixed_grad, states, starts = forward[:5]
     if by_hand:
-        made = make_products(gated_b, cotan_pair, normed_pair, gate_grad_b, modes, forward[5], out_proj)
+        step_pre = forward[5]
+        made = make_products(gated_b, cotan_pair, normed_pair, gate_grad_b, modes, forward[6], out_proj)
         products, partial_out, normed_t = made[:4], made[4], made[5]
         back = scan_backward(coeffs, step_pre, activated_b, mixed_grad, keep, a_log3, skip_row, states, starts,
                              products, partial_out)

time: 488 us -> 477 us (0.977)
  Pallas kernels: 449 us -> 439 us
    pallas_call x1, Pallas kernels: 117 us -> 105 us  [tail_exchange(): pl.pallas_call(functools.partial(tail_kernel, count), in_specs=[anywhere]...]
  transfers between devices with their start and end apart: 1 -> 1, of which waited for: 0 -> 0; matrix products, arithmetic and copies ran while one was open for 0% -> 0% of each run, Pallas kernels for 24% -> 22%
where the time goes in v6:
time: 477 us; the launch traced here: 472 us
  Pallas kernels  439 us (92%)
  between operations  14.7 us (3%)
  local copies, waits for them, and re-layouts  12.4 us (3%)
  other arithmetic  4.98 us (1%)
    pallas_call x1, Pallas kernels, tail_exchange(): pl.pallas_call(functools.partial(tail_kernel, count), in_specs=[anywhere]...  105 us
    pallas_call x1, Pallas kernels, middle(): pl.pallas_call(middle_kernel, in_specs=[vmem] * 16 + [anywhere] * 6, out_...  88.9 us
    pallas_call x1, Pallas kernels, scan_backward(): pl.pallas_call(functools.partial(scan_backward_kernel, states, groups, ro...  86.4 us
    pallas_call x1, Pallas kernels, front(): pl.pallas_call(functools.partial(front_kernel, coeffs_wide), in_specs=[vm...  63.1 us
    pallas_call x1, Pallas kernels, final(): pl.pallas_call(functools.partial(final_kernel, side, depth), in_specs=[pl...  33.9 us
    pallas_call x1, Pallas kernels, scan_forward(): pl.pallas_call(functools.partial(scan_forward_kernel, states, groups, row...  33.1 us
    pallas_call x1, Pallas kernels, make_products(): pl.pallas_call(products_kernel, in_specs=[anywhere] * 7, out_specs=[anywh...  29.1 us
  transfers between devices with their start and end apart: 1, of which 0 were waited for; matrix products, arithmetic and copies ran while one was open for 0% of the time, Pallas kernels for 22%

profile of v6, /device:TPU:0, one launch (start us, length us, event | category | flops | bytes accessed | tf_op | source)
XLA Modules:
  0.0 471.6 jit_solution(12475662923287953512)
XLA Ops:
  7.2 0.0 all-reduce.9.cloned.1.call-start
  7.2 0.7 fusion.7
  7.9 0.9 fusion
  8.8 0.2 copy.62.keep_ref
  9.0 0.1 fusion.3
  9.1 0.2 copy.63.mode_ref
  9.3 0.1 fusion.4
  9.4 0.1 fusion.5
  9.5 0.9 copy.61.docs
  10.5 0.9 copy.69
  11.3 2.2 pad.31.x_wide
  13.5 1.0 broadcast_in_dim.41.modes
  14.5 63.1 %front.1 = (bf16[2,2048,1024]{2,1,0:T(8,128)(2,1)}, bf16[2,2048,1024]{2,1,0:T(8,128)(2,1)}, bf16[1536,1024]{1,0:T(8,128)(2,1)}, bf16[1536,1024]{1,0:T(8,128)(2,1...) custom-call(bf16[768,2048]{1,0:T(8,128)(2,1)} %hidden.5, ...), custom_call_target="tpu_custom_call" | custom-call | flops 20000000000 | bytes 80000000 | tf_op jit(solution)/shard_map/front/pallas_call | solution.py:1207
  77.7 1.4 copy-done
  79.1 1.0 copy-done.1
  80.1 0.9 copy-done.5
  81.0 33.1 %scan_forward.1 = (bf16[1536,1024]{1,0:T(8,128)(2,1)}, bf16[1536,1024]{1,0:T(8,128)(2,1)}, f32[768,1024]{1,0:T(8,128)}, f32[768,16,8,128]{3,2,1,0:T(8,128)}, f32...) custom-call(f32[768,32]{1,0:T(8,128)S(1)} %bitcast.41, ...), custom_call_target="tpu_custom_call" | custom-call | tf_op jit(solution)/shard_map/scan_forward/pallas_call | solution.py:145
  114.2 0.9 copy-done.3
  115.0 29.1 %products.1 = (bf16[1024,1024]{1,0:T(8,128)(2,1)}, bf16[1024,1024]{1,0:T(8,128)(2,1)}, bf16[1024,1024]{1,0:T(8,128)(2,1)}, bf16[1024,1024]{1,0:T(8,128)(2,1)}, b...) custom-call(bf16[1536,1024]{1,0:T(8,128)(2,1)} %get-tuple-element.76.gated, ...), custom_call_target="tpu_custom_call" | custom-call | flops 20000000000 | bytes 45000000 | tf_op jit(solution)/shard_map/products/pallas_call | solution.py:1313
  144.1 86.4 %scan_backward.1 = (bf16[768,1024]{1,0:T(8,128)(2,1)}, f32[768,1024]{1,0:T(8,128)}, f32[768,128]{1,0:T(8,128)S(1)}, f32[16,8,128]{2,1,0:T(8,128)S(1)}, f32[1,102...) custom-call(f32[768,32]{1,0:T(8,128)S(1)} %bitcast.42, ...), custom_call_target="tpu_custom_call" | custom-call | flops 754974720 | bytes 50331648 | tf_op jit(solution)/shard_map/scan_backward/pallas_call | solution.py:1592
  230.5 0.7 copy-done.8
  231.3 0.9 pad_maximum_fusion.inv
  232.2 0.2 copy.65
  232.4 0.2 copy.66
  232.6 0.2 copy.67
  232.8 0.7 pad_maximum_fusion.1.extra
  233.4 1.1 maximum_bitcast_fusion.docs
  234.6 88.9 %middle.1 = (bf16[608,1024]{1,0:T(8,128)(2,1)}, bf16[768,2048]{1,0:T(8,128)(2,1)}, bf16[2,1024,1024]{2,1,0:T(8,128)(2,1)}, bf16[2,2,4,256,1024]{4,3,2,1,0:T(8,12...) custom-call(bf16[768,1024]{1,0:T(8,128)(2,1)} %get-tuple-element.87., ...), custom_call_target="tpu_custom_call", output_to_operand_aliasing={{5}: (21, {})} | custom-call | flops 27000000512 | bytes 60000000 | tf_op jit(solution)/shard_map/middle/pallas_call | solution.py:939
  323.5 105.0 %tail_exchange.1 = (bf16[2,2,4,256,1024]{4,3,2,1,0:T(8,128)(2,1)}, bf16[2,12,32,2048]{3,2,1,0:T(8,128)(2,1)}, bf16[2,256,1024]{2,1,0:T(8,128)(2,1)}) custom-call(bf16[2,1024,1024]{2,1,0:T(8,128)(2,1)} %get-tuple-element.103.refs_0_, bf16[2,12,32,2048]{3,2,1,0:T(8,128)(2,1)} %bitcast.48), custom_call_target="tpu_custom_call" | custom-call | flops 100000000 | bytes 300000000 | tf_op jit(solution)/shard_map/tail_exchange/pallas_call | solution.py:665
  428.6 0.6 pad_add_fusion.where_ref
  429.2 33.9 %final_rows.1 = (f32[2,1024,2048]{2,1,0:T(8,128)}, f32[2,2048,2,1024]{3,2,1,0:T(2,128)}, bf16[768,2048]{1,0:T(8,128)(2,1)}, bf16[768,2048]{1,0:T(8,128)(2,1)}, f...) custom-call(s32[3]{0:T(128)} %pad_add_fusion.where_ref, ...), custom_call_target="tpu_custom_call" | custom-call | flops 50000000 | bytes 91000000 | tf_op jit(solution)/shard_map/final_rows/pallas_call | solution.py:1424
  463.1 1.3 copy.74
  (30 shorter events, 0.2 us)
Async XLA Ops:
  7.2 422.0 %all-reduce.9.cloned.1.call-start = ((), (), s32[]{:S(2)}) async-start(), calls=%async_computation | async-start | bytes 2490368 | tf_op jit(solution)/shard_map/psum | solution.py:1809
  14.5 63.1 %copy-start.4 = (bf16[2,128,1024]{2,1,0:T(8,128)(2,1)S(1)}, bf16[2,128,1024]{2,1,0:T(8,128)(2,1)}, u32[]{:S(2)}) copy-start(bf16[2,128,1024]{2,1,0:T(8,128)(2,1)} %dt_proj.1) | copy-start | bytes 1572868
  14.5 63.2 %copy-start.6 = (f32[1024]{0:T(1024)S(1)}, f32[1024]{0:T(1024)}, u32[]{:S(2)}) copy-start(f32[1024]{0:T(1024)} %param.25) | copy-start | bytes 12292
  14.5 63.2 %copy-start.7 = (f32[2,1024]{1,0:T(2,128)S(1)}, f32[2,1024]{1,0:T(2,128)}, u32[]{:S(2)}) copy-start(f32[2,1024]{1,0:T(2,128)} %rest_1_.1) | copy-start | bytes 24580
  77.7 1.4 copy-start
  79.1 1.0 copy-start.1
  80.1 0.9 copy-start.5
  114.2 0.9 copy-start.3
  115.0 29.1 %copy-start.2 = (f32[768,128]{1,0:T(8,128)S(1)}, f32[768,128]{1,0:T(8,128)}, u32[]{:S(2)}) copy-start(f32[768,128]{1,0:T(8,128)} %get-tuple-element.67) | copy-start | bytes 1179652
  144.1 87.1 %copy-start.10 = (f32[16,1024]{1,0:T(8,128)S(1)}, f32[16,1024]{1,0:T(8,128)}, u32[]{:S(2)}) copy-start(f32[16,1024]{1,0:T(8,128)} %param.24) | copy-start | bytes 196612
  144.1 87.2 %copy-start.9 = (f32[768,128]{1,0:T(8,128)S(1)}, f32[768,128]{1,0:T(8,128)}, u32[]{:S(2)}) copy-start(f32[768,128]{1,0:T(8,128)} %get-tuple-element.93.inverse) | copy-start | bytes 1179652
  230.5 0.7 copy-start.8
Sparse Core Ops, SparseCore 0:
  323.6 67.7 all-reduce.8

commit v7 on v6

--- a/solution.py
+++ b/solution.py
@@ -166,7 +166,7 @@
             pltpu.VMEM((tokens, channels), low), pltpu.VMEM((tokens, channels), low),
             pltpu.SemaphoreType.DMA((count, 2)), pltpu.SemaphoreType.DMA((count, 2)), pltpu.SemaphoreType.DMA((count, 2)),
         ] if joined else []),
-        compiler_params=pltpu.CompilerParams(vmem_limit_bytes=48 * 1024 * 1024, **settings),
+        compiler_params=pltpu.CompilerParams(vmem_limit_bytes=60 * 1024 * 1024, **settings),
         name="scan_forward",
     )(bc, pre, act, z, gg, keep, a_log3, skip, mode, *dt)
 
@@ -1615,7 +1615,7 @@
         cost_estimate=pl.CostEstimate(flops=60 * tokens * channels * states,
                                       bytes_accessed=4 * tokens * channels * states,
                                       transcendentals=tokens * channels * states),
-        compiler_params=pltpu.CompilerParams(vmem_limit_bytes=52 * 1024 * 1024, **settings),
+        compiler_params=pltpu.CompilerParams(vmem_limit_bytes=60 * 1024 * 1024, **settings),
         name="scan_backward",
     )(bc, pre, act, mixed, keep, a_log3, skip, h, starts, *extra)
     return outs

time: 477 us -> 478 us (level)
  no operation moved by 1% of the time
where the time goes in v7:
time: 478 us; the launch traced here: 472 us
  Pallas kernels  442 us (92%)
  between operations  14.7 us (3%)
  local copies, waits for them, and re-layouts  9.65 us (2%)
  other arithmetic  6.53 us (1%)
    pallas_call x1, Pallas kernels, tail_exchange(): pl.pallas_call(functools.partial(tail_kernel, count), in_specs=[anywhere]...  106 us
    pallas_call x1, Pallas kernels, middle(): pl.pallas_call(middle_kernel, in_specs=[vmem] * 16 + [anywhere] * 6, out_...  88.3 us
    pallas_call x1, Pallas kernels, scan_backward(): pl.pallas_call(functools.partial(scan_backward_kernel, states, groups, ro...  87.4 us
    pallas_call x1, Pallas kernels, front(): pl.pallas_call(functools.partial(front_kernel, coeffs_wide), in_specs=[vm...  63 us
    pallas_call x1, Pallas kernels, final(): pl.pallas_call(functools.partial(final_kernel, side, depth), in_specs=[pl...  33.9 us
    pallas_call x1, Pallas kernels, scan_forward(): pl.pallas_call(functools.partial(scan_forward_kernel, states, groups, row...  33.7 us
    pallas_call x1, Pallas kernels, make_products(): pl.pallas_call(products_kernel, in_specs=[anywhere] * 7, out_specs=[anywh...  29 us
  transfers between devices with their start and end apart: 1, of which 0 were waited for; matrix products, arithmetic and copies ran while one was open for 0% of the time, Pallas kernels for 22%

profile of v7, /device:TPU:0, one launch (start us, length us, event | category | flops | bytes accessed | tf_op | source)
XLA Modules:
  0.0 472.4 jit_solution(14617690161056157755)
XLA Ops:
  7.2 0.0 all-reduce.9.cloned.1.call-start
  7.2 0.7 fusion.7
  7.9 0.9 fusion
  8.8 1.0 copy.62.keep_ref
  9.8 0.1 fusion.3
  9.9 1.0 copy.63.mode_ref
  10.9 0.1 fusion.4
  10.9 0.1 fusion.5
  11.0 0.9 copy.61.docs
  12.0 1.5 copy.69
  13.5 2.2 pad.31.x_wide
  15.7 1.0 broadcast_in_dim.41.modes
  16.7 63.0 %front.1 = (bf16[2,2048,1024]{2,1,0:T(8,128)(2,1)}, bf16[2,2048,1024]{2,1,0:T(8,128)(2,1)}, bf16[1536,1024]{1,0:T(8,128)(2,1)}, bf16[1536,1024]{1,0:T(8,128)(2,1...) custom-call(bf16[768,2048]{1,0:T(8,128)(2,1)} %hidden.5, ...), custom_call_target="tpu_custom_call" | custom-call | flops 20000000000 | bytes 80000000 | tf_op jit(solution)/shard_map/front/pallas_call | solution.py:1207
  79.7 33.7 %scan_forward.1 = (bf16[1536,1024]{1,0:T(8,128)(2,1)}, bf16[1536,1024]{1,0:T(8,128)(2,1)}, f32[768,1024]{1,0:T(8,128)}, f32[768,16,8,128]{3,2,1,0:T(8,128)}, f32...) custom-call(f32[768,32]{1,0:T(8,128)} %bitcast.46, ...), custom_call_target="tpu_custom_call" | custom-call | tf_op jit(solution)/shard_map/scan_forward/pallas_call | solution.py:145
  113.4 29.0 %products.1 = (bf16[1024,1024]{1,0:T(8,128)(2,1)}, bf16[1024,1024]{1,0:T(8,128)(2,1)}, bf16[1024,1024]{1,0:T(8,128)(2,1)}, bf16[1024,1024]{1,0:T(8,128)(2,1)}, b...) custom-call(bf16[1536,1024]{1,0:T(8,128)(2,1)} %get-tuple-element.76.gated, ...), custom_call_target="tpu_custom_call" | custom-call | flops 20000000000 | bytes 45000000 | tf_op jit(solution)/shard_map/products/pallas_call | solution.py:1313
  142.5 0.0 copy-start.2
  142.5 0.0 copy-start
  142.5 0.0 copy-start.1
  142.5 87.4 %scan_backward.1 = (bf16[768,1024]{1,0:T(8,128)(2,1)}, f32[768,1024]{1,0:T(8,128)}, f32[768,128]{1,0:T(8,128)}, f32[16,8,128]{2,1,0:T(8,128)}, f32[1,1024]{1,0:T...) custom-call(f32[768,32]{1,0:T(8,128)} %bitcast.47, ...), custom_call_target="tpu_custom_call" | custom-call | flops 754974720 | bytes 50331648 | tf_op jit(solution)/shard_map/scan_backward/pallas_call | solution.py:1592
  229.9 0.9 bitcast_multiply_fusion
  230.8 0.9 pad_maximum_fusion.inv
  231.7 0.2 copy.65
  231.9 0.2 copy.66
  232.1 0.2 copy.67
  232.3 1.3 pad_maximum_fusion.1.extra
  233.6 1.1 maximum_bitcast_fusion.docs
  234.7 88.3 %middle.1 = (bf16[608,1024]{1,0:T(8,128)(2,1)}, bf16[768,2048]{1,0:T(8,128)(2,1)}, bf16[2,1024,1024]{2,1,0:T(8,128)(2,1)}, bf16[2,2,4,256,1024]{4,3,2,1,0:T(8,12...) custom-call(bf16[768,1024]{1,0:T(8,128)(2,1)} %get-tuple-element.87., ...), custom_call_target="tpu_custom_call", output_to_operand_aliasing={{5}: (21, {})} | custom-call | flops 27000000512 | bytes 60000000 | tf_op jit(solution)/shard_map/middle/pallas_call | solution.py:939
  323.1 0.0 all-reduce.9.cloned.1.call-update
  323.1 106.2 %tail_exchange.1 = (bf16[2,2,4,256,1024]{4,3,2,1,0:T(8,128)(2,1)}, bf16[2,12,32,2048]{3,2,1,0:T(8,128)(2,1)}, bf16[2,256,1024]{2,1,0:T(8,128)(2,1)}) custom-call(bf16[2,1024,1024]{2,1,0:T(8,128)(2,1)} %get-tuple-element.103.refs_0_, bf16[2,12,32,2048]{3,2,1,0:T(8,128)(2,1)} %bitcast.41), custom_call_target="tpu_custom_call" | custom-call | flops 100000000 | bytes 300000000 | tf_op jit(solution)/shard_map/tail_exchange/pallas_call | solution.py:665
  429.3 0.7 pad_add_fusion.where_ref
  430.0 33.9 %final_rows.1 = (f32[2,1024,2048]{2,1,0:T(8,128)}, f32[2,2048,2,1024]{3,2,1,0:T(2,128)}, bf16[768,2048]{1,0:T(8,128)(2,1)}, bf16[768,2048]{1,0:T(8,128)(2,1)}, f...) custom-call(s32[3]{0:T(128)} %pad_add_fusion.where_ref, ...), custom_call_target="tpu_custom_call" | custom-call | flops 50000000 | bytes 91000000 | tf_op jit(solution)/shard_map/final_rows/pallas_call | solution.py:1424
  463.8 1.3 copy.74
  (14 shorter events, 0.1 us)
Async XLA Ops:
  7.2 422.8 %all-reduce.9.cloned.1.call-start = ((), (), s32[]{:S(2)}) async-start(), calls=%async_computation | async-start | bytes 2490368 | tf_op jit(solution)/shard_map/psum | solution.py:1809
  142.5 87.4 %copy-start.2 = (f32[16,1024]{1,0:T(8,128)S(1)}, f32[16,1024]{1,0:T(8,128)}, u32[]{:S(2)}) copy-start(f32[16,1024]{1,0:T(8,128)} %param.24) | copy-start | bytes 196612
  142.5 88.3 %copy-start = (f32[768,1]{1,0:T(8,128)S(1)}, f32[768,1]{1,0:T(8,128)}, u32[]{:S(2)}) copy-start(f32[768,1]{1,0:T(8,128)} %copy.63.mode_ref) | copy-start | bytes 9220
  142.5 88.3 %copy-start.1 = (f32[768,128]{1,0:T(8,128)S(1)}, f32[768,128]{1,0:T(8,128)}, u32[]{:S(2)}) copy-start(f32[768,128]{1,0:T(8,128)} %get-tuple-element.93.inverse) | copy-start | bytes 1179652
Sparse Core Ops, SparseCore 0:
  323.2 68.8 all-reduce.8
